TPU v7x, 512 devices: a whole 4x8x8 slice. The times are simulated.
512 devices in a mesh: sweep: 32 (over x, y), cross: 16 (over z, core).
Axes of the slice: x: 4, y: 8, z: 8, core: 2. Of those that a mesh axis runs over, the one named last changes fastest.
Arguments:
- source: bfloat16 [128, 32, 1, 135, 256], P('sweep', 'cross'), may hold values from -0.23925781 to 0.23925781
- inv_diag: bfloat16 [128, 32, 1, 135, 135], P('sweep', 'cross'), may hold values from -0.0801 to 1.602
- upstream: bfloat16 [128, 32, 1, 135, 135], P('sweep', 'cross'), may hold values from -1.25 to 0.125
- downstream: bfloat16 [128, 32, 1, 135, 135], P('sweep', 'cross'), may hold values from -0.125 to 1.25
- cross_lower: bfloat16 [128, 32, 1, 135, 135], P('sweep', 'cross'), may hold values from -0.25 to 0.25
- cross_upper: bfloat16 [128, 32, 1, 135, 135], P('sweep', 'cross'), may hold values from -0.25 to 0.25
Outputs:
- update: float32 [128, 32, 1, 135, 256], P('sweep', 'cross')
All inputs are finite; a program needn't handle non-finite values.
Results may differ from a plain program's by a relative error of at most 0.0003.
Values sent between devices are 32-bit elements; how exact they have to be, the bound alone decides.
No kernel may reach another device: no remote copies, remote signals or barrier semaphores. Data moves between devices by JAX's collectives and lax.ppermute only.
A program may use at most 128 MiB of HBM per device.

v0:
```python
import jax
import jax.numpy as jnp
from jax import lax
from jax.sharding import PartitionSpec as P


def from_behind(block, axis, distance):
    devices = range(lax.axis_size(axis))
    route = [(i - distance, i) for i in devices if i - distance in devices]
    return lax.ppermute(block, axis, route)


def with_halo(cells, sides, width):
    for axis, dim in sides:
        count = lax.axis_size(axis)
        ends = count - 1
        head = lax.slice_in_dim(cells, 0, width, axis=dim)
        tail = lax.slice_in_dim(cells, cells.shape[dim] - width, cells.shape[dim], axis=dim)
        cells = jnp.concatenate(
            [
                lax.ppermute(tail, axis, [(i, (i + 1) % count) for i in range(ends)]),
                cells,
                lax.ppermute(head, axis, [((i + 1) % count, i) for i in range(ends)]),
            ],
            axis=dim,
        )
    return cells


def carried_in(value, axis, combine, identity):
    peers, mine = (lax.axis_size(axis), lax.axis_index(axis))
    everything = jax.tree.map(lambda part: lax.all_gather(part, axis), value)
    start = jax.tree.map(
        lambda part, zero: jnp.broadcast_to(jnp.asarray(zero, part.dtype), part.shape),
        value,
        identity,
    )

    def turn(k, before):
        at = peers - 1 - k
        reached = at > mine
        new = combine(before, jax.tree.map(lambda part: part[at], everything))
        return jax.tree.map(lambda a, b: jnp.where(reached, a, b), new, before)

    return lax.fori_loop(0, peers, turn, start)


def direct(matrix, other):
    return jnp.einsum("nij,njr->nir", matrix, other, preferred_element_type=jnp.float32)


def precise(matrix, other):
    return jnp.einsum(
        "nij,njr->nir",
        matrix,
        other,
        precision=lax.Precision.HIGHEST,
        preferred_element_type=jnp.float32,
    )


def compose(earlier, later):
    return (precise(later[0], earlier[0]), precise(later[0], earlier[1]) + later[1])


def shards(source, inv_diag, upstream, downstream, cross_lower, cross_upper):
    positions, columns, planes, unknowns, vectors = source.shape
    elements = columns * planes
    source_rows = source.reshape(positions, elements, unknowns, vectors)
    inverse = inv_diag.reshape(positions, elements, unknowns, unknowns)
    before_face = upstream.reshape(positions, elements, unknowns, unknowns)
    after_face = downstream.reshape(positions, elements, unknowns, unknowns)
    lower_face = cross_lower.reshape(positions, elements, unknowns, unknowns)
    upper_face = cross_upper.reshape(positions, elements, unknowns, unknowns)
    unit_maps = jnp.broadcast_to(
        jnp.eye(unknowns, dtype=jnp.float32), (elements, unknowns, unknowns)
    )
    empty_vec = jnp.zeros((elements, unknowns, vectors), jnp.float32)
    fore_mat = -direct(inverse[0], before_face[0])
    fore_vec = direct(inverse[0], source_rows[0])
    for position in range(1, positions):
        step_mat = -direct(inverse[position], before_face[position])
        fore_mat = precise(step_mat, fore_mat)
        fore_vec = precise(step_mat, fore_vec) + direct(inverse[position], source_rows[position])

    def advance(turn_index, arriving):
        leaving = precise(fore_mat, arriving) + fore_vec
        return from_behind(leaving, "sweep", 1)

    incoming = lax.fori_loop(0, lax.axis_size("sweep") - 1, advance, empty_vec)
    previous = incoming
    partials = []
    values = []
    for position in range(positions):
        partial_value = source_rows[position].astype(jnp.float32) - precise(
            before_face[position], previous
        )
        previous = precise(inverse[position], partial_value)
        partials.append(partial_value)
        values.append(previous)
    forward = jnp.stack(values).reshape(positions, columns, planes, unknowns, vectors)
    padded = with_halo(forward, (("cross", 1),), 1)
    lower_rim = padded[:, :-2].reshape(positions, elements, unknowns, vectors)
    upper_rim = padded[:, 2:].reshape(positions, elements, unknowns, vectors)
    knowns = [
        partials[position]
        - precise(lower_face[position], lower_rim[position])
        - precise(upper_face[position], upper_rim[position])
        for position in range(positions)
    ]
    highest = positions - 1
    back_mat = -direct(inverse[highest], after_face[highest])
    back_vec = precise(inverse[highest], knowns[highest])
    for position in range(positions - 2, -1, -1):
        step_mat = -direct(inverse[position], after_face[position])
        back_mat = precise(step_mat, back_mat)
        back_vec = precise(step_mat, back_vec) + precise(inverse[position], knowns[position])
    suffix = carried_in((back_mat, back_vec), "sweep", compose, (unit_maps, empty_vec))
    following = suffix[1]
    results = [None] * positions
    for position in range(positions - 1, -1, -1):
        balance = knowns[position] - precise(after_face[position], following)
        following = precise(inverse[position], balance)
        results[position] = following
    return jnp.stack(results).reshape(positions, columns, planes, unknowns, vectors)


def solution(mesh):
    placed = (
        P("sweep", "cross", None, None, None),
        P("sweep", "cross", None, None, None),
        P("sweep", "cross", None, None, None),
        P("sweep", "cross", None, None, None),
        P("sweep", "cross", None, None, None),
        P("sweep", "cross", None, None, None),
    )
    return jax.shard_map(
        shards,
        mesh=mesh,
        in_specs=placed,
        out_specs=P("sweep", "cross", None, None, None),
        check_vma=False,
    )
```

profile of v0, /device:TPU:1, one launch (start us, length us, event | category | flops | bytes accessed | tf_op | source)
XLA Modules:
  0.0 604.1 jit_solution(10188176768652271743)
XLA Ops:
  16.5 337.7 %while.26 = (s32[]{:T(128)}, f32[2,135,256]{2,1,0:T(8,128)S(1)}, f32[2,135,135]{2,1,0:T(8,128)S(1)}, f32[2,135,256]{2,1,0:T(8,128)S(1)}, s32[]{:T(128)}) while((s32[]{:T(128)}, f32[2,135,256]{2,1,0:T(8,128)S(1)}, f32[2,135,135]{2,1,0:T(8,128)S(1)}, f32[2,135,256]{2,1,0:T(8,128)S(1)}, s32[]{:T(128)}) %tuple.76), condition=%wide.region_1.0_spmd, body=%wide.region_0.0_spmd.sunk | while | flops 112043520 | bytes 2081261 | solution.py:90
  24.9 5.1 collective-permute-start
  33.8 6.3 %collective-permute-start = (f32[2,135,256]{2,1,0:T(8,128)S(1)}, f32[2,135,256]{2,1,0:T(8,128)S(1)}, u32[]{:S(2)}, u32[]{:S(2)}) collective-permute-start(f32[2,135,256]{2,1,0:T(8,128)S(1)} %convolution_add_fusion.6), channel_id=1, source_target_pairs={{0,16},{16,32},{32,48},{48,64},{64,80},{80,96},{96,112},{112,128},... | collective-permute-start | bytes 829448 | tf_op jit(solution)/shard_map/while/body/eval_jaxpr/ppermute | solution.py:10
  40.1 4.4 collective-permute-done
  44.9 5.4 collective-permute-start
  50.3 5.1 collective-permute-done
  55.9 11.4 %collective-permute-start = (f32[2,135,256]{2,1,0:T(8,128)S(1)}, f32[2,135,256]{2,1,0:T(8,128)S(1)}, u32[]{:S(2)}, u32[]{:S(2)}) collective-permute-start(f32[2,135,256]{2,1,0:T(8,128)S(1)} %convolution_add_fusion.6), channel_id=1, source_target_pairs={{0,16},{16,32},{32,48},{48,64},{64,80},{80,96},{96,112},{112,128},... | collective-permute-start | bytes 829448 | tf_op jit(solution)/shard_map/while/body/eval_jaxpr/ppermute | solution.py:10
  75.3 10.5 %collective-permute-done = f32[2,135,256]{2,1,0:T(8,128)S(1)} collective-permute-done((f32[2,135,256]{2,1,0:T(8,128)S(1)}, f32[2,135,256]{2,1,0:T(8,128)S(1)}, u32[]{:S(2)}, u32[]{:S(2)}) %collective-permute-start) | collective-permute-done | bytes 276512 | tf_op jit(solution)/shard_map/while/body/eval_jaxpr/ppermute | solution.py:10
  86.2 4.2 collective-permute-start
  90.4 9.4 %collective-permute-done = f32[2,135,256]{2,1,0:T(8,128)S(1)} collective-permute-done((f32[2,135,256]{2,1,0:T(8,128)S(1)}, f32[2,135,256]{2,1,0:T(8,128)S(1)}, u32[]{:S(2)}, u32[]{:S(2)}) %collective-permute-start) | collective-permute-done | bytes 276512 | tf_op jit(solution)/shard_map/while/body/eval_jaxpr/ppermute | solution.py:10
  100.2 6.8 %collective-permute-start = (f32[2,135,256]{2,1,0:T(8,128)S(1)}, f32[2,135,256]{2,1,0:T(8,128)S(1)}, u32[]{:S(2)}, u32[]{:S(2)}) collective-permute-start(f32[2,135,256]{2,1,0:T(8,128)S(1)} %convolution_add_fusion.6), channel_id=1, source_target_pairs={{0,16},{16,32},{32,48},{48,64},{64,80},{80,96},{96,112},{112,128},... | collective-permute-start | bytes 829448 | tf_op jit(solution)/shard_map/while/body/eval_jaxpr/ppermute | solution.py:10
  107.1 9.8 %collective-permute-done = f32[2,135,256]{2,1,0:T(8,128)S(1)} collective-permute-done((f32[2,135,256]{2,1,0:T(8,128)S(1)}, f32[2,135,256]{2,1,0:T(8,128)S(1)}, u32[]{:S(2)}, u32[]{:S(2)}) %collective-permute-start) | collective-permute-done | bytes 276512 | tf_op jit(solution)/shard_map/while/body/eval_jaxpr/ppermute | solution.py:10
  117.3 7.1 %collective-permute-start = (f32[2,135,256]{2,1,0:T(8,128)S(1)}, f32[2,135,256]{2,1,0:T(8,128)S(1)}, u32[]{:S(2)}, u32[]{:S(2)}) collective-permute-start(f32[2,135,256]{2,1,0:T(8,128)S(1)} %convolution_add_fusion.6), channel_id=1, source_target_pairs={{0,16},{16,32},{32,48},{48,64},{64,80},{80,96},{96,112},{112,128},... | collective-permute-start | bytes 829448 | tf_op jit(solution)/shard_map/while/body/eval_jaxpr/ppermute | solution.py:10
  124.5 10.6 %collective-permute-done = f32[2,135,256]{2,1,0:T(8,128)S(1)} collective-permute-done((f32[2,135,256]{2,1,0:T(8,128)S(1)}, f32[2,135,256]{2,1,0:T(8,128)S(1)}, u32[]{:S(2)}, u32[]{:S(2)}) %collective-permute-start) | collective-permute-done | bytes 276512 | tf_op jit(solution)/shard_map/while/body/eval_jaxpr/ppermute | solution.py:10
  135.5 5.5 collective-permute-start
  144.9 5.4 collective-permute-start
  154.2 4.9 collective-permute-start
  159.0 4.2 collective-permute-done
  163.7 5.3 collective-permute-start
  169.0 5.1 collective-permute-done
  174.5 5.8 collective-permute-start
  180.3 6.1 %collective-permute-done = f32[2,135,256]{2,1,0:T(8,128)S(1)} collective-permute-done((f32[2,135,256]{2,1,0:T(8,128)S(1)}, f32[2,135,256]{2,1,0:T(8,128)S(1)}, u32[]{:S(2)}, u32[]{:S(2)}) %collective-permute-start) | collective-permute-done | bytes 276512 | tf_op jit(solution)/shard_map/while/body/eval_jaxpr/ppermute | solution.py:10
  186.8 5.9 collective-permute-start
  192.8 5.5 collective-permute-done
  198.7 4.8 collective-permute-start
  203.6 4.4 collective-permute-done
  216.3 5.1 collective-permute-start
  225.4 5.3 collective-permute-start
  234.6 5.3 collective-permute-start
  243.8 5.0 collective-permute-start
  252.7 5.3 collective-permute-start
  258.0 4.5 collective-permute-done
  262.9 5.6 collective-permute-start
  268.6 5.6 collective-permute-done
  274.5 5.9 collective-permute-start
  280.5 6.1 %collective-permute-done = f32[2,135,256]{2,1,0:T(8,128)S(1)} collective-permute-done((f32[2,135,256]{2,1,0:T(8,128)S(1)}, f32[2,135,256]{2,1,0:T(8,128)S(1)}, u32[]{:S(2)}, u32[]{:S(2)}) %collective-permute-start) | collective-permute-done | bytes 276512 | tf_op jit(solution)/shard_map/while/body/eval_jaxpr/ppermute | solution.py:10
  291.1 4.3 collective-permute-done
  303.8 4.4 collective-permute-start
  312.2 6.0 collective-permute-start
  322.1 6.2 %collective-permute-start = (f32[2,135,256]{2,1,0:T(8,128)S(1)}, f32[2,135,256]{2,1,0:T(8,128)S(1)}, u32[]{:S(2)}, u32[]{:S(2)}) collective-permute-start(f32[2,135,256]{2,1,0:T(8,128)S(1)} %convolution_add_fusion.6), channel_id=1, source_target_pairs={{0,16},{16,32},{32,48},{48,64},{64,80},{80,96},{96,112},{112,128},... | collective-permute-start | bytes 829448 | tf_op jit(solution)/shard_map/while/body/eval_jaxpr/ppermute | solution.py:10
  332.2 6.2 %collective-permute-start = (f32[2,135,256]{2,1,0:T(8,128)S(1)}, f32[2,135,256]{2,1,0:T(8,128)S(1)}, u32[]{:S(2)}, u32[]{:S(2)}) collective-permute-start(f32[2,135,256]{2,1,0:T(8,128)S(1)} %convolution_add_fusion.6), channel_id=1, source_target_pairs={{0,16},{16,32},{32,48},{48,64},{64,80},{80,96},{96,112},{112,128},... | collective-permute-start | bytes 829448 | tf_op jit(solution)/shard_map/while/body/eval_jaxpr/ppermute | solution.py:10
  338.4 4.2 collective-permute-done
  343.0 6.2 %collective-permute-start = (f32[2,135,256]{2,1,0:T(8,128)S(1)}, f32[2,135,256]{2,1,0:T(8,128)S(1)}, u32[]{:S(2)}, u32[]{:S(2)}) collective-permute-start(f32[2,135,256]{2,1,0:T(8,128)S(1)} %convolution_add_fusion.6), channel_id=1, source_target_pairs={{0,16},{16,32},{32,48},{48,64},{64,80},{80,96},{96,112},{112,128},... | collective-permute-start | bytes 829448 | tf_op jit(solution)/shard_map/while/body/eval_jaxpr/ppermute | solution.py:10
  349.3 5.0 collective-permute-done
  357.5 36.6 %collective-permute-start.1 = (f32[4,1,1,135,256]{4,0,3,2,1:T(4,128)S(1)}, f32[4,1,1,135,256]{4,0,3,2,1:T(4,128)S(1)}, u32[]{:S(2)}, u32[]{:S(2)}) collective-permute-start(f32[4,1,1,135,256]{4,0,3,2,1:T(4,128)S(1)} %copy.43), channel_id=1, source_target_pairs={{0,1},{1,2},{2,3},{3,4},{4,5},{5,6},{6,7},{7,8},{8,9},{9,10},{10,1... | collective-permute-start | bytes 1658888 | tf_op jit(solution)/shard_map/ppermute | solution.py:21
  400.6 4.5 collective-permute-done.2
  411.6 131.7 %all-gather.7.cloned.1.call-done = f32[64,135,256]{2,1,0:T(8,128)} async-done(((f32[2,135,256]{2,1,0:T(8,128)}), f32[64,135,256]{2,1,0:T(8,128)}) %all-gather.7.cloned.1.call-update) | async-done | bytes 8847376 | tf_op jit(solution)/shard_map/all_gather | solution.py:32
  543.3 49.0 %while.27 = (s32[]{:T(128)}, f32[2,135,256]{2,1,0:T(8,128)S(1)}, s32[]{:T(128)}, f32[32,2,135,135]{3,2,1,0:T(8,128)}, f32[32,2,135,256]{3,2,1,0:T(8,128)}, /*index=5*/s32[]{:T(128)}, s32[]{:T(128)}, s32[]{:T(128)}, s32[]{:T(128)}) while((s32[]{:T(128)}, f32[2,135,256]{2,1,0:T(8,128)S(1)}, s32[]{:T(128)}, ...), condition=%wide.region_3.4_spmd.clone, body=%wide.region_2.3_spmd.clone.sunk | while | flops 112250888 | bytes 1946277 | solution.py:45
  (227 shorter events, 159.8 us)
Async XLA Ops:
  6.5 1.8 copy-start.15
  6.5 1.8 copy-start.14
  6.5 405.0 %all-gather.5.cloned.1.call-start = ((), (), s32[]{:S(2)}) async-start(), calls=%async_computation | async-start | bytes 9191424 | tf_op jit(solution)/shard_map/all_gather | solution.py:32
  8.1 1.4 copy-start.2
  8.3 1.4 copy-start.12
  9.1 3.3 copy-start.4
  9.1 3.5 copy-start.6
  9.1 3.7 copy-start.8
  9.1 3.9 copy-start.10
  10.4 1.6 copy-start.16
  12.0 531.3 %all-gather.7.cloned.1.call-start = ((), (), s32[]{:S(2)}) async-start(), calls=%async_computation.1 | async-start | bytes 9191424 | tf_op jit(solution)/shard_map/all_gather | solution.py:32
  16.5 337.7 %copy-start.11 = (bf16[1,2,1,135,135]{4,1,3,2,0:T(2,128)(2,1)S(1)}, bf16[1,2,1,135,135]{4,1,3,2,0:T(2,128)(2,1)}, u32[]{:S(2)}) copy-start(bf16[1,2,1,135,135]{4,1,3,2,0:T(2,128)(2,1)} %copy-done.10) | copy-start | bytes 218704
  17.0 7.5 %collective-permute-start = (f32[2,135,256]{2,1,0:T(8,128)S(1)}, f32[2,135,256]{2,1,0:T(8,128)S(1)}, u32[]{:S(2)}, u32[]{:S(2)}) collective-permute-start(f32[2,135,256]{2,1,0:T(8,128)S(1)} %convolution_add_fusion.6), channel_id=1, source_target_pairs={{0,16},{16,32},{32,48},{48,64},{64,80},{80,96},{96,112},{112,128},... | collective-permute-start | bytes 829448 | tf_op jit(solution)/shard_map/while/body/eval_jaxpr/ppermute | solution.py:10
  24.9 8.5 %collective-permute-start = (f32[2,135,256]{2,1,0:T(8,128)S(1)}, f32[2,135,256]{2,1,0:T(8,128)S(1)}, u32[]{:S(2)}, u32[]{:S(2)}) collective-permute-start(f32[2,135,256]{2,1,0:T(8,128)S(1)} %convolution_add_fusion.6), channel_id=1, source_target_pairs={{0,16},{16,32},{32,48},{48,64},{64,80},{80,96},{96,112},{112,128},... | collective-permute-start | bytes 829448 | tf_op jit(solution)/shard_map/while/body/eval_jaxpr/ppermute | solution.py:10
  33.8 10.7 %collective-permute-start = (f32[2,135,256]{2,1,0:T(8,128)S(1)}, f32[2,135,256]{2,1,0:T(8,128)S(1)}, u32[]{:S(2)}, u32[]{:S(2)}) collective-permute-start(f32[2,135,256]{2,1,0:T(8,128)S(1)} %convolution_add_fusion.6), channel_id=1, source_target_pairs={{0,16},{16,32},{32,48},{48,64},{64,80},{80,96},{96,112},{112,128},... | collective-permute-start | bytes 829448 | tf_op jit(solution)/shard_map/while/body/eval_jaxpr/ppermute | solution.py:10
  44.9 10.5 %collective-permute-start = (f32[2,135,256]{2,1,0:T(8,128)S(1)}, f32[2,135,256]{2,1,0:T(8,128)S(1)}, u32[]{:S(2)}, u32[]{:S(2)}) collective-permute-start(f32[2,135,256]{2,1,0:T(8,128)S(1)} %convolution_add_fusion.6), channel_id=1, source_target_pairs={{0,16},{16,32},{32,48},{48,64},{64,80},{80,96},{96,112},{112,128},... | collective-permute-start | bytes 829448 | tf_op jit(solution)/shard_map/while/body/eval_jaxpr/ppermute | solution.py:10
  55.9 14.9 %collective-permute-start = (f32[2,135,256]{2,1,0:T(8,128)S(1)}, f32[2,135,256]{2,1,0:T(8,128)S(1)}, u32[]{:S(2)}, u32[]{:S(2)}) collective-permute-start(f32[2,135,256]{2,1,0:T(8,128)S(1)} %convolution_add_fusion.6), channel_id=1, source_target_pairs={{0,16},{16,32},{32,48},{48,64},{64,80},{80,96},{96,112},{112,128},... | collective-permute-start | bytes 829448 | tf_op jit(solution)/shard_map/while/body/eval_jaxpr/ppermute | solution.py:10
  71.2 14.6 %collective-permute-start = (f32[2,135,256]{2,1,0:T(8,128)S(1)}, f32[2,135,256]{2,1,0:T(8,128)S(1)}, u32[]{:S(2)}, u32[]{:S(2)}) collective-permute-start(f32[2,135,256]{2,1,0:T(8,128)S(1)} %convolution_add_fusion.6), channel_id=1, source_target_pairs={{0,16},{16,32},{32,48},{48,64},{64,80},{80,96},{96,112},{112,128},... | collective-permute-start | bytes 829448 | tf_op jit(solution)/shard_map/while/body/eval_jaxpr/ppermute | solution.py:10
  86.2 13.7 %collective-permute-start = (f32[2,135,256]{2,1,0:T(8,128)S(1)}, f32[2,135,256]{2,1,0:T(8,128)S(1)}, u32[]{:S(2)}, u32[]{:S(2)}) collective-permute-start(f32[2,135,256]{2,1,0:T(8,128)S(1)} %convolution_add_fusion.6), channel_id=1, source_target_pairs={{0,16},{16,32},{32,48},{48,64},{64,80},{80,96},{96,112},{112,128},... | collective-permute-start | bytes 829448 | tf_op jit(solution)/shard_map/while/body/eval_jaxpr/ppermute | solution.py:10
  100.2 16.6 %collective-permute-start = (f32[2,135,256]{2,1,0:T(8,128)S(1)}, f32[2,135,256]{2,1,0:T(8,128)S(1)}, u32[]{:S(2)}, u32[]{:S(2)}) collective-permute-start(f32[2,135,256]{2,1,0:T(8,128)S(1)} %convolution_add_fusion.6), channel_id=1, source_target_pairs={{0,16},{16,32},{32,48},{48,64},{64,80},{80,96},{96,112},{112,128},... | collective-permute-start | bytes 829448 | tf_op jit(solution)/shard_map/while/body/eval_jaxpr/ppermute | solution.py:10
  117.3 17.8 %collective-permute-start = (f32[2,135,256]{2,1,0:T(8,128)S(1)}, f32[2,135,256]{2,1,0:T(8,128)S(1)}, u32[]{:S(2)}, u32[]{:S(2)}) collective-permute-start(f32[2,135,256]{2,1,0:T(8,128)S(1)} %convolution_add_fusion.6), channel_id=1, source_target_pairs={{0,16},{16,32},{32,48},{48,64},{64,80},{80,96},{96,112},{112,128},... | collective-permute-start | bytes 829448 | tf_op jit(solution)/shard_map/while/body/eval_jaxpr/ppermute | solution.py:10
  135.5 9.0 %collective-permute-start = (f32[2,135,256]{2,1,0:T(8,128)S(1)}, f32[2,135,256]{2,1,0:T(8,128)S(1)}, u32[]{:S(2)}, u32[]{:S(2)}) collective-permute-start(f32[2,135,256]{2,1,0:T(8,128)S(1)} %convolution_add_fusion.6), channel_id=1, source_target_pairs={{0,16},{16,32},{32,48},{48,64},{64,80},{80,96},{96,112},{112,128},... | collective-permute-start | bytes 829448 | tf_op jit(solution)/shard_map/while/body/eval_jaxpr/ppermute | solution.py:10
  144.9 8.8 %collective-permute-start = (f32[2,135,256]{2,1,0:T(8,128)S(1)}, f32[2,135,256]{2,1,0:T(8,128)S(1)}, u32[]{:S(2)}, u32[]{:S(2)}) collective-permute-start(f32[2,135,256]{2,1,0:T(8,128)S(1)} %convolution_add_fusion.6), channel_id=1, source_target_pairs={{0,16},{16,32},{32,48},{48,64},{64,80},{80,96},{96,112},{112,128},... | collective-permute-start | bytes 829448 | tf_op jit(solution)/shard_map/while/body/eval_jaxpr/ppermute | solution.py:10
  154.2 9.1 %collective-permute-start = (f32[2,135,256]{2,1,0:T(8,128)S(1)}, f32[2,135,256]{2,1,0:T(8,128)S(1)}, u32[]{:S(2)}, u32[]{:S(2)}) collective-permute-start(f32[2,135,256]{2,1,0:T(8,128)S(1)} %convolution_add_fusion.6), channel_id=1, source_target_pairs={{0,16},{16,32},{32,48},{48,64},{64,80},{80,96},{96,112},{112,128},... | collective-permute-start | bytes 829448 | tf_op jit(solution)/shard_map/while/body/eval_jaxpr/ppermute | solution.py:10
  163.7 10.4 %collective-permute-start = (f32[2,135,256]{2,1,0:T(8,128)S(1)}, f32[2,135,256]{2,1,0:T(8,128)S(1)}, u32[]{:S(2)}, u32[]{:S(2)}) collective-permute-start(f32[2,135,256]{2,1,0:T(8,128)S(1)} %convolution_add_fusion.6), channel_id=1, source_target_pairs={{0,16},{16,32},{32,48},{48,64},{64,80},{80,96},{96,112},{112,128},... | collective-permute-start | bytes 829448 | tf_op jit(solution)/shard_map/while/body/eval_jaxpr/ppermute | solution.py:10
  174.5 11.9 %collective-permute-start = (f32[2,135,256]{2,1,0:T(8,128)S(1)}, f32[2,135,256]{2,1,0:T(8,128)S(1)}, u32[]{:S(2)}, u32[]{:S(2)}) collective-permute-start(f32[2,135,256]{2,1,0:T(8,128)S(1)} %convolution_add_fusion.6), channel_id=1, source_target_pairs={{0,16},{16,32},{32,48},{48,64},{64,80},{80,96},{96,112},{112,128},... | collective-permute-start | bytes 829448 | tf_op jit(solution)/shard_map/while/body/eval_jaxpr/ppermute | solution.py:10
  186.8 11.5 %collective-permute-start = (f32[2,135,256]{2,1,0:T(8,128)S(1)}, f32[2,135,256]{2,1,0:T(8,128)S(1)}, u32[]{:S(2)}, u32[]{:S(2)}) collective-permute-start(f32[2,135,256]{2,1,0:T(8,128)S(1)} %convolution_add_fusion.6), channel_id=1, source_target_pairs={{0,16},{16,32},{32,48},{48,64},{64,80},{80,96},{96,112},{112,128},... | collective-permute-start | bytes 829448 | tf_op jit(solution)/shard_map/while/body/eval_jaxpr/ppermute | solution.py:10
  198.7 9.2 %collective-permute-start = (f32[2,135,256]{2,1,0:T(8,128)S(1)}, f32[2,135,256]{2,1,0:T(8,128)S(1)}, u32[]{:S(2)}, u32[]{:S(2)}) collective-permute-start(f32[2,135,256]{2,1,0:T(8,128)S(1)} %convolution_add_fusion.6), channel_id=1, source_target_pairs={{0,16},{16,32},{32,48},{48,64},{64,80},{80,96},{96,112},{112,128},... | collective-permute-start | bytes 829448 | tf_op jit(solution)/shard_map/while/body/eval_jaxpr/ppermute | solution.py:10
  208.3 7.6 %collective-permute-start = (f32[2,135,256]{2,1,0:T(8,128)S(1)}, f32[2,135,256]{2,1,0:T(8,128)S(1)}, u32[]{:S(2)}, u32[]{:S(2)}) collective-permute-start(f32[2,135,256]{2,1,0:T(8,128)S(1)} %convolution_add_fusion.6), channel_id=1, source_target_pairs={{0,16},{16,32},{32,48},{48,64},{64,80},{80,96},{96,112},{112,128},... | collective-permute-start | bytes 829448 | tf_op jit(solution)/shard_map/while/body/eval_jaxpr/ppermute | solution.py:10
  216.3 8.6 %collective-permute-start = (f32[2,135,256]{2,1,0:T(8,128)S(1)}, f32[2,135,256]{2,1,0:T(8,128)S(1)}, u32[]{:S(2)}, u32[]{:S(2)}) collective-permute-start(f32[2,135,256]{2,1,0:T(8,128)S(1)} %convolution_add_fusion.6), channel_id=1, source_target_pairs={{0,16},{16,32},{32,48},{48,64},{64,80},{80,96},{96,112},{112,128},... | collective-permute-start | bytes 829448 | tf_op jit(solution)/shard_map/while/body/eval_jaxpr/ppermute | solution.py:10
  225.4 8.8 %collective-permute-start = (f32[2,135,256]{2,1,0:T(8,128)S(1)}, f32[2,135,256]{2,1,0:T(8,128)S(1)}, u32[]{:S(2)}, u32[]{:S(2)}) collective-permute-start(f32[2,135,256]{2,1,0:T(8,128)S(1)} %convolution_add_fusion.6), channel_id=1, source_target_pairs={{0,16},{16,32},{32,48},{48,64},{64,80},{80,96},{96,112},{112,128},... | collective-permute-start | bytes 829448 | tf_op jit(solution)/shard_map/while/body/eval_jaxpr/ppermute | solution.py:10
  234.6 8.8 %collective-permute-start = (f32[2,135,256]{2,1,0:T(8,128)S(1)}, f32[2,135,256]{2,1,0:T(8,128)S(1)}, u32[]{:S(2)}, u32[]{:S(2)}) collective-permute-start(f32[2,135,256]{2,1,0:T(8,128)S(1)} %convolution_add_fusion.6), channel_id=1, source_target_pairs={{0,16},{16,32},{32,48},{48,64},{64,80},{80,96},{96,112},{112,128},... | collective-permute-start | bytes 829448 | tf_op jit(solution)/shard_map/while/body/eval_jaxpr/ppermute | solution.py:10
  243.8 8.5 %collective-permute-start = (f32[2,135,256]{2,1,0:T(8,128)S(1)}, f32[2,135,256]{2,1,0:T(8,128)S(1)}, u32[]{:S(2)}, u32[]{:S(2)}) collective-permute-start(f32[2,135,256]{2,1,0:T(8,128)S(1)} %convolution_add_fusion.6), channel_id=1, source_target_pairs={{0,16},{16,32},{32,48},{48,64},{64,80},{80,96},{96,112},{112,128},... | collective-permute-start | bytes 829448 | tf_op jit(solution)/shard_map/while/body/eval_jaxpr/ppermute | solution.py:10
  252.7 9.8 %collective-permute-start = (f32[2,135,256]{2,1,0:T(8,128)S(1)}, f32[2,135,256]{2,1,0:T(8,128)S(1)}, u32[]{:S(2)}, u32[]{:S(2)}) collective-permute-start(f32[2,135,256]{2,1,0:T(8,128)S(1)} %convolution_add_fusion.6), channel_id=1, source_target_pairs={{0,16},{16,32},{32,48},{48,64},{64,80},{80,96},{96,112},{112,128},... | collective-permute-start | bytes 829448 | tf_op jit(solution)/shard_map/while/body/eval_jaxpr/ppermute | solution.py:10
  262.9 11.2 %collective-permute-start = (f32[2,135,256]{2,1,0:T(8,128)S(1)}, f32[2,135,256]{2,1,0:T(8,128)S(1)}, u32[]{:S(2)}, u32[]{:S(2)}) collective-permute-start(f32[2,135,256]{2,1,0:T(8,128)S(1)} %convolution_add_fusion.6), channel_id=1, source_target_pairs={{0,16},{16,32},{32,48},{48,64},{64,80},{80,96},{96,112},{112,128},... | collective-permute-start | bytes 829448 | tf_op jit(solution)/shard_map/while/body/eval_jaxpr/ppermute | solution.py:10
  274.5 12.0 %collective-permute-start = (f32[2,135,256]{2,1,0:T(8,128)S(1)}, f32[2,135,256]{2,1,0:T(8,128)S(1)}, u32[]{:S(2)}, u32[]{:S(2)}) collective-permute-start(f32[2,135,256]{2,1,0:T(8,128)S(1)} %convolution_add_fusion.6), channel_id=1, source_target_pairs={{0,16},{16,32},{32,48},{48,64},{64,80},{80,96},{96,112},{112,128},... | collective-permute-start | bytes 829448 | tf_op jit(solution)/shard_map/while/body/eval_jaxpr/ppermute | solution.py:10
  287.0 8.4 %collective-permute-start = (f32[2,135,256]{2,1,0:T(8,128)S(1)}, f32[2,135,256]{2,1,0:T(8,128)S(1)}, u32[]{:S(2)}, u32[]{:S(2)}) collective-permute-start(f32[2,135,256]{2,1,0:T(8,128)S(1)} %convolution_add_fusion.6), channel_id=1, source_target_pairs={{0,16},{16,32},{32,48},{48,64},{64,80},{80,96},{96,112},{112,128},... | collective-permute-start | bytes 829448 | tf_op jit(solution)/shard_map/while/body/eval_jaxpr/ppermute | solution.py:10
  295.8 7.6 %collective-permute-start = (f32[2,135,256]{2,1,0:T(8,128)S(1)}, f32[2,135,256]{2,1,0:T(8,128)S(1)}, u32[]{:S(2)}, u32[]{:S(2)}) collective-permute-start(f32[2,135,256]{2,1,0:T(8,128)S(1)} %convolution_add_fusion.6), channel_id=1, source_target_pairs={{0,16},{16,32},{32,48},{48,64},{64,80},{80,96},{96,112},{112,128},... | collective-permute-start | bytes 829448 | tf_op jit(solution)/shard_map/while/body/eval_jaxpr/ppermute | solution.py:10
  303.8 7.9 %collective-permute-start = (f32[2,135,256]{2,1,0:T(8,128)S(1)}, f32[2,135,256]{2,1,0:T(8,128)S(1)}, u32[]{:S(2)}, u32[]{:S(2)}) collective-permute-start(f32[2,135,256]{2,1,0:T(8,128)S(1)} %convolution_add_fusion.6), channel_id=1, source_target_pairs={{0,16},{16,32},{32,48},{48,64},{64,80},{80,96},{96,112},{112,128},... | collective-permute-start | bytes 829448 | tf_op jit(solution)/shard_map/while/body/eval_jaxpr/ppermute | solution.py:10
  312.2 9.5 %collective-permute-start = (f32[2,135,256]{2,1,0:T(8,128)S(1)}, f32[2,135,256]{2,1,0:T(8,128)S(1)}, u32[]{:S(2)}, u32[]{:S(2)}) collective-permute-start(f32[2,135,256]{2,1,0:T(8,128)S(1)} %convolution_add_fusion.6), channel_id=1, source_target_pairs={{0,16},{16,32},{32,48},{48,64},{64,80},{80,96},{96,112},{112,128},... | collective-permute-start | bytes 829448 | tf_op jit(solution)/shard_map/while/body/eval_jaxpr/ppermute | solution.py:10
  322.1 9.7 %collective-permute-start = (f32[2,135,256]{2,1,0:T(8,128)S(1)}, f32[2,135,256]{2,1,0:T(8,128)S(1)}, u32[]{:S(2)}, u32[]{:S(2)}) collective-permute-start(f32[2,135,256]{2,1,0:T(8,128)S(1)} %convolution_add_fusion.6), channel_id=1, source_target_pairs={{0,16},{16,32},{32,48},{48,64},{64,80},{80,96},{96,112},{112,128},... | collective-permute-start | bytes 829448 | tf_op jit(solution)/shard_map/while/body/eval_jaxpr/ppermute | solution.py:10
  332.2 10.4 %collective-permute-start = (f32[2,135,256]{2,1,0:T(8,128)S(1)}, f32[2,135,256]{2,1,0:T(8,128)S(1)}, u32[]{:S(2)}, u32[]{:S(2)}) collective-permute-start(f32[2,135,256]{2,1,0:T(8,128)S(1)} %convolution_add_fusion.6), channel_id=1, source_target_pairs={{0,16},{16,32},{32,48},{48,64},{64,80},{80,96},{96,112},{112,128},... | collective-permute-start | bytes 829448 | tf_op jit(solution)/shard_map/while/body/eval_jaxpr/ppermute | solution.py:10
  343.0 11.2 %collective-permute-start = (f32[2,135,256]{2,1,0:T(8,128)S(1)}, f32[2,135,256]{2,1,0:T(8,128)S(1)}, u32[]{:S(2)}, u32[]{:S(2)}) collective-permute-start(f32[2,135,256]{2,1,0:T(8,128)S(1)} %convolution_add_fusion.6), channel_id=1, source_target_pairs={{0,16},{16,32},{32,48},{48,64},{64,80},{80,96},{96,112},{112,128},... | collective-permute-start | bytes 829448 | tf_op jit(solution)/shard_map/while/body/eval_jaxpr/ppermute | solution.py:10
  357.2 39.1 %copy-start.17 = (bf16[4,2,1,135,135]{4,1,3,2,0:T(2,128)(2,1)S(1)}, bf16[4,2,1,135,135]{4,1,3,2,0:T(2,128)(2,1)}, u32[]{:S(2)}) copy-start(bf16[4,2,1,135,135]{4,1,3,2,0:T(2,128)(2,1)} %param.14) | copy-start | bytes 874804
  357.5 39.3 %copy-start.18 = (bf16[4,2,1,135,135]{4,1,3,2,0:T(2,128)(2,1)S(1)}, bf16[4,2,1,135,135]{4,1,3,2,0:T(2,128)(2,1)}, u32[]{:S(2)}) copy-start(bf16[4,2,1,135,135]{4,1,3,2,0:T(2,128)(2,1)} %param.15) | copy-start | bytes 874804
  357.5 43.0 %collective-permute-start.1 = (f32[4,1,1,135,256]{4,0,3,2,1:T(4,128)S(1)}, f32[4,1,1,135,256]{4,0,3,2,1:T(4,128)S(1)}, u32[]{:S(2)}, u32[]{:S(2)}) collective-permute-start(f32[4,1,1,135,256]{4,0,3,2,1:T(4,128)S(1)} %copy.43), channel_id=1, source_target_pairs={{0,1},{1,2},{2,3},{3,4},{4,5},{5,6},{6,7},{7,8},{8,9},{9,10},{10,1... | collective-permute-start | bytes 1658888 | tf_op jit(solution)/shard_map/ppermute | solution.py:21
  394.3 10.8 %collective-permute-start.2 = (f32[4,1,1,135,256]{4,0,3,2,1:T(4,128)S(1)}, f32[4,1,1,135,256]{4,0,3,2,1:T(4,128)S(1)}, u32[]{:S(2)}, u32[]{:S(2)}) collective-permute-start(f32[4,1,1,135,256]{4,0,3,2,1:T(4,128)S(1)} %copy.46), channel_id=1, source_target_pairs={{1,0},{2,1},{3,2},{4,3},{5,4},{6,5},{7,6},{8,7},{9,8},{10,9},{11,1... | collective-permute-start | bytes 1658888 | tf_op jit(solution)/shard_map/ppermute | solution.py:23
  543.3 49.0 %copy-start.13 = (bf16[2,135,135]{1,2,0:T(8,128)(2,1)S(1)}, bf16[2,135,135]{1,2,0:T(8,128)(2,1)}, u32[]{:S(2)}) copy-start(bf16[2,135,135]{1,2,0:T(8,128)(2,1)} %copy-done.12) | copy-start | bytes 218704
  (6 other events, 6.3 us)
Sparse Core Ops, SparseCore 0:
  12.1 128.2 all-gather.4
  411.7 131.5 all-gather.6
where the time goes:
time: 606 us; the launch traced here: 604 us
  waiting for transfers between devices  293 us (48%)
  starting transfers between devices  210 us (35%)
  matrix products  77.6 us (13%)
  between operations  14.1 us (2%)
  local copies, waits for them, and re-layouts  7.71 us (1%)
    ppermute x31, starting transfers between devices, from_behind(): return lax.ppermute(block, axis, route)  171 us
    ppermute x31, waiting for transfers between devices, from_behind(): return lax.ppermute(block, axis, route)  153 us
    all_gather x2, waiting for transfers between devices, carried_in(): everything = jax.tree.map(lambda part: lax.all_gather(part, axis), value)  132 us
    dot_general x103, matrix products, precise(): jnp.einsum('nij,njr->nir', matrix, other, precision=lax.Precision.HIGHEST...  75.3 us
    ppermute x1, starting transfers between devices, with_halo(): lax.ppermute(tail, axis, [(i, (i + 1) % count) for i in range(ends)])  36.6 us
  transfers between devices with their start and end apart: 35, of which 34 were waited for; matrix products, arithmetic and copies ran while one was open for 5% of the time, Pallas kernels for 0%

commit v1 on v0

v1 whole, which is shorter than its diff:
```python
import functools

import jax
import jax.numpy as jnp
from jax import lax
from jax.experimental import pallas as pl
from jax.experimental.pallas import tpu as pltpu
from jax.sharding import PartitionSpec as P

ROW = 8
LANES = 128
F32 = jnp.float32
BF16 = jnp.bfloat16


def halves(x):
    high = x.astype(BF16)
    return high, (x - high.astype(F32)).astype(BF16)


def mul(a, b):
    return jnp.dot(a, b, preferred_element_type=F32)


def exact_by_float(a, b):
    high, low = halves(b)
    return mul(a, high) + mul(a, low)


def float_by_float(a, b):
    a_high, a_low = halves(a)
    b_high, b_low = halves(b)
    return mul(a_high, b_high) + (mul(a_high, b_low) + mul(a_low, b_high))


def lane(shape):
    return lax.broadcasted_iota(jnp.int32, shape, len(shape) - 1)


def put(ref, at, value):
    rows = value.shape[0]
    full = ref.shape[-2]
    tail = full - full % 8 if full % 8 else full - 8
    ref[(*at, slice(tail, full), slice(None))] = jnp.zeros((full - tail, ref.shape[-1]), F32)
    ref[(*at, slice(0, rows), slice(0, value.shape[1]))] = value


def pack_map(matrix):
    rows = matrix.shape[0]
    strip = jnp.where(lane((rows, LANES)) < 8, matrix[:, LANES:], 0.0)
    folded = strip[:8]
    for t in range(1, 16):
        folded = folded + pltpu.roll(strip[8 * t : 8 * t + 8], 8 * t, 1)
    return jnp.concatenate([matrix[:, :LANES], folded, strip[128:]], axis=0)


def unpack_map(block):
    rows = block.shape[0] - 16
    folded = block[rows : rows + 8]
    parts = [folded] + [pltpu.roll(folded, LANES - 8 * t, 1) for t in range(1, 16)]
    strip = jnp.concatenate(parts + [block[rows + 8 :]], axis=0)
    strip = jnp.where(lane(strip.shape) < 8, strip, 0.0)
    return jnp.concatenate([block[:rows], strip], axis=1)


def fold_rows(low, high):
    top = (low.shape[0] // 8 + 1) // 2 * 8
    under = jnp.concatenate(
        [high[top:], jnp.zeros((2 * top - high.shape[0], LANES), F32)], axis=0
    )
    return jnp.where(lane((top, LANES)) < 64, low[:top], under)


def pack_slice(pair, odd):
    turned = pltpu.roll(pair, 64, 1)
    return fold_rows(turned, pair) if odd else fold_rows(pair, turned)


def unpack_slice(block, rows, odd):
    turned = pltpu.roll(block, 64, 1)
    first, second = (turned, block) if odd else (block, turned)
    both = jnp.concatenate([first, second[: rows - block.shape[0]]], axis=0)
    keep = lane(both.shape) >= 64 if odd else lane(both.shape) < 64
    return jnp.where(keep, both, 0.0)


def prepare(inverse, before, after, source, sent, fore_maps, fore_values, back_maps, back_steps):
    positions, columns, unknowns, vectors = source.shape
    full = fore_maps.shape[-2]
    last = positions - 1
    for s in range(positions):
        for c in range(columns):
            diagonal = inverse[s, c]
            step = -mul(diagonal, before[s, c])
            value = mul(diagonal, source[s, c])
            back_steps[s, c] = jnp.zeros((full, 2 * LANES), F32)
            put(back_steps, (s, c), -mul(diagonal, after[s, c]))
            if s == 0:
                fore_maps[s, c] = jnp.zeros((full, 2 * LANES), F32)
                put(fore_maps, (s, c), step)
                put(fore_values, (s, c), value)
            else:
                put(fore_maps, (s, c), float_by_float(step, fore_maps[s - 1, c, :unknowns]))
                put(
                    fore_values,
                    (s, c),
                    value + float_by_float(step, fore_values[s - 1, c, :unknowns]),
                )
    for c in range(columns):
        back_maps[last, c] = back_steps[last, c]
    for s in range(last - 1, -1, -1):
        for c in range(columns):
            back_maps[s, c] = float_by_float(back_steps[s, c, :, :full], back_maps[s + 1, c])
    peers = ROW // columns
    room = full + 16
    for c in range(columns):
        fore = pack_map(fore_maps[last, c])
        back = pack_map(back_maps[0, c])
        for q in range(peers):
            at = c * peers + q
            sent[at, 0:room] = fore
            sent[at, room : 2 * room] = back
            pair = fore_values[last, c, :, q // 2 * LANES : (q // 2 + 1) * LANES]
            sent[at, 2 * room :] = pack_slice(pair, q % 2)


def scan_maps(full, offset, order, received, states, maps=None):
    room = full + 16
    state = None
    for k, d in enumerate(order):
        matrix = unpack_map(received[d, offset : offset + room])
        if maps is not None:
            maps[k] = matrix
        state = matrix if state is None else float_by_float(matrix[:, :full], state)
        states[k] = state


def ship_row(full, state, sent):
    block = jnp.concatenate([pack_map(state), pack_slice(state[:, LANES:], 1)], axis=0)
    for x in range(sent.shape[0]):
        sent[x] = block


def fore_scan(full, received, states, sent):
    room = full + 16
    state = None
    for d in range(ROW):
        matrix = unpack_map(received[d, 0:room])
        value = unpack_slice(received[d, 2 * room :], full, 1)
        value = jnp.concatenate([jnp.zeros_like(value), value], axis=1)
        if state is None:
            state = matrix + value
        else:
            state = float_by_float(matrix[:, :full], state) + value
        states[d] = state
    ship_row(full, state, sent)


def back_scan(full, maps, products, received, states, sent):
    value = None
    for k in range(ROW):
        piece = unpack_slice(received[ROW - 1 - k], full, 1)
        if value is None:
            value = piece
        else:
            high, low = halves(maps[k][:, :full])
            v_high = value.astype(BF16).astype(F32)
            both = (v_high + pltpu.roll(value - v_high, 64, 1)).astype(BF16)
            first = mul(high, both)
            rest = pltpu.roll(first, 64, 1) + mul(low, v_high.astype(BF16))
            value = jnp.where(lane(first.shape) >= 64, first + rest, 0.0) + piece
        state = products[k]
        state = jnp.concatenate([state[:, :LANES], state[:, LANES:] + value], axis=1)
        states[k] = state
        if k == ROW - 1:
            ship_row(full, state, sent)


def enter(full, backward, row, received, states, sent):
    rows = received.shape[0]
    room = full + 16
    order = list(range(rows - 1, 0, -1)) if backward else list(range(rows - 1))
    mine = row[0]
    value = None
    found = jnp.zeros((full, LANES), F32)
    for x in order:
        piece = unpack_slice(received[x, room:], full, 0)
        if value is not None:
            matrix = unpack_map(received[x, 0:room])
            piece = float_by_float(matrix[:, :full], value) + piece
        value = piece
        found = jnp.where(mine == (x - 1 if backward else x + 1), value, found)
    high = found.astype(BF16).astype(F32)
    low = found - high
    under = jnp.zeros((2 * LANES - 64 - full, LANES), F32)
    corner = (
        lax.broadcasted_iota(jnp.int32, (64, LANES), 0) == lane((64, LANES))
    ).astype(F32)
    top = jnp.concatenate([high, under, corner], axis=0)
    bottom = jnp.concatenate([low, under, jnp.zeros((64, LANES), F32)], axis=0)
    both = (top + pltpu.roll(bottom, 64, 1)).astype(BF16)
    stack = states[0 : ROW - 1].reshape((ROW - 1) * full, 2 * LANES)
    s_high, s_low = halves(stack)
    first = mul(s_high, both)
    every = first + (pltpu.roll(first, 64, 1) + mul(s_low, top.astype(BF16)))
    sent[ROW - 1 if backward else 0] = pack_slice(found, 0)
    for k in range(ROW - 1):
        at = ROW - 2 - k if backward else k + 1
        sent[at] = pack_slice(every[k * full : (k + 1) * full], 0)


def gather_columns(full, received, c, columns):
    peers = ROW // columns
    parts = []
    for h in range(peers // 2):
        at = c * peers + 2 * h
        parts.append(
            unpack_slice(received[at], full, 0)
            + pltpu.roll(unpack_slice(received[at + 1], full, 0), 64, 1)
        )
    return jnp.concatenate(parts, axis=1)


def spread(received, maps, base, *outs):
    positions, columns, full, vectors = base.shape
    for c in range(columns):
        entering = gather_columns(full, received, c, columns)
        stack = jnp.concatenate([maps[s, c, :, :full] for s in range(positions)], axis=0)
        product = float_by_float(stack, entering)
        for s in range(positions):
            value = product[s * full : (s + 1) * full] + base[s, c]
            if len(outs) == 1:
                rows = outs[0].shape[-2]
                outs[0][s, c] = value[:rows]
            else:
                outs[c][s] = value


def own_part(inverse, lower, upper, head, tail, own):
    positions, columns, unknowns, _ = inverse.shape
    forward = (head, tail)
    for s in range(positions):
        for c in range(columns):
            value = forward[c][s]
            near = upper[s, c] if c == 0 else lower[s, c]
            drop = exact_by_float(near, forward[1 - c][s, :unknowns])
            put(own, (s, c), value[:unknowns] - exact_by_float(inverse[s, c], drop))


def back_part(inverse, lower, upper, below, above, steps, own, values, sent):
    positions, columns, unknowns, _ = inverse.shape
    full = own.shape[-2]
    halo = (below, above)
    for s in range(positions - 1, -1, -1):
        for c in range(columns):
            far = lower[s, c] if c == 0 else upper[s, c]
            drop = exact_by_float(far, halo[c][s, :unknowns])
            put(values, (s, c), own[s, c, :unknowns] - exact_by_float(inverse[s, c], drop))
            if s < positions - 1:
                values[s, c] += float_by_float(steps[s, c, :, :full], values[s + 1, c])
    peers = ROW // columns
    for c in range(columns):
        for q in range(peers):
            pair = values[0, c, :, q // 2 * LANES : (q // 2 + 1) * LANES]
            sent[c * peers + q] = pack_slice(pair, q % 2)


def call(kernel, outs, *args, flops=10**8, smem=()):
    vmem = pl.BlockSpec(memory_space=pltpu.VMEM)
    moved = sum(a.size * a.dtype.itemsize for a in args)
    return pl.pallas_call(
        kernel,
        out_shape=[jax.ShapeDtypeStruct(shape, F32) for shape in outs],
        in_specs=[
            pl.BlockSpec(memory_space=pltpu.SMEM) if i in smem else vmem for i in range(len(args))
        ],
        out_specs=[vmem] * len(outs),
        compiler_params=pltpu.CompilerParams(vmem_limit_bytes=28 * 2**20),
        cost_estimate=pl.CostEstimate(flops=flops, bytes_accessed=moved, transcendentals=0),
    )(*args)


def shards(source, inv_diag, upstream, downstream, cross_lower, cross_upper):
    positions, columns, planes, unknowns, vectors = source.shape
    squeeze = lambda a: a.reshape(positions, columns, *a.shape[3:])
    source, inverse, before = squeeze(source), squeeze(inv_diag), squeeze(upstream)
    after, lower, upper = squeeze(downstream), squeeze(cross_lower), squeeze(cross_upper)
    full = -(-unknowns // 8) * 8
    room = full + 16
    fold = (full // 8 + 1) // 2 * 8
    count = lax.axis_size("sweep")
    rows = count // ROW
    inside = [[r * ROW + i for i in range(ROW)] for r in range(rows)]
    across = [[r * ROW + i for r in range(rows)] for i in range(ROW)]
    row = (lax.axis_index("sweep") // ROW).astype(jnp.int32).reshape(1)
    block = (positions, columns, full, 2 * LANES)

    def exchange(x, groups):
        return lax.all_to_all(x, "sweep", 0, 0, axis_index_groups=groups)

    sent, fore_maps, fore_values, back_maps, back_steps = call(
        prepare,
        [(ROW, 2 * room + fold, LANES), block, block, block, block],
        inverse,
        before,
        after,
        source,
    )
    received = exchange(sent, inside)
    states, sent = call(
        functools.partial(fore_scan, full),
        [(ROW, full, 2 * LANES), (rows, room + fold, LANES)],
        received,
    )
    joined = exchange(sent, across)
    (sent,) = call(
        functools.partial(enter, full, False),
        [(ROW, fold, LANES)],
        row,
        joined,
        states,
        smem=(0,),
    )
    entering = exchange(sent, inside)
    head, tail = call(
        spread, [(positions, full, vectors)] * 2, entering, fore_maps, fore_values
    )
    ends = lax.axis_size("cross") - 1
    below = lax.ppermute(tail, "cross", [(i, i + 1) for i in range(ends)])
    above = lax.ppermute(head, "cross", [(i + 1, i) for i in range(ends)])
    (own,) = call(own_part, [block], inverse, lower, upper, head, tail)
    products, maps = call(
        functools.partial(scan_maps, full, room, range(ROW - 1, -1, -1)),
        [(ROW, full, 2 * LANES)] * 2,
        received,
    )
    values, sent = call(
        back_part,
        [block, (ROW, fold, LANES)],
        inverse,
        lower,
        upper,
        below,
        above,
        back_steps,
        own,
    )
    received = exchange(sent, inside)
    states, sent = call(
        functools.partial(back_scan, full),
        [(ROW, full, 2 * LANES), (rows, room + fold, LANES)],
        maps,
        products,
        received,
    )
    joined = exchange(sent, across)
    (sent,) = call(
        functools.partial(enter, full, True),
        [(ROW, fold, LANES)],
        row,
        joined,
        states,
        smem=(0,),
    )
    entering = exchange(sent, inside)
    (update,) = call(
        spread, [(positions, columns, unknowns, vectors)], entering, back_maps, values
    )
    return update.reshape(positions, columns, planes, unknowns, vectors)


def solution(mesh):
    placed = P("sweep", "cross", None, None, None)
    return jax.shard_map(
        shards,
        mesh=mesh,
        in_specs=(placed,) * 6,
        out_specs=placed,
        check_vma=False,
    )
```

time: 606 us -> 153 us (0.25)
  the two profiles are of different devices: /device:TPU:1 before, /device:TPU:256 now
where the time goes in v1:
time: 153 us; the launch traced here: 152 us
  blocking collectives  85.3 us (56%)
  waiting for transfers between devices  24.4 us (16%)
  Pallas kernels  16.5 us (11%)
  starting transfers between devices  14.5 us (9%)
  local copies, waits for them, and re-layouts  11.5 us (8%)
    all_to_all x4, blocking collectives, exchange(): return lax.all_to_all(x, 'sweep', 0, 0, axis_index_groups=groups)  85.3 us
    all_to_all x2, waiting for transfers between devices, exchange(): return lax.all_to_all(x, 'sweep', 0, 0, axis_index_groups=groups)  18.5 us
    pallas_call x10, Pallas kernels, call(): pl.pallas_call(kernel, out_shape=[jax.ShapeDtypeStruct(shape, F32) for sh...  16.5 us
    unnamed x40, local copies, waits for them, and re-layouts  9.08 us
    all_to_all x2, starting transfers between devices, exchange(): return lax.all_to_all(x, 'sweep', 0, 0, axis_index_groups=groups)  7.72 us
    ppermute x1, starting transfers between devices, shards(): above = lax.ppermute(head, 'cross', [(i + 1, i) for i in range(ends)])  4.85 us
    ppermute x1, waiting for transfers between devices, shards(): below = lax.ppermute(tail, 'cross', [(i, i + 1) for i in range(ends)])  4.13 us
  transfers between devices with their start and end apart: 4, of which 4 were waited for; matrix products, arithmetic and copies ran while one was open for 0% of the time, Pallas kernels for 2%

profile of v1, /device:TPU:256, one launch (start us, length us, event | category | flops | bytes accessed | tf_op | source)
XLA Modules:
  0.0 152.4 jit_solution(18328313974640541558)
XLA Ops:
  0.0 1.3 copy.21
  1.3 0.0 copy-done.14
  1.3 0.1 copy.20
  1.4 0.0 copy-done.16
  1.4 0.2 copy-done.15
  1.6 0.2 copy_bitcast_fusion.3
  1.7 2.6 %shard_map.64 = (f32[8,376,128]{2,1,0:T(8,128)S(1)}, f32[4,2,136,256]{3,2,1,0:T(8,128)S(1)}, f32[4,2,136,256]{3,2,1,0:T(8,128)S(1)}, f32[4,2,136,256]{3,2,1,0:T(8,128)S(1)}, f32[4,2,136,256]{3,2,1,0:T(8,128)S(1)}) custom-call(bf16[4,2,135,135]{3,2,1,0:T(8,128)(2,1)S(1)} %bitcast.16, bf16[4,2,135,135]{3,2,1,0:T(8,128)(2,1)S(1)} %get-tuple-element.36.before, ...), custom_call_target="tpu_custom_call" | custom-call | flops 100000000 | bytes 1427760 | tf_op jit(solution)/shard_map/pallas_call | solution.py:271
  4.3 0.0 copy-start.4
  4.3 1.0 copy-done.4
  5.3 1.0 copy-done.8
  6.3 46.1 %all_to_all.30.received = f32[8,376,128]{2,1,0:T(8,128)S(1)} all-to-all(f32[8,376,128]{2,1,0:T(8,128)S(1)} %get-tuple-element.20), channel_id=1, replica_groups={{0,16,32,48,64,80,96,112},{128,144,160,176,192,208,224,240},{256,272,28..., dimensions={0} | all-to-all | bytes 3080192 | tf_op jit(solution)/shard_map/all_to_all | solution.py:299
  52.5 0.0 copy-done
  52.5 0.0 copy-done.2
  52.5 2.5 %shard_map.66 = (f32[8,136,256]{2,1,0:T(8,128)S(1)}, f32[4,224,128]{2,1,0:T(8,128)}) custom-call(f32[8,376,128]{2,1,0:T(8,128)S(1)} %all_to_all.30.received), custom_call_target="tpu_custom_call" | custom-call | flops 100000000 | bytes 1540096 | tf_op jit(solution)/shard_map/pallas_call | solution.py:271
  55.0 1.0 copy-done.10
  56.0 4.3 %all-to-all-start.1 = ((f32[4,224,128]{2,1,0:T(8,128)}), f32[4,224,128]{2,1,0:T(8,128)S(1)}, u32[]{:S(2)}, u32[]{:S(2)}) async-start(f32[4,224,128]{2,1,0:T(8,128)} %get-tuple-element.23), calls=%async_computation.1 | async-start | bytes 917504 | tf_op jit(solution)/shard_map/all_to_all | solution.py:299
  60.3 7.7 %all-to-all-done.1.received = f32[4,224,128]{2,1,0:T(8,128)S(1)} async-done(((f32[4,224,128]{2,1,0:T(8,128)}), f32[4,224,128]{2,1,0:T(8,128)S(1)}, u32[]{:S(2)}, u32[]{:S(2)}) %all-to-all-start.1) | async-done | bytes 458784 | tf_op jit(solution)/shard_map/all_to_all | solution.py:299
  68.1 1.2 copy-done.11
  69.3 1.1 shard_map.67
  70.4 13.2 %all_to_all.31.received = f32[8,72,128]{2,1,0:T(8,128)S(1)} all-to-all(f32[8,72,128]{2,1,0:T(8,128)S(1)} %shard_map.67), channel_id=1, replica_groups={{0,16,32,48,64,80,96,112},{128,144,160,176,192,208,224,240},{256,272,28..., dimensions={0} | all-to-all | bytes 589824 | tf_op jit(solution)/shard_map/all_to_all | solution.py:299
  83.6 0.0 copy-done.3
  83.6 0.0 copy-done.5
  83.6 0.8 shard_map.68
  84.4 1.9 %collective-permute-start = (f32[4,136,256]{2,1,0:T(8,128)S(1)}, f32[4,136,256]{2,1,0:T(8,128)S(1)}, u32[]{:S(2)}, u32[]{:S(2)}) collective-permute-start(f32[4,136,256]{2,1,0:T(8,128)S(1)} %get-tuple-element.27.tail), channel_id=1, source_target_pairs={{0,1},{1,2},{2,3},{3,4},{4,5},{5,6},{6,7},{7,8},{8,9},{9,10},{10,1... | collective-permute-start | bytes 1671176 | tf_op jit(solution)/shard_map/ppermute | solution.py:329
  86.4 4.9 %collective-permute-start.1 = (f32[4,136,256]{2,1,0:T(8,128)S(1)}, f32[4,136,256]{2,1,0:T(8,128)S(1)}, u32[]{:S(2)}, u32[]{:S(2)}) collective-permute-start(f32[4,136,256]{2,1,0:T(8,128)S(1)} %get-tuple-element.28.head), channel_id=1, source_target_pairs={{1,0},{2,1},{3,2},{4,3},{5,4},{6,5},{7,6},{8,7},{9,8},{10,9},{11,1... | collective-permute-start | bytes 1671176 | tf_op jit(solution)/shard_map/ppermute | solution.py:330
  91.2 0.0 copy-done.17
  91.2 0.0 copy-done.18
  91.3 0.2 copy_bitcast_fusion
  91.4 0.0 copy-start.1
  91.4 0.9 shard_map.69.own
  92.4 4.1 %collective-permute-done.below = f32[4,136,256]{2,1,0:T(8,128)S(1)} collective-permute-done((f32[4,136,256]{2,1,0:T(8,128)S(1)}, f32[4,136,256]{2,1,0:T(8,128)S(1)}, u32[]{:S(2)}, u32[]{:S(2)}) %collective-permute-start) | collective-permute-done | bytes 557088 | tf_op jit(solution)/shard_map/ppermute | solution.py:329
  96.5 1.8 %collective-permute-done.1.above = f32[4,136,256]{2,1,0:T(8,128)S(1)} collective-permute-done((f32[4,136,256]{2,1,0:T(8,128)S(1)}, f32[4,136,256]{2,1,0:T(8,128)S(1)}, u32[]{:S(2)}, u32[]{:S(2)}) %collective-permute-start.1) | collective-permute-done | bytes 557088 | tf_op jit(solution)/shard_map/ppermute | solution.py:330
  98.3 0.0 copy-done.1
  98.3 2.7 %shard_map.70 = (f32[4,2,136,256]{3,2,1,0:T(8,128)S(1)}, f32[8,72,128]{2,1,0:T(8,128)}) custom-call(bf16[4,2,135,135]{3,2,1,0:T(8,128)(2,1)S(1)} %bitcast.18, bf16[4,2,135,135]{3,2,1,0:T(8,128)(2,1)S(1)} %get-tuple-element.38.lower, bf16[4,2,135,135]{3,2,1,0:T(8,128)(2,1)S(1)} %get-tuple-element.37.upper, f32[4,136,256]{2,1,0:T(8,128)S(1)} %collective-permute-done.below, ...), custom_call_target="tpu_custom_call" | custom-call | flops 100000000 | bytes 4217136 | tf_op jit(solution)/shard_map/pallas_call | solution.py:271
  101.0 1.0 copy-done.12
  102.0 3.4 %all-to-all-start.3 = ((f32[8,72,128]{2,1,0:T(8,128)}), f32[8,72,128]{2,1,0:T(8,128)S(1)}, u32[]{:S(2)}, u32[]{:S(2)}) async-start(f32[8,72,128]{2,1,0:T(8,128)} %get-tuple-element.30), calls=%async_computation.3 | async-start | bytes 589824 | tf_op jit(solution)/shard_map/all_to_all | solution.py:299
  105.4 1.6 %shard_map.65 = (f32[8,136,256]{2,1,0:T(8,128)S(1)}, f32[8,136,256]{2,1,0:T(8,128)S(1)}) custom-call(f32[8,376,128]{2,1,0:T(8,128)S(1)} %all_to_all.30.received), custom_call_target="tpu_custom_call" | custom-call | flops 100000000 | bytes 1540096 | tf_op jit(solution)/shard_map/pallas_call | solution.py:271
  107.1 0.0 copy-start.6
  107.1 1.0 copy-done.6
  108.1 10.8 %all-to-all-done.3.received = f32[8,72,128]{2,1,0:T(8,128)S(1)} async-done(((f32[8,72,128]{2,1,0:T(8,128)}), f32[8,72,128]{2,1,0:T(8,128)S(1)}, u32[]{:S(2)}, u32[]{:S(2)}) %all-to-all-start.3) | async-done | bytes 294944 | tf_op jit(solution)/shard_map/all_to_all | solution.py:299
  118.9 1.2 copy-done.7
  120.1 2.3 %shard_map.71 = (f32[8,136,256]{2,1,0:T(8,128)S(1)}, f32[4,224,128]{2,1,0:T(8,128)S(1)}) custom-call(f32[8,136,256]{2,1,0:T(8,128)S(1)} %copy-done.7, f32[8,136,256]{2,1,0:T(8,128)S(1)} %get-tuple-element.22.products, f32[8,72,128]{2,1,0:T(8,128)S(1)} %all-to-all-done.3.received), custom_call_target="tpu_custom_call" | custom-call | flops 100000000 | bytes 2523136 | tf_op jit(solution)/shard_map/pallas_call | solution.py:271
  122.4 11.7 %all_to_all.32.received = f32[4,224,128]{2,1,0:T(8,128)S(1)} all-to-all(f32[4,224,128]{2,1,0:T(8,128)S(1)} %get-tuple-element.31), channel_id=1, replica_groups={{0,128,256,384},{16,144,272,400},{32,160,288,416},{48,176,304,432},{64,..., dimensions={0} | all-to-all | bytes 917504 | tf_op jit(solution)/shard_map/all_to_all | solution.py:299
  134.1 1.1 shard_map.72
  135.2 14.3 %all_to_all.33.received = f32[8,72,128]{2,1,0:T(8,128)S(1)} all-to-all(f32[8,72,128]{2,1,0:T(8,128)S(1)} %shard_map.72), channel_id=1, replica_groups={{0,16,32,48,64,80,96,112},{128,144,160,176,192,208,224,240},{256,272,28..., dimensions={0} | all-to-all | bytes 589824 | tf_op jit(solution)/shard_map/all_to_all | solution.py:299
  149.5 0.0 copy-done.9
  149.5 0.8 shard_map.73
  150.3 2.1 %copy.13 = f32[4,2,1,135,256]{4,2,3,1,0:T(1,128)} copy(f32[4,2,1,135,256]{4,3,1,0,2:T(8,128)S(1)} %bitcast.19) | data formatting | bytes 2211840 | tf_op jit(solution)/shard_map/reshape | solution.py:369
  (17 shorter events, 0.0 us)
Async XLA Ops:
  0.0 1.3 copy-start.14
  0.0 1.4 copy-start.16
  0.0 1.5 %copy-start.15 = (bf16[4,2,1,135,135]{4,1,3,2,0:T(2,128)(2,1)S(1)}, bf16[4,2,1,135,135]{4,1,3,2,0:T(2,128)(2,1)}, u32[]{:S(2)}) copy-start(bf16[4,2,1,135,135]{4,1,3,2,0:T(2,128)(2,1)} %param.9) | copy-start | bytes 874804
  4.3 1.0 copy-start.4
  5.3 1.0 copy-start.8
  6.3 46.1 %copy-start = (f32[4,2,136,256]{3,2,1,0:T(8,128)}, f32[4,2,136,256]{3,2,1,0:T(8,128)S(1)}, u32[]{:S(2)}) copy-start(f32[4,2,136,256]{3,2,1,0:T(8,128)S(1)} %get-tuple-element.29.steps) | copy-start | bytes 3342340
  6.3 46.1 %copy-start.2 = (f32[4,2,136,256]{3,2,1,0:T(8,128)}, f32[4,2,136,256]{3,2,1,0:T(8,128)S(1)}, u32[]{:S(2)}) copy-start(f32[4,2,136,256]{3,2,1,0:T(8,128)S(1)} %get-tuple-element.25.maps) | copy-start | bytes 3342340
  55.0 1.0 copy-start.10
  56.0 12.0 %all-to-all-start.1 = ((f32[4,224,128]{2,1,0:T(8,128)}), f32[4,224,128]{2,1,0:T(8,128)S(1)}, u32[]{:S(2)}, u32[]{:S(2)}) async-start(f32[4,224,128]{2,1,0:T(8,128)} %get-tuple-element.23), calls=%async_computation.1 | async-start | bytes 917504 | tf_op jit(solution)/shard_map/all_to_all | solution.py:299
  68.1 1.2 copy-start.11
  69.3 14.3 %copy-start.3 = (f32[4,2,136,256]{3,2,1,0:T(8,128)S(1)}, f32[4,2,136,256]{3,2,1,0:T(8,128)}, u32[]{:S(2)}) copy-start(f32[4,2,136,256]{3,2,1,0:T(8,128)} %copy-done.2) | copy-start | bytes 3342340
  69.3 14.3 %copy-start.5 = (f32[4,2,136,256]{3,2,1,0:T(8,128)S(1)}, f32[4,2,136,256]{3,2,1,0:T(8,128)}, u32[]{:S(2)}) copy-start(f32[4,2,136,256]{3,2,1,0:T(8,128)} %copy-done.4) | copy-start | bytes 3342340
  83.6 7.6 %copy-start.17 = (bf16[4,2,1,135,135]{4,1,3,2,0:T(2,128)(2,1)S(1)}, bf16[4,2,1,135,135]{4,1,3,2,0:T(2,128)(2,1)}, u32[]{:S(2)}) copy-start(bf16[4,2,1,135,135]{4,1,3,2,0:T(2,128)(2,1)} %param.11) | copy-start | bytes 874804
  83.6 7.6 %copy-start.18 = (bf16[4,2,1,135,135]{4,1,3,2,0:T(2,128)(2,1)S(1)}, bf16[4,2,1,135,135]{4,1,3,2,0:T(2,128)(2,1)}, u32[]{:S(2)}) copy-start(bf16[4,2,1,135,135]{4,1,3,2,0:T(2,128)(2,1)} %param.10) | copy-start | bytes 874804
  84.4 12.1 %collective-permute-start = (f32[4,136,256]{2,1,0:T(8,128)S(1)}, f32[4,136,256]{2,1,0:T(8,128)S(1)}, u32[]{:S(2)}, u32[]{:S(2)}) collective-permute-start(f32[4,136,256]{2,1,0:T(8,128)S(1)} %get-tuple-element.27.tail), channel_id=1, source_target_pairs={{0,1},{1,2},{2,3},{3,4},{4,5},{5,6},{6,7},{7,8},{8,9},{9,10},{10,1... | collective-permute-start | bytes 1671176 | tf_op jit(solution)/shard_map/ppermute | solution.py:329
  86.4 11.9 %collective-permute-start.1 = (f32[4,136,256]{2,1,0:T(8,128)S(1)}, f32[4,136,256]{2,1,0:T(8,128)S(1)}, u32[]{:S(2)}, u32[]{:S(2)}) collective-permute-start(f32[4,136,256]{2,1,0:T(8,128)S(1)} %get-tuple-element.28.head), channel_id=1, source_target_pairs={{1,0},{2,1},{3,2},{4,3},{5,4},{6,5},{7,6},{8,7},{9,8},{10,9},{11,1... | collective-permute-start | bytes 1671176 | tf_op jit(solution)/shard_map/ppermute | solution.py:330
  91.4 6.9 %copy-start.1 = (f32[4,2,136,256]{3,2,1,0:T(8,128)S(1)}, f32[4,2,136,256]{3,2,1,0:T(8,128)}, u32[]{:S(2)}) copy-start(f32[4,2,136,256]{3,2,1,0:T(8,128)} %copy-done) | copy-start | bytes 3342340
  101.0 1.0 copy-start.12
  102.0 16.9 %all-to-all-start.3 = ((f32[8,72,128]{2,1,0:T(8,128)}), f32[8,72,128]{2,1,0:T(8,128)S(1)}, u32[]{:S(2)}, u32[]{:S(2)}) async-start(f32[8,72,128]{2,1,0:T(8,128)} %get-tuple-element.30), calls=%async_computation.3 | async-start | bytes 589824 | tf_op jit(solution)/shard_map/all_to_all | solution.py:299
  107.1 1.0 copy-start.6
  118.9 1.2 copy-start.7
  134.1 15.4 %copy-start.9 = (f32[4,2,136,256]{3,2,1,0:T(8,128)S(1)}, f32[4,2,136,256]{3,2,1,0:T(8,128)}, u32[]{:S(2)}) copy-start(f32[4,2,136,256]{3,2,1,0:T(8,128)} %copy-done.8) | copy-start | bytes 3342340
  134.1 15.4 %copy-start.13 = (f32[4,2,136,256]{3,2,1,0:T(8,128)S(1)}, f32[4,2,136,256]{3,2,1,0:T(8,128)}, u32[]{:S(2)}) copy-start(f32[4,2,136,256]{3,2,1,0:T(8,128)} %copy-done.12) | copy-start | bytes 3342340

commit v2 on v1

v2 whole, which is shorter than its diff:
```python
import functools

import jax
import jax.numpy as jnp
from jax import lax
from jax.experimental import pallas as pl
from jax.experimental.pallas import tpu as pltpu
from jax.sharding import PartitionSpec as P

ROW = 8
LANES = 128
F32 = jnp.float32
BF16 = jnp.bfloat16


def halves(x):
    high = x.astype(BF16)
    return high, (x - high.astype(F32)).astype(BF16)


def mul(a, b):
    return jnp.dot(a, b, preferred_element_type=F32)


def exact_by_float(a, b):
    high, low = halves(b)
    return mul(a, high) + mul(a, low)


def float_by_float(a, b):
    a_high, a_low = halves(a)
    b_high, b_low = halves(b)
    return mul(a_high, b_high) + (mul(a_high, b_low) + mul(a_low, b_high))


def lane(shape):
    return lax.broadcasted_iota(jnp.int32, shape, len(shape) - 1)


def put(ref, at, value):
    rows = value.shape[0]
    full = ref.shape[-2]
    tail = full - full % 8 if full % 8 else full - 8
    ref[(*at, slice(tail, full), slice(None))] = jnp.zeros((full - tail, ref.shape[-1]), F32)
    ref[(*at, slice(0, rows), slice(0, value.shape[1]))] = value


def pack_map(matrix, width=7):
    rows = matrix.shape[0]
    strip = jnp.where(lane((rows, LANES)) < width, matrix[:, LANES:], 0.0)
    folded = strip[:8]
    for t in range(1, rows // 8):
        folded = folded + pltpu.roll(strip[8 * t : 8 * t + 8], width * t, 1)
    return jnp.concatenate([matrix[:, :LANES], folded], axis=0)


def unpack_map(block, width=7):
    rows = block.shape[0] - 8
    folded = block[rows:]
    parts = [folded] + [pltpu.roll(folded, LANES - width * t, 1) for t in range(1, rows // 8)]
    strip = jnp.concatenate(parts, axis=0)
    strip = jnp.where(lane(strip.shape) < width, strip, 0.0)
    return jnp.concatenate([block[:rows], strip], axis=1)


def fold_rows(low, high):
    top = (low.shape[0] // 8 + 1) // 2 * 8
    under = jnp.concatenate(
        [high[top:], jnp.zeros((2 * top - high.shape[0], LANES), F32)], axis=0
    )
    return jnp.where(lane((top, LANES)) < 64, low[:top], under)


def pack_slice(pair, odd):
    turned = pltpu.roll(pair, 64, 1)
    return fold_rows(turned, pair) if odd else fold_rows(pair, turned)


def unpack_slice(block, rows, odd):
    turned = pltpu.roll(block, 64, 1)
    first, second = (turned, block) if odd else (block, turned)
    both = jnp.concatenate([first, second[: rows - block.shape[0]]], axis=0)
    keep = lane(both.shape) >= 64 if odd else lane(both.shape) < 64
    return jnp.where(keep, both, 0.0)


def compose(inverse, before, source, fore):
    positions, columns, unknowns, _ = source.shape
    full = fore.shape[-2]
    for s in range(positions):
        for c in range(columns):
            diagonal = inverse[s, c]
            step = -mul(diagonal, before[s, c])
            value = mul(diagonal, source[s, c])
            if s == 0:
                fore[c][s, 0] = jnp.zeros((full, 2 * LANES), F32)
                put(fore[c], (s, 0), step)
                put(fore[c], (s, 1), value)
            else:
                put(fore[c], (s, 0), float_by_float(step, fore[c][s - 1, 0, :unknowns]))
                put(fore[c], (s, 1), value + float_by_float(step, fore[c][s - 1, 1, :unknowns]))


class Pair(tuple):
    @property
    def shape(self):
        return self[0].shape


def compose_back(inverse, after, maps, steps):
    positions, columns = inverse.shape[:2]
    full = maps.shape[-2]
    last = positions - 1
    for s in range(positions):
        for c in range(columns):
            steps[s, c] = jnp.zeros((full, 2 * LANES), F32)
            put(steps, (s, c), -mul(inverse[s, c], after[s, c]))
    for c in range(columns):
        maps[last, c] = steps[last, c]
    for s in range(last - 1, -1, -1):
        for c in range(columns):
            maps[s, c] = float_by_float(steps[s, c, :, :full], maps[s + 1, c])


def start(inverse, before, after, source, sent, head, tail, maps, steps):
    positions, columns = source.shape[:2]
    full = head.shape[-2]
    last = positions - 1
    fore = Pair((head, tail))
    compose(inverse, before, source, fore)
    compose_back(inverse, after, maps, steps)
    peers = ROW // columns
    room = full + 8
    for c in range(columns):
        forth, back = pack_map(fore[c][last, 0]), pack_map(maps[0, c])
        for q in range(peers):
            at = c * peers + q
            sent[at, 0:room] = forth
            sent[at, room : 2 * room] = back
            pair = fore[c][last, 1, :, q // 2 * LANES : (q // 2 + 1) * LANES]
            sent[at, 2 * room :] = pack_slice(pair, q % 2)


def prepare(inverse, before, source, first, second, head, tail):
    positions, columns = source.shape[:2]
    full = head.shape[-2]
    room = full + 8
    compose(inverse, before, source, Pair((head, tail)))
    for fore, sent in ((head, first), (tail, second)):
        for s in range(positions):
            sent[s, 0:room] = pack_map(fore[s, 0])
            sent[s, room : room + full] = fore[s, 1, :, :LANES]
            sent[s, room + full :] = fore[s, 1, :, LANES:]


def ship_row(full, state, sent):
    block = jnp.concatenate([pack_map(state), pack_slice(state[:, LANES:], 1)], axis=0)
    for x in range(sent.shape[0]):
        sent[x] = block


def unpack_step(full, matrix, block):
    value = unpack_slice(block, full, 1)
    return unpack_map(matrix) + jnp.concatenate([jnp.zeros_like(value), value], axis=1)


def follow(full, earlier, later):
    product = float_by_float(later[:, :full], earlier)
    kept = lane((full, LANES)) >= 64
    value = jnp.where(kept, later[:, LANES:], 0.0)
    return product + jnp.concatenate([jnp.zeros_like(value), value], axis=1)


def whole_run(full, order, matrices, blocks, sent):
    steps = [unpack_step(full, matrices[d], blocks[d]) for d in order]
    while len(steps) > 1:
        steps = [follow(full, *steps[k : k + 2]) for k in range(0, len(steps), 2)]
    ship_row(full, steps[0], sent)


def prefixes(full, order, matrices, blocks, states):
    state = None
    for k, d in enumerate(order[: states.shape[0]]):
        step = unpack_step(full, matrices[d], blocks[d])
        state = step if state is None else follow(full, state, step)
        states[k] = state


def fore_views(full, received):
    room = full + 8
    return received.at[:, 0:room], received.at[:, 2 * room :]


def fore_run(full, received, sent):
    whole_run(full, range(ROW), *fore_views(full, received), sent)


def fore_prefixes(full, received, states, later, sem):
    room = full + 8
    copy = pltpu.make_async_copy(received.at[:, room : 2 * room], later, sem)
    copy.start()
    prefixes(full, range(ROW), *fore_views(full, received), states)
    copy.wait()


def enter(full, backward, row, received, states, sent):
    rows = received.shape[0]
    room = full + 8
    order = list(range(rows - 1, 0, -1)) if backward else list(range(rows - 1))
    mine = row[0]
    value = None
    found = jnp.zeros((full, LANES), F32)
    for x in order:
        piece = unpack_slice(received[x, room:], full, 0)
        if value is not None:
            matrix = unpack_map(received[x, 0:room])
            piece = float_by_float(matrix[:, :full], value) + piece
        value = piece
        found = jnp.where(mine == (x - 1 if backward else x + 1), value, found)
    high = found.astype(BF16).astype(F32)
    low = found - high
    under = jnp.zeros((2 * LANES - 64 - full, LANES), F32)
    corner = (
        lax.broadcasted_iota(jnp.int32, (64, LANES), 0) == lane((64, LANES))
    ).astype(F32)
    top = jnp.concatenate([high, under, corner], axis=0)
    bottom = jnp.concatenate([low, under, jnp.zeros((64, LANES), F32)], axis=0)
    both = (top + pltpu.roll(bottom, 64, 1)).astype(BF16)
    stack = states[...].reshape((ROW - 1) * full, 2 * LANES)
    s_high, s_low = halves(stack)
    first = mul(s_high, both)
    every = first + (pltpu.roll(first, 64, 1) + mul(s_low, top.astype(BF16)))
    sent[ROW - 1 if backward else 0] = pack_slice(found, 0)
    for k in range(ROW - 1):
        at = ROW - 2 - k if backward else k + 1
        sent[at] = pack_slice(every[k * full : (k + 1) * full], 0)


def unpack_columns(full, received, first, count):
    parts = []
    for h in range(count // 2):
        at = first + 2 * h
        parts.append(
            unpack_slice(received[at], full, 0)
            + pltpu.roll(unpack_slice(received[at + 1], full, 0), 64, 1)
        )
    return jnp.concatenate(parts, axis=1)


def couple(inverse, lower, upper, head, tail, below, above, steps, plan, more):
    positions, columns, unknowns, _ = inverse.shape
    full = plan.shape[-2]
    room = full + 8
    forward = (head, tail)
    halo = (below, above)
    for c in range(columns):
        near, far = (upper, lower) if c == 0 else (lower, upper)
        kept = None
        for s in range(positions - 1, -1, -1):
            by_near = mul(inverse[s, c], near[s, c])
            by_far = mul(inverse[s, c], far[s, c])
            far_map = unpack_map(halo[c][s, 0:room])
            far_value = jnp.concatenate(
                [halo[c][s, room : room + full], halo[c][s, room + full :]], axis=1
            )
            parts = [
                forward[c][s, 0, :unknowns],
                -float_by_float(by_near, forward[1 - c][s, 0, :unknowns]),
                -float_by_float(by_far, far_map[:unknowns]),
                forward[c][s, 1, :unknowns]
                - float_by_float(by_near, forward[1 - c][s, 1, :unknowns])
                - float_by_float(by_far, far_value[:unknowns]),
            ]
            if kept is not None:
                step = steps[s, c, :unknowns, :unknowns]
                parts = [part + float_by_float(step, old) for part, old in zip(parts, kept)]
            kept = parts
            for k in range(4):
                put(*((plan, (c, k)) if s == 0 else (more, (s - 1, c, k))), kept[k])


def near_part(received, plan, part):
    columns, full, _ = part.shape
    peers = ROW // columns
    entering = [unpack_columns(full, received, c * peers, peers) for c in range(columns)]
    for c in range(columns):
        part[c] = plan[c, 3] + (
            float_by_float(plan[c, 0, :, :full], entering[c])
            + float_by_float(plan[c, 1, :, :full], entering[1 - c])
        )


def far_part(below, above, plan, part, sent, values):
    columns, full, _ = part.shape
    peers = ROW // columns
    halo = (below, above)
    for c in range(columns):
        entering = unpack_columns(full, halo[c], 0, peers)
        value = part[c] + float_by_float(plan[c, 2, :, :full], entering)
        values[c] = value
        for q in range(peers):
            pair = value[:, q // 2 * LANES : (q // 2 + 1) * LANES]
            sent[c * peers + q] = pack_slice(pair, q % 2)


def levels(received, below, above, more, values):
    others, columns, full, _ = values.shape
    peers = ROW // columns
    entering = [unpack_columns(full, received, c * peers, peers) for c in range(columns)]
    halo = [unpack_columns(full, got, 0, peers) for got in (below, above)]
    for c in range(columns):
        total = None
        for k, value in enumerate((entering[c], entering[1 - c], halo[c])):
            stack = jnp.concatenate([more[s, c, k, :, :full] for s in range(others)], axis=0)
            product = float_by_float(stack, value)
            total = product if total is None else total + product
        for s in range(others):
            values[s, c] = more[s, c, 3] + total[s * full : (s + 1) * full]


def finish(received, maps, first, rest, result, out, sems):
    positions, columns, full, vectors = maps.shape
    peers = ROW // columns
    total = out.shape[0]
    unknowns = total // (2 * positions * columns)
    entering = [unpack_columns(full, received, c * peers, peers) for c in range(columns)]
    copies = []
    for part in range(2):
        levels = range(part * positions // 2, (part + 1) * positions // 2)
        for c in range(columns):
            stack = jnp.concatenate([maps[s, c, :, :full] for s in levels], axis=0)
            product = float_by_float(stack, entering[c])
            for k, s in enumerate(levels):
                value = product[k * full : (k + 1) * full] + (rest[s - 1, c] if s else first[c])
                at = 2 * unknowns * (s * columns + c)
                for h in range(2):
                    half = value[:unknowns, h * LANES : (h + 1) * LANES]
                    out[pl.ds(at + h, unknowns, stride=2), :] = half
        span = pl.ds(part * total // 2, total // 2)
        copies.append(pltpu.make_async_copy(out.at[span], result.at[span], sems.at[part]))
        copies[-1].start()
    for copy in copies:
        copy.wait()


def call(kernel, outs, *args, us, smem=(), scratch=(), kept=0, direct=0):
    vmem, hbm = (pl.BlockSpec(memory_space=space) for space in (pltpu.VMEM, pltpu.HBM))
    away = kept or direct
    near = len(outs) - away

    def with_copies(*refs):
        refs, sems = refs[:-1], refs[-1]
        ins, rest = refs[: len(args)], refs[len(args) :]
        results, far, rest = rest[:near], rest[near : len(outs)], rest[len(outs) :]
        staged, rest = rest[:kept], rest[kept:]
        kernel(*ins, *results, *staged, *rest)
        copies = [
            pltpu.make_async_copy(here, there, sems.at[k])
            for k, (here, there) in enumerate(zip(staged, far))
        ]
        for copy in copies:
            copy.start()
        for copy in copies:
            copy.wait()

    if kept:
        scratch = [pltpu.VMEM(shape, F32) for shape in outs[near:]] + list(scratch)
        scratch.append(pltpu.SemaphoreType.DMA((kept,)))
    return pl.pallas_call(
        with_copies if kept else kernel,
        out_shape=[jax.ShapeDtypeStruct(shape, F32) for shape in outs[:near]]
        + [pltpu.HBM(shape, F32) for shape in outs[near:]],
        in_specs=[
            pl.BlockSpec(memory_space=pltpu.SMEM) if i in smem else vmem for i in range(len(args))
        ],
        out_specs=[vmem] * near + [hbm] * away,
        scratch_shapes=scratch,
        compiler_params=pltpu.CompilerParams(vmem_limit_bytes=28 * 2**20),
        cost_estimate=pl.CostEstimate(
            flops=int(us * 10**9), bytes_accessed=int(us * 10**6), transcendentals=0
        ),
    )(*args)


def shards(source, inv_diag, upstream, downstream, cross_lower, cross_upper):
    positions, columns, planes, unknowns, vectors = source.shape
    squeeze = lambda a: a.reshape(positions, columns, *a.shape[3:])
    source_in = source
    source, inverse, before = squeeze(source), squeeze(inv_diag), squeeze(upstream)
    after, lower, upper = squeeze(downstream), squeeze(cross_lower), squeeze(cross_upper)
    full = -(-unknowns // 8) * 8
    room = full + 8
    fold = (full // 8 + 1) // 2 * 8
    peers = ROW // columns
    count = lax.axis_size("sweep")
    rows = count // ROW
    inside = [[r * ROW + i for i in range(ROW)] for r in range(rows)]
    across = [[r * ROW + i for r in range(rows)] for i in range(ROW)]
    row = (lax.axis_index("sweep") // ROW).astype(jnp.int32).reshape(1)
    ends = lax.axis_size("cross") - 1
    block = (positions, columns, full, vectors)
    others = (positions - 1, columns, full, vectors)
    side = (positions, 2, full, vectors)

    def exchange(x, groups):
        return lax.all_to_all(x, "sweep", 0, 0, axis_index_groups=groups)

    def from_below(x):
        return lax.ppermute(x, "cross", [(i, i + 1) for i in range(ends)])

    def from_above(x):
        return lax.ppermute(x, "cross", [(i + 1, i) for i in range(ends)])

    def settle(backward, joined, states):
        (sent,) = call(
            functools.partial(enter, full, backward),
            [(ROW, fold, LANES)],
            row,
            joined,
            states,
            us=1,
            smem=(0,),
        )
        return exchange(sent, inside)

    (sent,) = call(
        start,
        [(ROW, 2 * room + fold, LANES)],
        inverse,
        before,
        after,
        source,
        us=4,
        scratch=[pltpu.VMEM(shape, F32) for shape in (side, side, block, block)],
    )
    received = exchange(sent, inside)
    *raw, sent = lax.optimization_barrier((inv_diag, upstream, downstream, source_in, sent))
    inverse, before, after, source = map(squeeze, raw)
    ends_sent = (positions, room + 2 * full, LANES)
    first, second, head, tail = call(
        prepare, [ends_sent, ends_sent, side, side], inverse, before, source, us=3, kept=4
    )
    back_maps, back_steps = call(
        compose_back, [block, block], inverse, after, us=2, kept=2
    )
    below, above = from_below(second), from_above(first)
    plan, more = call(
        couple,
        [(columns, 4, full, vectors), (positions - 1, columns, 4, full, vectors)],
        inverse,
        lower,
        upper,
        head,
        tail,
        below,
        above,
        back_steps,
        us=6,
        kept=2,
    )
    received, plan, more = lax.optimization_barrier((received, plan, more))
    (sent,) = call(
        functools.partial(fore_run, full), [(rows, room + fold, LANES)], received, us=1.5
    )
    joined = exchange(sent, across)
    states, later = call(
        functools.partial(fore_prefixes, full),
        [(ROW - 1, full, 2 * LANES), (ROW, room, LANES)],
        received,
        us=2.5,
        direct=1,
        scratch=[pltpu.SemaphoreType.DMA],
    )
    entering = settle(False, joined, states)
    below, above = from_below(entering[peers:]), from_above(entering[:peers])
    (part,) = call(near_part, [(columns, full, vectors)], entering, plan, us=0.6)
    sent, first = call(
        far_part,
        [(ROW, fold, LANES), (columns, full, vectors)],
        below,
        above,
        plan,
        part,
        us=0.6,
    )
    received = exchange(sent, inside)
    (values,) = call(levels, [others], entering, below, above, more, us=3, kept=1)
    received, values = lax.optimization_barrier((received, values))
    order = range(ROW - 1, -1, -1)
    (sent,) = call(
        functools.partial(whole_run, full, order),
        [(rows, room + fold, LANES)],
        later,
        received,
        us=1.5,
    )
    joined = exchange(sent, across)
    (states,) = call(
        functools.partial(prefixes, full, order),
        [(ROW - 1, full, 2 * LANES)],
        later,
        received,
        us=2.5,
    )
    entering = settle(True, joined, states)
    lines = positions * columns * unknowns * 2
    (update,) = call(
        finish,
        [(lines, LANES)],
        entering,
        back_maps,
        first,
        values,
        us=2,
        direct=1,
        scratch=[pltpu.VMEM((lines, LANES), F32), pltpu.SemaphoreType.DMA((2,))],
    )
    return update.reshape(positions, columns, planes, unknowns, vectors)


def solution(mesh):
    placed = P("sweep", "cross", None, None, None)
    return jax.shard_map(
        shards,
        mesh=mesh,
        in_specs=(placed,) * 6,
        out_specs=placed,
        check_vma=False,
    )
```

time: 153 us -> 140 us (0.915)
  the two profiles are of different devices: /device:TPU:256 before, /device:TPU:1 now
where the time goes in v2:
time: 140 us; the launch traced here: 137 us
  waiting for transfers between devices  37.5 us (27%)
  starting transfers between devices  34.3 us (24%)
  Pallas kernels  31.8 us (23%)
  blocking collectives  27.6 us (20%)
  local copies, waits for them, and re-layouts  5.13 us (4%)
    pallas_call x14, Pallas kernels, call(): pl.pallas_call(with_copies if kept else kernel, out_shape=[jax.ShapeDtype...  31.8 us
    all_to_all x2, blocking collectives, exchange(): return lax.all_to_all(x, 'sweep', 0, 0, axis_index_groups=groups)  27.6 us
    all_to_all x4, waiting for transfers between devices, exchange(): return lax.all_to_all(x, 'sweep', 0, 0, axis_index_groups=groups)  24.1 us
    all_to_all x4, starting transfers between devices, exchange(): return lax.all_to_all(x, 'sweep', 0, 0, axis_index_groups=groups)  18 us
    ppermute x2, starting transfers between devices, from_below(): return lax.ppermute(x, 'cross', [(i, i + 1) for i in range(ends)])  12.3 us
    ppermute x2, waiting for transfers between devices, from_above(): return lax.ppermute(x, 'cross', [(i + 1, i) for i in range(ends)])  8.34 us
    ppermute x2, waiting for transfers between devices, from_below(): return lax.ppermute(x, 'cross', [(i, i + 1) for i in range(ends)])  5.1 us
    unnamed x30, local copies, waits for them, and re-layouts  4.47 us
  transfers between devices with their start and end apart: 8, of which 7 were waited for; matrix products, arithmetic and copies ran while one was open for 0% of the time, Pallas kernels for 14%

profile of v2, /device:TPU:1, one launch (start us, length us, event | category | flops | bytes accessed | tf_op | source)
XLA Modules:
  0.0 136.9 jit_solution(14049889837433908178)
XLA Ops:
  0.0 1.3 copy.43
  1.3 0.1 copy.44
  1.4 0.0 copy-done.10
  1.4 0.2 copy-done.11
  1.6 0.2 copy_bitcast_fusion.7
  1.7 4.0 %shard_map.64 = f32[8,360,128]{2,1,0:T(8,128)} custom-call(bf16[4,2,135,135]{3,2,1,0:T(8,128)(2,1)S(1)} %bitcast.32, bf16[4,2,135,135]{3,2,1,0:T(8,128)(2,1)S(1)} %get-tuple-element.50.before, bf16[4,2,135,135]{3,2,1,0:T(8,128)(2,1)S(1)} %get-tuple-element.49.after, bf16[4,2,135,256]{3,2,1,0:T(8,128)(2,1)S(1)} %bitcast.31), custom_call_target="tpu_custom_call" | custom-call | flops 4000000000 | bytes 4000000 | tf_op jit(solution)/shard_map/pallas_call | solution.py:369
  5.8 7.6 %all-to-all-start = ((f32[8,360,128]{2,1,0:T(8,128)}), f32[8,360,128]{2,1,0:T(8,128)S(1)}, u32[]{:S(2)}, u32[]{:S(2)}) async-start(f32[8,360,128]{2,1,0:T(8,128)} %shard_map.64), calls=%async_computation | async-start | bytes 2949120 | tf_op jit(solution)/shard_map/all_to_all | solution.py:406
  13.4 0.1 copy.42
  13.5 1.0 copy-done.9
  14.5 0.1 copy.40
  14.6 0.1 copy.41
  14.6 3.7 %shard_map.65 = (f32[4,416,128]{2,1,0:T(8,128)}, f32[4,416,128]{2,1,0:T(8,128)}, f32[4,2,136,256]{3,2,1,0:T(8,128)}, f32[4,2,136,256]{3,2,1,0:T(8,128)}) custom-call(bf16[4,2,135,135]{3,2,1,0:T(8,128)(2,1)S(1)} %bitcast.28, bf16[4,2,135,135]{3,2,1,0:T(8,128)(2,1)S(1)} %bitcast.34, bf16[4,2,135,256]{3,2,1,0:T(8,128)(2,1)S(1)} %bitcast.33), custom_call_target="tpu_custom_call" | custom-call | flops 3000000000 | bytes 3000000 | tf_op jit(solution)/shard_map/pallas_call | solution.py:369
  18.4 4.8 %collective-permute-start = (f32[4,416,128]{2,1,0:T(8,128)}, f32[4,416,128]{2,1,0:T(8,128)S(1)}, u32[]{:S(2)}, u32[]{:S(2)}) collective-permute-start(f32[4,416,128]{2,1,0:T(8,128)} %get-tuple-element.31), channel_id=1, source_target_pairs={{0,1},{1,2},{2,3},{3,4},{4,5},{5,6},{6,7},{7,8},{8,9},{9,10},{10,1... | collective-permute-start | bytes 2555912 | tf_op jit(solution)/shard_map/ppermute | solution.py:409
  23.2 1.9 %collective-permute-start.1 = (f32[4,416,128]{2,1,0:T(8,128)}, f32[4,416,128]{2,1,0:T(8,128)S(1)}, u32[]{:S(2)}, u32[]{:S(2)}) collective-permute-start(f32[4,416,128]{2,1,0:T(8,128)} %get-tuple-element.32), channel_id=1, source_target_pairs={{1,0},{2,1},{3,2},{4,3},{5,4},{6,5},{7,6},{8,7},{9,8},{10,9},{11,1... | collective-permute-start | bytes 2555912 | tf_op jit(solution)/shard_map/ppermute | solution.py:412
  25.2 0.1 copy.39
  25.2 0.0 copy-start.12
  25.3 0.0 copy-start.13
  25.3 2.6 %shard_map.66 = (f32[4,2,136,256]{3,2,1,0:T(8,128)}, f32[4,2,136,256]{3,2,1,0:T(8,128)}) custom-call(bf16[4,2,135,135]{3,2,1,0:T(8,128)(2,1)S(1)} %bitcast.29, bf16[4,2,135,135]{3,2,1,0:T(8,128)(2,1)S(1)} %bitcast.35), custom_call_target="tpu_custom_call" | custom-call | flops 2000000000 | bytes 2000000 | tf_op jit(solution)/shard_map/pallas_call | solution.py:369
  27.9 0.2 copy_bitcast_fusion.3
  28.1 5.1 %collective-permute-done.refs_5_ = f32[4,416,128]{2,1,0:T(8,128)S(1)} collective-permute-done((f32[4,416,128]{2,1,0:T(8,128)}, f32[4,416,128]{2,1,0:T(8,128)S(1)}, u32[]{:S(2)}, u32[]{:S(2)}) %collective-permute-start) | collective-permute-done | bytes 852000 | tf_op jit(solution)/shard_map/ppermute | solution.py:409
  33.2 4.6 %collective-permute-done.1.refs_6_ = f32[4,416,128]{2,1,0:T(8,128)S(1)} collective-permute-done((f32[4,416,128]{2,1,0:T(8,128)}, f32[4,416,128]{2,1,0:T(8,128)S(1)}, u32[]{:S(2)}, u32[]{:S(2)}) %collective-permute-start.1) | collective-permute-done | bytes 852000 | tf_op jit(solution)/shard_map/ppermute | solution.py:412
  37.7 0.0 copy-done.7
  37.8 6.6 %shard_map.67 = (f32[2,4,136,256]{3,2,1,0:T(8,128)}, f32[3,2,4,136,256]{4,3,2,1,0:T(8,128)}) custom-call(bf16[4,2,135,135]{3,2,1,0:T(8,128)(2,1)S(1)} %bitcast.30, bf16[4,2,135,135]{3,2,1,0:T(8,128)(2,1)S(1)} %get-tuple-element.52.refs_1_, bf16[4,2,135,135]{3,2,1,0:T(8,128)(2,1)S(1)} %get-tuple-element.51.refs_2_, f32[4,2,136,256]{3,2,1,0:T(8,128)S(1)} %copy-done.6, ...), custom_call_target="tpu_custom_call" | custom-call | flops 6000000000 | bytes 6000000 | tf_op jit(solution)/shard_map/pallas_call | solution.py:369
  44.4 7.4 %all-to-all-done.received = f32[8,360,128]{2,1,0:T(8,128)S(1)} async-done(((f32[8,360,128]{2,1,0:T(8,128)}), f32[8,360,128]{2,1,0:T(8,128)S(1)}, u32[]{:S(2)}, u32[]{:S(2)}) %all-to-all-start) | async-done | bytes 1474592 | tf_op jit(solution)/shard_map/all_to_all | solution.py:406
  51.7 1.8 %shard_map.69 = f32[4,216,128]{2,1,0:T(8,128)} custom-call(f32[8,360,128]{2,1,0:T(8,128)S(1)} %all-to-all-done.received), custom_call_target="tpu_custom_call" | custom-call | flops 1500000000 | bytes 1500000 | tf_op jit(solution)/shard_map/pallas_call | solution.py:369
  53.5 3.5 %all-to-all-start.1 = ((f32[4,216,128]{2,1,0:T(8,128)}), f32[4,216,128]{2,1,0:T(8,128)S(1)}, u32[]{:S(2)}, u32[]{:S(2)}) async-start(f32[4,216,128]{2,1,0:T(8,128)} %shard_map.69), calls=%async_computation.1 | async-start | bytes 884736 | tf_op jit(solution)/shard_map/all_to_all | solution.py:406
  57.0 1.9 %shard_map.68 = (f32[7,136,256]{2,1,0:T(8,128)S(1)}, f32[8,144,128]{2,1,0:T(8,128)}) custom-call(f32[8,360,128]{2,1,0:T(8,128)S(1)} %all-to-all-done.received), custom_call_target="tpu_custom_call" | custom-call | flops 2500000000 | bytes 2500000 | tf_op jit(solution)/shard_map/pallas_call | solution.py:369
  58.9 5.0 %all-to-all-done.1.received = f32[4,216,128]{2,1,0:T(8,128)S(1)} async-done(((f32[4,216,128]{2,1,0:T(8,128)}), f32[4,216,128]{2,1,0:T(8,128)S(1)}, u32[]{:S(2)}, u32[]{:S(2)}) %all-to-all-start.1) | async-done | bytes 442400 | tf_op jit(solution)/shard_map/all_to_all | solution.py:406
  63.9 1.1 shard_map.70
  65.0 12.2 %all_to_all.30.received.refs_0_ = f32[8,72,128]{2,1,0:T(8,128)S(1)} all-to-all(f32[8,72,128]{2,1,0:T(8,128)S(1)} %shard_map.70), channel_id=1, replica_groups={{0,16,32,48,64,80,96,112},{128,144,160,176,192,208,224,240},{256,272,28..., dimensions={0} | all-to-all | bytes 589824 | tf_op jit(solution)/shard_map/all_to_all | solution.py:406
  77.3 7.5 %collective-permute-start.2 = (f32[4,72,128]{2,1,0:T(8,128)S(1)}, f32[4,72,128]{2,1,0:T(8,128)S(1)}, u32[]{:S(2)}, u32[]{:S(2)}) collective-permute-start(f32[4,72,128]{2,1,0:T(8,128)S(1)} %get-tuple-element.48), channel_id=1, source_target_pairs={{0,1},{1,2},{2,3},{3,4},{4,5},{5,6},{6,7},{7,8},{8,9},{9,10},{10,1... | collective-permute-start | bytes 442376 | tf_op jit(solution)/shard_map/ppermute | solution.py:409
  84.8 2.1 %collective-permute-start.3 = (f32[4,72,128]{2,1,0:T(8,128)S(1)}, f32[4,72,128]{2,1,0:T(8,128)S(1)}, u32[]{:S(2)}, u32[]{:S(2)}) collective-permute-start(f32[4,72,128]{2,1,0:T(8,128)S(1)} %get-tuple-element.47), channel_id=1, source_target_pairs={{1,0},{2,1},{3,2},{4,3},{5,4},{6,5},{7,6},{8,7},{9,8},{10,9},{11,1... | collective-permute-start | bytes 442376 | tf_op jit(solution)/shard_map/ppermute | solution.py:412
  86.9 0.6 shard_map.71.part
  87.5 0.0 collective-permute-done.2.below.refs_1_
  87.5 3.8 %collective-permute-done.3.above.refs_2_ = f32[4,72,128]{2,1,0:T(8,128)S(1)} collective-permute-done((f32[4,72,128]{2,1,0:T(8,128)S(1)}, f32[4,72,128]{2,1,0:T(8,128)S(1)}, u32[]{:S(2)}, u32[]{:S(2)}) %collective-permute-start.3) | collective-permute-done | bytes 147488 | tf_op jit(solution)/shard_map/ppermute | solution.py:412
  91.2 1.3 shard_map.72
  92.5 3.4 %all-to-all-start.3 = ((f32[8,72,128]{2,1,0:T(8,128)}), f32[8,72,128]{2,1,0:T(8,128)S(1)}, u32[]{:S(2)}, u32[]{:S(2)}) async-start(f32[8,72,128]{2,1,0:T(8,128)} %get-tuple-element.41), calls=%async_computation.3 | async-start | bytes 589824 | tf_op jit(solution)/shard_map/all_to_all | solution.py:406
  95.9 0.0 copy-start.1
  96.0 1.9 %copy-done.1 = f32[3,2,4,136,256]{4,3,2,1,0:T(8,128)S(1)} copy-done((f32[3,2,4,136,256]{4,3,2,1,0:T(8,128)S(1)}, f32[3,2,4,136,256]{4,3,2,1,0:T(8,128)}, u32[]{:S(2)}) %copy-start.1) | copy-done | bytes 3342360
  97.9 2.3 %shard_map.73.rest = f32[3,2,136,256]{3,2,1,0:T(8,128)} custom-call(f32[8,72,128]{2,1,0:T(8,128)S(1)} %all_to_all.30.received.refs_0_, f32[4,72,128]{2,1,0:T(8,128)S(1)} %collective-permute-done.2.below.refs_1_, f32[4,72,128]{2,1,0:T(8,128)S(1)} %collective-permute-done.3.above.refs_2_, f32[3,2,4,136,256]{4,3,2,1,0:T(8,128)S(1)} %copy-done.1), custom_call_target="tpu_custom_call" | custom-call | flops 3000000000 | bytes 3000000 | tf_op jit(solution)/shard_map/pallas_call | solution.py:369
  100.2 5.8 %all-to-all-done.3.blocks = f32[8,72,128]{2,1,0:T(8,128)S(1)} async-done(((f32[8,72,128]{2,1,0:T(8,128)}), f32[8,72,128]{2,1,0:T(8,128)S(1)}, u32[]{:S(2)}, u32[]{:S(2)}) %all-to-all-start.3) | async-done | bytes 294944 | tf_op jit(solution)/shard_map/all_to_all | solution.py:406
  106.0 1.8 %shard_map.74 = f32[4,216,128]{2,1,0:T(8,128)} custom-call(f32[8,144,128]{2,1,0:T(8,128)S(1)} %copy-done.4, f32[8,72,128]{2,1,0:T(8,128)S(1)} %all-to-all-done.3.blocks), custom_call_target="tpu_custom_call" | custom-call | flops 1500000000 | bytes 1500000 | tf_op jit(solution)/shard_map/pallas_call | solution.py:369
  107.7 3.5 %all-to-all-start.4 = ((f32[4,216,128]{2,1,0:T(8,128)}), f32[4,216,128]{2,1,0:T(8,128)S(1)}, u32[]{:S(2)}, u32[]{:S(2)}) async-start(f32[4,216,128]{2,1,0:T(8,128)} %shard_map.74), calls=%async_computation.4 | async-start | bytes 884736 | tf_op jit(solution)/shard_map/all_to_all | solution.py:406
  111.2 1.5 %shard_map.75.states = f32[7,136,256]{2,1,0:T(8,128)S(1)} custom-call(f32[8,144,128]{2,1,0:T(8,128)S(1)} %copy-done.4, f32[8,72,128]{2,1,0:T(8,128)S(1)} %all-to-all-done.3.blocks), custom_call_target="tpu_custom_call" | custom-call | flops 2500000000 | bytes 2500000 | tf_op jit(solution)/shard_map/pallas_call | solution.py:369
  112.7 5.9 %all-to-all-done.4.received = f32[4,216,128]{2,1,0:T(8,128)S(1)} async-done(((f32[4,216,128]{2,1,0:T(8,128)}), f32[4,216,128]{2,1,0:T(8,128)S(1)}, u32[]{:S(2)}, u32[]{:S(2)}) %all-to-all-start.4) | async-done | bytes 442400 | tf_op jit(solution)/shard_map/all_to_all | solution.py:406
  118.6 1.1 shard_map.76
  119.7 15.4 %all_to_all.31.received = f32[8,72,128]{2,1,0:T(8,128)S(1)} all-to-all(f32[8,72,128]{2,1,0:T(8,128)S(1)} %shard_map.76), channel_id=1, replica_groups={{0,16,32,48,64,80,96,112},{128,144,160,176,192,208,224,240},{256,272,28..., dimensions={0} | all-to-all | bytes 589824 | tf_op jit(solution)/shard_map/all_to_all | solution.py:406
  135.1 1.6 %shard_map.77 = f32[2160,128]{1,0:T(8,128)} custom-call(f32[8,72,128]{2,1,0:T(8,128)S(1)} %all_to_all.31.received, f32[4,2,136,256]{3,2,1,0:T(8,128)S(1)} %copy-done.2, f32[2,136,256]{2,1,0:T(8,128)S(1)} %get-tuple-element.45.first, f32[3,2,136,256]{3,2,1,0:T(8,128)S(1)} %copy-done.3), custom_call_target="tpu_custom_call" | custom-call | flops 2000000000 | bytes 2000000 | tf_op jit(solution)/shard_map/pallas_call | solution.py:369
  (21 shorter events, 0.1 us)
Async XLA Ops:
  0.0 1.3 copy-start.8
  0.0 1.4 %copy-start.10 = (bf16[4,2,1,135,135]{4,1,3,2,0:T(2,128)(2,1)S(1)}, bf16[4,2,1,135,135]{4,1,3,2,0:T(2,128)(2,1)}, u32[]{:S(2)}) copy-start(bf16[4,2,1,135,135]{4,1,3,2,0:T(2,128)(2,1)} %param.8) | copy-start | bytes 874804
  0.0 1.5 %copy-start.11 = (bf16[4,2,1,135,135]{4,1,3,2,0:T(2,128)(2,1)S(1)}, bf16[4,2,1,135,135]{4,1,3,2,0:T(2,128)(2,1)}, u32[]{:S(2)}) copy-start(bf16[4,2,1,135,135]{4,1,3,2,0:T(2,128)(2,1)} %param.9) | copy-start | bytes 874804
  5.8 46.0 %all-to-all-start = ((f32[8,360,128]{2,1,0:T(8,128)}), f32[8,360,128]{2,1,0:T(8,128)S(1)}, u32[]{:S(2)}, u32[]{:S(2)}) async-start(f32[8,360,128]{2,1,0:T(8,128)} %shard_map.64), calls=%async_computation | async-start | bytes 2949120 | tf_op jit(solution)/shard_map/all_to_all | solution.py:406
  13.4 1.1 copy-start.9
  18.4 14.8 %collective-permute-start = (f32[4,416,128]{2,1,0:T(8,128)}, f32[4,416,128]{2,1,0:T(8,128)S(1)}, u32[]{:S(2)}, u32[]{:S(2)}) collective-permute-start(f32[4,416,128]{2,1,0:T(8,128)} %get-tuple-element.31), channel_id=1, source_target_pairs={{0,1},{1,2},{2,3},{3,4},{4,5},{5,6},{6,7},{7,8},{8,9},{9,10},{10,1... | collective-permute-start | bytes 2555912 | tf_op jit(solution)/shard_map/ppermute | solution.py:409
  23.2 14.5 %collective-permute-start.1 = (f32[4,416,128]{2,1,0:T(8,128)}, f32[4,416,128]{2,1,0:T(8,128)S(1)}, u32[]{:S(2)}, u32[]{:S(2)}) collective-permute-start(f32[4,416,128]{2,1,0:T(8,128)} %get-tuple-element.32), channel_id=1, source_target_pairs={{1,0},{2,1},{3,2},{4,3},{5,4},{6,5},{7,6},{8,7},{9,8},{10,9},{11,1... | collective-permute-start | bytes 2555912 | tf_op jit(solution)/shard_map/ppermute | solution.py:412
  25.2 2.6 %copy-start.12 = (bf16[4,2,1,135,135]{4,1,3,2,0:T(2,128)(2,1)S(1)}, bf16[4,2,1,135,135]{4,1,3,2,0:T(2,128)(2,1)}, u32[]{:S(2)}) copy-start(bf16[4,2,1,135,135]{4,1,3,2,0:T(2,128)(2,1)} %param.11) | copy-start | bytes 874804
  25.3 2.6 %copy-start.13 = (bf16[4,2,1,135,135]{4,1,3,2,0:T(2,128)(2,1)S(1)}, bf16[4,2,1,135,135]{4,1,3,2,0:T(2,128)(2,1)}, u32[]{:S(2)}) copy-start(bf16[4,2,1,135,135]{4,1,3,2,0:T(2,128)(2,1)} %param.10) | copy-start | bytes 874804
  25.3 12.5 %copy-start.7 = (f32[4,2,136,256]{3,2,1,0:T(8,128)S(1)}, f32[4,2,136,256]{3,2,1,0:T(8,128)}, u32[]{:S(2)}) copy-start(f32[4,2,136,256]{3,2,1,0:T(8,128)} %get-tuple-element.30.refs_4_) | copy-start | bytes 3342340
  27.9 9.9 %copy-start.5 = (f32[4,2,136,256]{3,2,1,0:T(8,128)S(1)}, f32[4,2,136,256]{3,2,1,0:T(8,128)}, u32[]{:S(2)}) copy-start(f32[4,2,136,256]{3,2,1,0:T(8,128)} %get-tuple-element.34.refs_7_) | copy-start | bytes 3342340
  27.9 9.9 %copy-start.6 = (f32[4,2,136,256]{3,2,1,0:T(8,128)S(1)}, f32[4,2,136,256]{3,2,1,0:T(8,128)}, u32[]{:S(2)}) copy-start(f32[4,2,136,256]{3,2,1,0:T(8,128)} %get-tuple-element.29.refs_3_) | copy-start | bytes 3342340
  53.5 10.4 %all-to-all-start.1 = ((f32[4,216,128]{2,1,0:T(8,128)}), f32[4,216,128]{2,1,0:T(8,128)S(1)}, u32[]{:S(2)}, u32[]{:S(2)}) async-start(f32[4,216,128]{2,1,0:T(8,128)} %shard_map.69), calls=%async_computation.1 | async-start | bytes 884736 | tf_op jit(solution)/shard_map/all_to_all | solution.py:406
  65.0 21.9 %copy-start = (f32[2,4,136,256]{3,2,1,0:T(8,128)S(1)}, f32[2,4,136,256]{3,2,1,0:T(8,128)}, u32[]{:S(2)}) copy-start(f32[2,4,136,256]{3,2,1,0:T(8,128)} %get-tuple-element.40.plan) | copy-start | bytes 3342340
  77.3 10.2 %collective-permute-start.2 = (f32[4,72,128]{2,1,0:T(8,128)S(1)}, f32[4,72,128]{2,1,0:T(8,128)S(1)}, u32[]{:S(2)}, u32[]{:S(2)}) collective-permute-start(f32[4,72,128]{2,1,0:T(8,128)S(1)} %get-tuple-element.48), channel_id=1, source_target_pairs={{0,1},{1,2},{2,3},{3,4},{4,5},{5,6},{6,7},{7,8},{8,9},{9,10},{10,1... | collective-permute-start | bytes 442376 | tf_op jit(solution)/shard_map/ppermute | solution.py:409
  84.8 6.5 %collective-permute-start.3 = (f32[4,72,128]{2,1,0:T(8,128)S(1)}, f32[4,72,128]{2,1,0:T(8,128)S(1)}, u32[]{:S(2)}, u32[]{:S(2)}) collective-permute-start(f32[4,72,128]{2,1,0:T(8,128)S(1)} %get-tuple-element.47), channel_id=1, source_target_pairs={{1,0},{2,1},{3,2},{4,3},{5,4},{6,5},{7,6},{8,7},{9,8},{10,9},{11,1... | collective-permute-start | bytes 442376 | tf_op jit(solution)/shard_map/ppermute | solution.py:412
  92.5 13.4 %all-to-all-start.3 = ((f32[8,72,128]{2,1,0:T(8,128)}), f32[8,72,128]{2,1,0:T(8,128)S(1)}, u32[]{:S(2)}, u32[]{:S(2)}) async-start(f32[8,72,128]{2,1,0:T(8,128)} %get-tuple-element.41), calls=%async_computation.3 | async-start | bytes 589824 | tf_op jit(solution)/shard_map/all_to_all | solution.py:406
  95.9 1.9 %copy-start.1 = (f32[3,2,4,136,256]{4,3,2,1,0:T(8,128)S(1)}, f32[3,2,4,136,256]{4,3,2,1,0:T(8,128)}, u32[]{:S(2)}) copy-start(f32[3,2,4,136,256]{4,3,2,1,0:T(8,128)} %get-tuple-element.42.refs_3_) | copy-start | bytes 10027012
  97.9 8.1 %copy-start.4 = (f32[8,144,128]{2,1,0:T(8,128)S(1)}, f32[8,144,128]{2,1,0:T(8,128)}, u32[]{:S(2)}) copy-start(f32[8,144,128]{2,1,0:T(8,128)} %get-tuple-element.38.matrices) | copy-start | bytes 1769476
  107.7 10.9 %all-to-all-start.4 = ((f32[4,216,128]{2,1,0:T(8,128)}), f32[4,216,128]{2,1,0:T(8,128)S(1)}, u32[]{:S(2)}, u32[]{:S(2)}) async-start(f32[4,216,128]{2,1,0:T(8,128)} %shard_map.74), calls=%async_computation.4 | async-start | bytes 884736 | tf_op jit(solution)/shard_map/all_to_all | solution.py:406
  112.7 22.4 %copy-start.2 = (f32[4,2,136,256]{3,2,1,0:T(8,128)S(1)}, f32[4,2,136,256]{3,2,1,0:T(8,128)}, u32[]{:S(2)}) copy-start(f32[4,2,136,256]{3,2,1,0:T(8,128)} %get-tuple-element.44.maps) | copy-start | bytes 3342340
  118.6 16.5 %copy-start.3 = (f32[3,2,136,256]{3,2,1,0:T(8,128)S(1)}, f32[3,2,136,256]{3,2,1,0:T(8,128)}, u32[]{:S(2)}) copy-start(f32[3,2,136,256]{3,2,1,0:T(8,128)} %shard_map.73.rest) | copy-start | bytes 2506756

commit v3 on v2

--- a/solution.py
+++ b/solution.py
@@ -122,23 +122,49 @@
             maps[s, c] = float_by_float(steps[s, c, :, :full], maps[s + 1, c])
 
 
-def start(inverse, before, after, source, sent, head, tail, maps, steps):
-    positions, columns = source.shape[:2]
-    full = head.shape[-2]
-    last = positions - 1
-    fore = Pair((head, tail))
-    compose(inverse, before, source, fore)
-    compose_back(inverse, after, maps, steps)
+def start(inverse, before, after, source, sent, maps, values, sems):
+    positions, columns, unknowns, vectors = source.shape
+    full = values.shape[-2]
+    room = full + 8
     peers = ROW // columns
-    room = full + 8
-    for c in range(columns):
-        forth, back = pack_map(fore[c][last, 0]), pack_map(maps[0, c])
+    copies = []
+
+    def send(ref, at, low):
+        there = sent.at[at, pl.ds(low, ref.shape[0])]
+        copies.append(pltpu.make_async_copy(ref, there, sems.at[len(copies)]))
+        copies[-1].start()
+
+    def padded(value):
+        rows, lanes = full - value.shape[0], 2 * LANES - value.shape[1]
+        return jnp.pad(value, ((0, rows), (0, lanes)))
+
+    for c in range(columns):
+        steps = [-mul(inverse[s, c], after[s, c]) for s in range(positions)]
+        while len(steps) > 1:
+            steps = [float_by_float(*steps[k : k + 2]) for k in range(0, len(steps), 2)]
+        maps[c, 1] = pack_map(padded(steps[0]))
         for q in range(peers):
-            at = c * peers + q
-            sent[at, 0:room] = forth
-            sent[at, room : 2 * room] = back
-            pair = fore[c][last, 1, :, q // 2 * LANES : (q // 2 + 1) * LANES]
-            sent[at, 2 * room :] = pack_slice(pair, q % 2)
+            send(maps.at[c, 1], c * peers + q, room)
+    for c in range(columns):
+        steps = [
+            (-mul(inverse[s, c], before[s, c]), mul(inverse[s, c], source[s, c]))
+            for s in range(positions)
+        ]
+        while len(steps) > 1:
+            steps = [
+                (float_by_float(later[0], earlier[0]), later[1] + float_by_float(later[0], earlier[1]))
+                for earlier, later in zip(steps[::2], steps[1::2])
+            ]
+        maps[c, 0] = pack_map(padded(steps[0][0]))
+        value = padded(steps[0][1])
+        for q in range(peers):
+            send(maps.at[c, 0], c * peers + q, 0)
+            pair = value[:, q // 2 * LANES : (q // 2 + 1) * LANES]
+            fold = (full // 8 + 1) // 2 * 8
+            values[c, q, 0:fold] = pack_slice(pair, q % 2)
+            send(values.at[c, q, pl.ds(0, fold)], c * peers + q, 2 * room)
+    for copy in copies:
+        copy.wait()
 
 
 def prepare(inverse, before, source, first, second, head, tail):
@@ -321,7 +347,7 @@
 def finish(received, maps, first, rest, result, out, sems):
     positions, columns, full, vectors = maps.shape
     peers = ROW // columns
-    total = out.shape[0]
+    total = result.shape[0]
     unknowns = total // (2 * positions * columns)
     entering = [unpack_columns(full, received, c * peers, peers) for c in range(columns)]
     copies = []
@@ -431,7 +457,12 @@
         after,
         source,
         us=4,
-        scratch=[pltpu.VMEM(shape, F32) for shape in (side, side, block, block)],
+        direct=1,
+        scratch=[
+            pltpu.VMEM((columns, 2, room, LANES), F32),
+            pltpu.VMEM((columns, peers, full, LANES), F32),
+            pltpu.SemaphoreType.DMA((3 * ROW,)),
+        ],
     )
     received = exchange(sent, inside)
     *raw, sent = lax.optimization_barrier((inv_diag, upstream, downstream, source_in, sent))
@@ -513,7 +544,7 @@
         values,
         us=2,
         direct=1,
-        scratch=[pltpu.VMEM((lines, LANES), F32), pltpu.SemaphoreType.DMA((2,))],
+        scratch=[pltpu.VMEM((lines + 16, LANES), F32), pltpu.SemaphoreType.DMA((2,))],
     )
     return update.reshape(positions, columns, planes, unknowns, vectors)
 

time: 140 us -> 139 us (level)
  no operation moved by 1% of the time
where the time goes in v3:
time: 139 us; the launch traced here: 136 us
  waiting for transfers between devices  37.6 us (27%)
  starting transfers between devices  34.3 us (25%)
  Pallas kernels  31.2 us (22%)
  blocking collectives  27.6 us (20%)
  local copies, waits for them, and re-layouts  5.12 us (4%)
    pallas_call x14, Pallas kernels, call(): pl.pallas_call(with_copies if kept else kernel, out_shape=[jax.ShapeDtype...  31.2 us
    all_to_all x2, blocking collectives, exchange(): return lax.all_to_all(x, 'sweep', 0, 0, axis_index_groups=groups)  27.6 us
    all_to_all x4, waiting for transfers between devices, exchange(): return lax.all_to_all(x, 'sweep', 0, 0, axis_index_groups=groups)  24.1 us
    all_to_all x4, starting transfers between devices, exchange(): return lax.all_to_all(x, 'sweep', 0, 0, axis_index_groups=groups)  18 us
    ppermute x2, starting transfers between devices, from_below(): return lax.ppermute(x, 'cross', [(i, i + 1) for i in range(ends)])  12.3 us
    ppermute x2, waiting for transfers between devices, from_above(): return lax.ppermute(x, 'cross', [(i + 1, i) for i in range(ends)])  8.34 us
    ppermute x2, waiting for transfers between devices, from_below(): return lax.ppermute(x, 'cross', [(i, i + 1) for i in range(ends)])  5.09 us
    unnamed x30, local copies, waits for them, and re-layouts  4.47 us
  transfers between devices with their start and end apart: 8, of which 7 were waited for; matrix products, arithmetic and copies ran while one was open for 0% of the time, Pallas kernels for 14%

profile of v3, /device:TPU:1, one launch (start us, length us, event | category | flops | bytes accessed | tf_op | source)
XLA Modules:
  0.0 136.3 jit_solution(18218858750392768134)
XLA Ops:
  0.0 1.3 copy.43
  1.3 0.1 copy.44
  1.4 0.0 copy-done.10
  1.4 0.2 copy-done.11
  1.6 0.2 copy_bitcast_fusion.7
  1.7 3.5 %shard_map.64 = f32[8,360,128]{2,1,0:T(8,128)} custom-call(bf16[4,2,135,135]{3,2,1,0:T(8,128)(2,1)S(1)} %bitcast.32, bf16[4,2,135,135]{3,2,1,0:T(8,128)(2,1)S(1)} %get-tuple-element.50.before, bf16[4,2,135,135]{3,2,1,0:T(8,128)(2,1)S(1)} %get-tuple-element.49.after, bf16[4,2,135,256]{3,2,1,0:T(8,128)(2,1)S(1)} %bitcast.31), custom_call_target="tpu_custom_call" | custom-call | flops 4000000000 | bytes 4000000 | tf_op jit(solution)/shard_map/pallas_call | solution.py:395
  5.2 7.7 %all-to-all-start = ((f32[8,360,128]{2,1,0:T(8,128)}), f32[8,360,128]{2,1,0:T(8,128)S(1)}, u32[]{:S(2)}, u32[]{:S(2)}) async-start(f32[8,360,128]{2,1,0:T(8,128)} %shard_map.64), calls=%async_computation | async-start | bytes 2949120 | tf_op jit(solution)/shard_map/all_to_all | solution.py:432
  12.9 0.1 copy.42
  12.9 1.0 copy-done.9
  13.9 0.1 copy.40
  14.0 0.1 copy.41
  14.1 3.7 %shard_map.65 = (f32[4,416,128]{2,1,0:T(8,128)}, f32[4,416,128]{2,1,0:T(8,128)}, f32[4,2,136,256]{3,2,1,0:T(8,128)}, f32[4,2,136,256]{3,2,1,0:T(8,128)}) custom-call(bf16[4,2,135,135]{3,2,1,0:T(8,128)(2,1)S(1)} %bitcast.28, bf16[4,2,135,135]{3,2,1,0:T(8,128)(2,1)S(1)} %bitcast.34, bf16[4,2,135,256]{3,2,1,0:T(8,128)(2,1)S(1)} %bitcast.33), custom_call_target="tpu_custom_call" | custom-call | flops 3000000000 | bytes 3000000 | tf_op jit(solution)/shard_map/pallas_call | solution.py:395
  17.8 4.8 %collective-permute-start = (f32[4,416,128]{2,1,0:T(8,128)}, f32[4,416,128]{2,1,0:T(8,128)S(1)}, u32[]{:S(2)}, u32[]{:S(2)}) collective-permute-start(f32[4,416,128]{2,1,0:T(8,128)} %get-tuple-element.31), channel_id=1, source_target_pairs={{0,1},{1,2},{2,3},{3,4},{4,5},{5,6},{6,7},{7,8},{8,9},{9,10},{10,1... | collective-permute-start | bytes 2555912 | tf_op jit(solution)/shard_map/ppermute | solution.py:435
  22.7 1.9 %collective-permute-start.1 = (f32[4,416,128]{2,1,0:T(8,128)}, f32[4,416,128]{2,1,0:T(8,128)S(1)}, u32[]{:S(2)}, u32[]{:S(2)}) collective-permute-start(f32[4,416,128]{2,1,0:T(8,128)} %get-tuple-element.32), channel_id=1, source_target_pairs={{1,0},{2,1},{3,2},{4,3},{5,4},{6,5},{7,6},{8,7},{9,8},{10,9},{11,1... | collective-permute-start | bytes 2555912 | tf_op jit(solution)/shard_map/ppermute | solution.py:438
  24.6 0.1 copy.39
  24.7 0.0 copy-start.12
  24.7 0.0 copy-start.13
  24.7 0.0 copy-start.7
  24.7 2.6 %shard_map.66 = (f32[4,2,136,256]{3,2,1,0:T(8,128)}, f32[4,2,136,256]{3,2,1,0:T(8,128)}) custom-call(bf16[4,2,135,135]{3,2,1,0:T(8,128)(2,1)S(1)} %bitcast.29, bf16[4,2,135,135]{3,2,1,0:T(8,128)(2,1)S(1)} %bitcast.35), custom_call_target="tpu_custom_call" | custom-call | flops 2000000000 | bytes 2000000 | tf_op jit(solution)/shard_map/pallas_call | solution.py:395
  27.3 0.2 copy_bitcast_fusion.3
  27.5 5.1 %collective-permute-done.refs_5_ = f32[4,416,128]{2,1,0:T(8,128)S(1)} collective-permute-done((f32[4,416,128]{2,1,0:T(8,128)}, f32[4,416,128]{2,1,0:T(8,128)S(1)}, u32[]{:S(2)}, u32[]{:S(2)}) %collective-permute-start) | collective-permute-done | bytes 852000 | tf_op jit(solution)/shard_map/ppermute | solution.py:435
  32.6 4.6 %collective-permute-done.1.refs_6_ = f32[4,416,128]{2,1,0:T(8,128)S(1)} collective-permute-done((f32[4,416,128]{2,1,0:T(8,128)}, f32[4,416,128]{2,1,0:T(8,128)S(1)}, u32[]{:S(2)}, u32[]{:S(2)}) %collective-permute-start.1) | collective-permute-done | bytes 852000 | tf_op jit(solution)/shard_map/ppermute | solution.py:438
  37.2 6.6 %shard_map.67 = (f32[2,4,136,256]{3,2,1,0:T(8,128)}, f32[3,2,4,136,256]{4,3,2,1,0:T(8,128)}) custom-call(bf16[4,2,135,135]{3,2,1,0:T(8,128)(2,1)S(1)} %bitcast.30, bf16[4,2,135,135]{3,2,1,0:T(8,128)(2,1)S(1)} %get-tuple-element.52.refs_1_, bf16[4,2,135,135]{3,2,1,0:T(8,128)(2,1)S(1)} %get-tuple-element.51.refs_2_, f32[4,2,136,256]{3,2,1,0:T(8,128)S(1)} %copy-done.6, ...), custom_call_target="tpu_custom_call" | custom-call | flops 6000000000 | bytes 6000000 | tf_op jit(solution)/shard_map/pallas_call | solution.py:395
  43.8 7.4 %all-to-all-done.received = f32[8,360,128]{2,1,0:T(8,128)S(1)} async-done(((f32[8,360,128]{2,1,0:T(8,128)}), f32[8,360,128]{2,1,0:T(8,128)S(1)}, u32[]{:S(2)}, u32[]{:S(2)}) %all-to-all-start) | async-done | bytes 1474592 | tf_op jit(solution)/shard_map/all_to_all | solution.py:432
  51.2 1.8 %shard_map.69 = f32[4,216,128]{2,1,0:T(8,128)} custom-call(f32[8,360,128]{2,1,0:T(8,128)S(1)} %all-to-all-done.received), custom_call_target="tpu_custom_call" | custom-call | flops 1500000000 | bytes 1500000 | tf_op jit(solution)/shard_map/pallas_call | solution.py:395
  52.9 3.5 %all-to-all-start.1 = ((f32[4,216,128]{2,1,0:T(8,128)}), f32[4,216,128]{2,1,0:T(8,128)S(1)}, u32[]{:S(2)}, u32[]{:S(2)}) async-start(f32[4,216,128]{2,1,0:T(8,128)} %shard_map.69), calls=%async_computation.1 | async-start | bytes 884736 | tf_op jit(solution)/shard_map/all_to_all | solution.py:432
  56.4 1.9 %shard_map.68 = (f32[7,136,256]{2,1,0:T(8,128)S(1)}, f32[8,144,128]{2,1,0:T(8,128)}) custom-call(f32[8,360,128]{2,1,0:T(8,128)S(1)} %all-to-all-done.received), custom_call_target="tpu_custom_call" | custom-call | flops 2500000000 | bytes 2500000 | tf_op jit(solution)/shard_map/pallas_call | solution.py:395
  58.4 5.0 %all-to-all-done.1.received = f32[4,216,128]{2,1,0:T(8,128)S(1)} async-done(((f32[4,216,128]{2,1,0:T(8,128)}), f32[4,216,128]{2,1,0:T(8,128)S(1)}, u32[]{:S(2)}, u32[]{:S(2)}) %all-to-all-start.1) | async-done | bytes 442400 | tf_op jit(solution)/shard_map/all_to_all | solution.py:432
  63.4 1.1 shard_map.70
  64.5 12.2 %all_to_all.30.received.refs_0_ = f32[8,72,128]{2,1,0:T(8,128)S(1)} all-to-all(f32[8,72,128]{2,1,0:T(8,128)S(1)} %shard_map.70), channel_id=1, replica_groups={{0,16,32,48,64,80,96,112},{128,144,160,176,192,208,224,240},{256,272,28..., dimensions={0} | all-to-all | bytes 589824 | tf_op jit(solution)/shard_map/all_to_all | solution.py:432
  76.8 7.4 %collective-permute-start.2 = (f32[4,72,128]{2,1,0:T(8,128)S(1)}, f32[4,72,128]{2,1,0:T(8,128)S(1)}, u32[]{:S(2)}, u32[]{:S(2)}) collective-permute-start(f32[4,72,128]{2,1,0:T(8,128)S(1)} %get-tuple-element.48), channel_id=1, source_target_pairs={{0,1},{1,2},{2,3},{3,4},{4,5},{5,6},{6,7},{7,8},{8,9},{9,10},{10,1... | collective-permute-start | bytes 442376 | tf_op jit(solution)/shard_map/ppermute | solution.py:435
  84.2 2.1 %collective-permute-start.3 = (f32[4,72,128]{2,1,0:T(8,128)S(1)}, f32[4,72,128]{2,1,0:T(8,128)S(1)}, u32[]{:S(2)}, u32[]{:S(2)}) collective-permute-start(f32[4,72,128]{2,1,0:T(8,128)S(1)} %get-tuple-element.47), channel_id=1, source_target_pairs={{1,0},{2,1},{3,2},{4,3},{5,4},{6,5},{7,6},{8,7},{9,8},{10,9},{11,1... | collective-permute-start | bytes 442376 | tf_op jit(solution)/shard_map/ppermute | solution.py:438
  86.3 0.6 shard_map.71.part
  86.9 0.0 collective-permute-done.2.below.refs_1_
  86.9 3.8 %collective-permute-done.3.above.refs_2_ = f32[4,72,128]{2,1,0:T(8,128)S(1)} collective-permute-done((f32[4,72,128]{2,1,0:T(8,128)S(1)}, f32[4,72,128]{2,1,0:T(8,128)S(1)}, u32[]{:S(2)}, u32[]{:S(2)}) %collective-permute-start.3) | collective-permute-done | bytes 147488 | tf_op jit(solution)/shard_map/ppermute | solution.py:438
  90.7 1.3 shard_map.72
  92.0 3.4 %all-to-all-start.3 = ((f32[8,72,128]{2,1,0:T(8,128)}), f32[8,72,128]{2,1,0:T(8,128)S(1)}, u32[]{:S(2)}, u32[]{:S(2)}) async-start(f32[8,72,128]{2,1,0:T(8,128)} %get-tuple-element.41), calls=%async_computation.3 | async-start | bytes 589824 | tf_op jit(solution)/shard_map/all_to_all | solution.py:432
  95.4 1.9 %copy-done.1 = f32[3,2,4,136,256]{4,3,2,1,0:T(8,128)S(1)} copy-done((f32[3,2,4,136,256]{4,3,2,1,0:T(8,128)S(1)}, f32[3,2,4,136,256]{4,3,2,1,0:T(8,128)}, u32[]{:S(2)}) %copy-start.1) | copy-done | bytes 3342360
  97.3 2.3 %shard_map.73.rest = f32[3,2,136,256]{3,2,1,0:T(8,128)} custom-call(f32[8,72,128]{2,1,0:T(8,128)S(1)} %all_to_all.30.received.refs_0_, f32[4,72,128]{2,1,0:T(8,128)S(1)} %collective-permute-done.2.below.refs_1_, f32[4,72,128]{2,1,0:T(8,128)S(1)} %collective-permute-done.3.above.refs_2_, f32[3,2,4,136,256]{4,3,2,1,0:T(8,128)S(1)} %copy-done.1), custom_call_target="tpu_custom_call" | custom-call | flops 3000000000 | bytes 3000000 | tf_op jit(solution)/shard_map/pallas_call | solution.py:395
  99.6 5.8 %all-to-all-done.3.blocks = f32[8,72,128]{2,1,0:T(8,128)S(1)} async-done(((f32[8,72,128]{2,1,0:T(8,128)}), f32[8,72,128]{2,1,0:T(8,128)S(1)}, u32[]{:S(2)}, u32[]{:S(2)}) %all-to-all-start.3) | async-done | bytes 294944 | tf_op jit(solution)/shard_map/all_to_all | solution.py:432
  105.4 1.8 %shard_map.74 = f32[4,216,128]{2,1,0:T(8,128)} custom-call(f32[8,144,128]{2,1,0:T(8,128)S(1)} %copy-done.4, f32[8,72,128]{2,1,0:T(8,128)S(1)} %all-to-all-done.3.blocks), custom_call_target="tpu_custom_call" | custom-call | flops 1500000000 | bytes 1500000 | tf_op jit(solution)/shard_map/pallas_call | solution.py:395
  107.2 3.5 %all-to-all-start.4 = ((f32[4,216,128]{2,1,0:T(8,128)}), f32[4,216,128]{2,1,0:T(8,128)S(1)}, u32[]{:S(2)}, u32[]{:S(2)}) async-start(f32[4,216,128]{2,1,0:T(8,128)} %shard_map.74), calls=%async_computation.4 | async-start | bytes 884736 | tf_op jit(solution)/shard_map/all_to_all | solution.py:432
  110.6 1.5 %shard_map.75.states = f32[7,136,256]{2,1,0:T(8,128)S(1)} custom-call(f32[8,144,128]{2,1,0:T(8,128)S(1)} %copy-done.4, f32[8,72,128]{2,1,0:T(8,128)S(1)} %all-to-all-done.3.blocks), custom_call_target="tpu_custom_call" | custom-call | flops 2500000000 | bytes 2500000 | tf_op jit(solution)/shard_map/pallas_call | solution.py:395
  112.1 5.9 %all-to-all-done.4.received = f32[4,216,128]{2,1,0:T(8,128)S(1)} async-done(((f32[4,216,128]{2,1,0:T(8,128)}), f32[4,216,128]{2,1,0:T(8,128)S(1)}, u32[]{:S(2)}, u32[]{:S(2)}) %all-to-all-start.4) | async-done | bytes 442400 | tf_op jit(solution)/shard_map/all_to_all | solution.py:432
  118.1 1.1 shard_map.76
  119.2 15.4 %all_to_all.31.received = f32[8,72,128]{2,1,0:T(8,128)S(1)} all-to-all(f32[8,72,128]{2,1,0:T(8,128)S(1)} %shard_map.76), channel_id=1, replica_groups={{0,16,32,48,64,80,96,112},{128,144,160,176,192,208,224,240},{256,272,28..., dimensions={0} | all-to-all | bytes 589824 | tf_op jit(solution)/shard_map/all_to_all | solution.py:432
  134.6 0.0 copy-done.3
  134.6 1.6 %shard_map.77 = f32[2160,128]{1,0:T(8,128)} custom-call(f32[8,72,128]{2,1,0:T(8,128)S(1)} %all_to_all.31.received, f32[4,2,136,256]{3,2,1,0:T(8,128)S(1)} %copy-done.2, f32[2,136,256]{2,1,0:T(8,128)S(1)} %get-tuple-element.45.first, f32[3,2,136,256]{3,2,1,0:T(8,128)S(1)} %copy-done.3), custom_call_target="tpu_custom_call" | custom-call | flops 2000000000 | bytes 2000000 | tf_op jit(solution)/shard_map/pallas_call | solution.py:395
  (21 shorter events, 0.1 us)
Async XLA Ops:
  0.0 1.3 copy-start.8
  0.0 1.4 %copy-start.10 = (bf16[4,2,1,135,135]{4,1,3,2,0:T(2,128)(2,1)S(1)}, bf16[4,2,1,135,135]{4,1,3,2,0:T(2,128)(2,1)}, u32[]{:S(2)}) copy-start(bf16[4,2,1,135,135]{4,1,3,2,0:T(2,128)(2,1)} %param.8) | copy-start | bytes 874804
  0.0 1.5 %copy-start.11 = (bf16[4,2,1,135,135]{4,1,3,2,0:T(2,128)(2,1)S(1)}, bf16[4,2,1,135,135]{4,1,3,2,0:T(2,128)(2,1)}, u32[]{:S(2)}) copy-start(bf16[4,2,1,135,135]{4,1,3,2,0:T(2,128)(2,1)} %param.9) | copy-start | bytes 874804
  5.2 46.0 %all-to-all-start = ((f32[8,360,128]{2,1,0:T(8,128)}), f32[8,360,128]{2,1,0:T(8,128)S(1)}, u32[]{:S(2)}, u32[]{:S(2)}) async-start(f32[8,360,128]{2,1,0:T(8,128)} %shard_map.64), calls=%async_computation | async-start | bytes 2949120 | tf_op jit(solution)/shard_map/all_to_all | solution.py:432
  12.9 1.1 copy-start.9
  17.8 14.8 %collective-permute-start = (f32[4,416,128]{2,1,0:T(8,128)}, f32[4,416,128]{2,1,0:T(8,128)S(1)}, u32[]{:S(2)}, u32[]{:S(2)}) collective-permute-start(f32[4,416,128]{2,1,0:T(8,128)} %get-tuple-element.31), channel_id=1, source_target_pairs={{0,1},{1,2},{2,3},{3,4},{4,5},{5,6},{6,7},{7,8},{8,9},{9,10},{10,1... | collective-permute-start | bytes 2555912 | tf_op jit(solution)/shard_map/ppermute | solution.py:435
  22.7 14.5 %collective-permute-start.1 = (f32[4,416,128]{2,1,0:T(8,128)}, f32[4,416,128]{2,1,0:T(8,128)S(1)}, u32[]{:S(2)}, u32[]{:S(2)}) collective-permute-start(f32[4,416,128]{2,1,0:T(8,128)} %get-tuple-element.32), channel_id=1, source_target_pairs={{1,0},{2,1},{3,2},{4,3},{5,4},{6,5},{7,6},{8,7},{9,8},{10,9},{11,1... | collective-permute-start | bytes 2555912 | tf_op jit(solution)/shard_map/ppermute | solution.py:438
  24.7 2.6 %copy-start.12 = (bf16[4,2,1,135,135]{4,1,3,2,0:T(2,128)(2,1)S(1)}, bf16[4,2,1,135,135]{4,1,3,2,0:T(2,128)(2,1)}, u32[]{:S(2)}) copy-start(bf16[4,2,1,135,135]{4,1,3,2,0:T(2,128)(2,1)} %param.11) | copy-start | bytes 874804
  24.7 2.6 %copy-start.13 = (bf16[4,2,1,135,135]{4,1,3,2,0:T(2,128)(2,1)S(1)}, bf16[4,2,1,135,135]{4,1,3,2,0:T(2,128)(2,1)}, u32[]{:S(2)}) copy-start(bf16[4,2,1,135,135]{4,1,3,2,0:T(2,128)(2,1)} %param.10) | copy-start | bytes 874804
  24.7 12.5 %copy-start.7 = (f32[4,2,136,256]{3,2,1,0:T(8,128)S(1)}, f32[4,2,136,256]{3,2,1,0:T(8,128)}, u32[]{:S(2)}) copy-start(f32[4,2,136,256]{3,2,1,0:T(8,128)} %get-tuple-element.30.refs_4_) | copy-start | bytes 3342340
  27.3 9.9 %copy-start.5 = (f32[4,2,136,256]{3,2,1,0:T(8,128)S(1)}, f32[4,2,136,256]{3,2,1,0:T(8,128)}, u32[]{:S(2)}) copy-start(f32[4,2,136,256]{3,2,1,0:T(8,128)} %get-tuple-element.34.refs_7_) | copy-start | bytes 3342340
  27.3 9.9 %copy-start.6 = (f32[4,2,136,256]{3,2,1,0:T(8,128)S(1)}, f32[4,2,136,256]{3,2,1,0:T(8,128)}, u32[]{:S(2)}) copy-start(f32[4,2,136,256]{3,2,1,0:T(8,128)} %get-tuple-element.29.refs_3_) | copy-start | bytes 3342340
  52.9 10.4 %all-to-all-start.1 = ((f32[4,216,128]{2,1,0:T(8,128)}), f32[4,216,128]{2,1,0:T(8,128)S(1)}, u32[]{:S(2)}, u32[]{:S(2)}) async-start(f32[4,216,128]{2,1,0:T(8,128)} %shard_map.69), calls=%async_computation.1 | async-start | bytes 884736 | tf_op jit(solution)/shard_map/all_to_all | solution.py:432
  64.5 21.9 %copy-start = (f32[2,4,136,256]{3,2,1,0:T(8,128)S(1)}, f32[2,4,136,256]{3,2,1,0:T(8,128)}, u32[]{:S(2)}) copy-start(f32[2,4,136,256]{3,2,1,0:T(8,128)} %get-tuple-element.40.plan) | copy-start | bytes 3342340
  76.8 10.2 %collective-permute-start.2 = (f32[4,72,128]{2,1,0:T(8,128)S(1)}, f32[4,72,128]{2,1,0:T(8,128)S(1)}, u32[]{:S(2)}, u32[]{:S(2)}) collective-permute-start(f32[4,72,128]{2,1,0:T(8,128)S(1)} %get-tuple-element.48), channel_id=1, source_target_pairs={{0,1},{1,2},{2,3},{3,4},{4,5},{5,6},{6,7},{7,8},{8,9},{9,10},{10,1... | collective-permute-start | bytes 442376 | tf_op jit(solution)/shard_map/ppermute | solution.py:435
  84.2 6.5 %collective-permute-start.3 = (f32[4,72,128]{2,1,0:T(8,128)S(1)}, f32[4,72,128]{2,1,0:T(8,128)S(1)}, u32[]{:S(2)}, u32[]{:S(2)}) collective-permute-start(f32[4,72,128]{2,1,0:T(8,128)S(1)} %get-tuple-element.47), channel_id=1, source_target_pairs={{1,0},{2,1},{3,2},{4,3},{5,4},{6,5},{7,6},{8,7},{9,8},{10,9},{11,1... | collective-permute-start | bytes 442376 | tf_op jit(solution)/shard_map/ppermute | solution.py:438
  92.0 13.5 %all-to-all-start.3 = ((f32[8,72,128]{2,1,0:T(8,128)}), f32[8,72,128]{2,1,0:T(8,128)S(1)}, u32[]{:S(2)}, u32[]{:S(2)}) async-start(f32[8,72,128]{2,1,0:T(8,128)} %get-tuple-element.41), calls=%async_computation.3 | async-start | bytes 589824 | tf_op jit(solution)/shard_map/all_to_all | solution.py:432
  95.4 1.9 %copy-start.1 = (f32[3,2,4,136,256]{4,3,2,1,0:T(8,128)S(1)}, f32[3,2,4,136,256]{4,3,2,1,0:T(8,128)}, u32[]{:S(2)}) copy-start(f32[3,2,4,136,256]{4,3,2,1,0:T(8,128)} %get-tuple-element.42.refs_3_) | copy-start | bytes 10027012
  97.3 8.1 %copy-start.4 = (f32[8,144,128]{2,1,0:T(8,128)S(1)}, f32[8,144,128]{2,1,0:T(8,128)}, u32[]{:S(2)}) copy-start(f32[8,144,128]{2,1,0:T(8,128)} %get-tuple-element.38.matrices) | copy-start | bytes 1769476
  107.2 10.9 %all-to-all-start.4 = ((f32[4,216,128]{2,1,0:T(8,128)}), f32[4,216,128]{2,1,0:T(8,128)S(1)}, u32[]{:S(2)}, u32[]{:S(2)}) async-start(f32[4,216,128]{2,1,0:T(8,128)} %shard_map.74), calls=%async_computation.4 | async-start | bytes 884736 | tf_op jit(solution)/shard_map/all_to_all | solution.py:432
  112.1 22.4 %copy-start.2 = (f32[4,2,136,256]{3,2,1,0:T(8,128)S(1)}, f32[4,2,136,256]{3,2,1,0:T(8,128)}, u32[]{:S(2)}) copy-start(f32[4,2,136,256]{3,2,1,0:T(8,128)} %get-tuple-element.44.maps) | copy-start | bytes 3342340
  118.1 16.5 %copy-start.3 = (f32[3,2,136,256]{3,2,1,0:T(8,128)S(1)}, f32[3,2,136,256]{3,2,1,0:T(8,128)}, u32[]{:S(2)}) copy-start(f32[3,2,136,256]{3,2,1,0:T(8,128)} %shard_map.73.rest) | copy-start | bytes 2506756

commit v4 on v3

--- a/solution.py
+++ b/solution.py
@@ -515,8 +515,8 @@
         us=0.6,
     )
     received = exchange(sent, inside)
+    received, more = lax.optimization_barrier((received, more))
     (values,) = call(levels, [others], entering, below, above, more, us=3, kept=1)
-    received, values = lax.optimization_barrier((received, values))
     order = range(ROW - 1, -1, -1)
     (sent,) = call(
         functools.partial(whole_run, full, order),
@@ -533,6 +533,7 @@
         received,
         us=2.5,
     )
+    joined, values = lax.optimization_barrier((joined, values))
     entering = settle(True, joined, states)
     lines = positions * columns * unknowns * 2
     (update,) = call(

time: 139 us -> 137 us (0.986)
  blocking collectives: 27.6 us -> 40.2 us
  waiting for transfers between devices: 37.6 us -> 28.7 us
  starting transfers between devices: 34.3 us -> 30.9 us
  local copies, waits for them, and re-layouts: 5.12 us -> 3.64 us
    all_to_all x2 -> x3, blocking collectives: 27.6 us -> 40.2 us  [exchange(): return lax.all_to_all(x, 'sweep', 0, 0, axis_index_groups=groups)]
    all_to_all x4 -> x3, waiting for transfers between devices: 24.1 us -> 15.2 us  [exchange(): return lax.all_to_all(x, 'sweep', 0, 0, axis_index_groups=groups)]
    all_to_all x4 -> x3, starting transfers between devices: 18 us -> 14.6 us  [exchange(): return lax.all_to_all(x, 'sweep', 0, 0, axis_index_groups=groups)]
    unnamed x30, local copies, waits for them, and re-layouts: 4.47 us -> 2.99 us
  transfers between devices with their start and end apart: 8 -> 7, of which waited for: 7 -> 6; matrix products, arithmetic and copies ran while one was open for 0% -> 0% of each run, Pallas kernels for 14% -> 14%
where the time goes in v4:
time: 137 us; the launch traced here: 134 us
  blocking collectives  40.2 us (29%)
  starting transfers between devices  30.9 us (23%)
  Pallas kernels  30.5 us (22%)
  waiting for transfers between devices  28.7 us (21%)
  local copies, waits for them, and re-layouts  3.64 us (3%)
    all_to_all x3, blocking collectives, exchange(): return lax.all_to_all(x, 'sweep', 0, 0, axis_index_groups=groups)  40.2 us
    pallas_call x14, Pallas kernels, call(): pl.pallas_call(with_copies if kept else kernel, out_shape=[jax.ShapeDtype...  30.5 us
    all_to_all x3, waiting for transfers between devices, exchange(): return lax.all_to_all(x, 'sweep', 0, 0, axis_index_groups=groups)  15.2 us
    all_to_all x3, starting transfers between devices, exchange(): return lax.all_to_all(x, 'sweep', 0, 0, axis_index_groups=groups)  14.6 us
    ppermute x2, starting transfers between devices, from_below(): return lax.ppermute(x, 'cross', [(i, i + 1) for i in range(ends)])  12.3 us
    ppermute x2, waiting for transfers between devices, from_above(): return lax.ppermute(x, 'cross', [(i + 1, i) for i in range(ends)])  8.33 us
    ppermute x2, waiting for transfers between devices, from_below(): return lax.ppermute(x, 'cross', [(i, i + 1) for i in range(ends)])  5.11 us
    ppermute x2, starting transfers between devices, from_above(): return lax.ppermute(x, 'cross', [(i + 1, i) for i in range(ends)])  4.02 us
  transfers between devices with their start and end apart: 7, of which 6 were waited for; matrix products, arithmetic and copies ran while one was open for 0% of the time, Pallas kernels for 14%

profile of v4, /device:TPU:1, one launch (start us, length us, event | category | flops | bytes accessed | tf_op | source)
XLA Modules:
  0.0 134.4 jit_solution(3495133568001164446)
XLA Ops:
  0.0 1.3 copy.43
  1.3 0.1 copy.44
  1.4 0.0 copy-done.10
  1.4 0.2 copy-done.11
  1.6 0.2 copy_bitcast_fusion.7
  1.7 3.5 %shard_map.64 = f32[8,360,128]{2,1,0:T(8,128)} custom-call(bf16[4,2,135,135]{3,2,1,0:T(8,128)(2,1)S(1)} %bitcast.32, bf16[4,2,135,135]{3,2,1,0:T(8,128)(2,1)S(1)} %get-tuple-element.54.before, bf16[4,2,135,135]{3,2,1,0:T(8,128)(2,1)S(1)} %get-tuple-element.53.after, bf16[4,2,135,256]{3,2,1,0:T(8,128)(2,1)S(1)} %bitcast.31), custom_call_target="tpu_custom_call" | custom-call | flops 4000000000 | bytes 4000000 | tf_op jit(solution)/shard_map/pallas_call | solution.py:395
  5.2 7.7 %all-to-all-start = ((f32[8,360,128]{2,1,0:T(8,128)}), f32[8,360,128]{2,1,0:T(8,128)S(1)}, u32[]{:S(2)}, u32[]{:S(2)}) async-start(f32[8,360,128]{2,1,0:T(8,128)} %shard_map.64), calls=%async_computation | async-start | bytes 2949120 | tf_op jit(solution)/shard_map/all_to_all | solution.py:432
  12.9 0.1 copy.42
  12.9 1.0 copy-done.9
  13.9 0.1 copy.40
  14.0 0.1 copy.41
  14.1 3.8 %shard_map.65 = (f32[4,416,128]{2,1,0:T(8,128)}, f32[4,416,128]{2,1,0:T(8,128)}, f32[4,2,136,256]{3,2,1,0:T(8,128)}, f32[4,2,136,256]{3,2,1,0:T(8,128)}) custom-call(bf16[4,2,135,135]{3,2,1,0:T(8,128)(2,1)S(1)} %bitcast.28, bf16[4,2,135,135]{3,2,1,0:T(8,128)(2,1)S(1)} %bitcast.34, bf16[4,2,135,256]{3,2,1,0:T(8,128)(2,1)S(1)} %bitcast.33), custom_call_target="tpu_custom_call" | custom-call | flops 3000000000 | bytes 3000000 | tf_op jit(solution)/shard_map/pallas_call | solution.py:395
  17.8 4.8 %collective-permute-start = (f32[4,416,128]{2,1,0:T(8,128)}, f32[4,416,128]{2,1,0:T(8,128)S(1)}, u32[]{:S(2)}, u32[]{:S(2)}) collective-permute-start(f32[4,416,128]{2,1,0:T(8,128)} %get-tuple-element.33), channel_id=1, source_target_pairs={{0,1},{1,2},{2,3},{3,4},{4,5},{5,6},{6,7},{7,8},{8,9},{9,10},{10,1... | collective-permute-start | bytes 2555912 | tf_op jit(solution)/shard_map/ppermute | solution.py:435
  22.7 1.9 %collective-permute-start.1 = (f32[4,416,128]{2,1,0:T(8,128)}, f32[4,416,128]{2,1,0:T(8,128)S(1)}, u32[]{:S(2)}, u32[]{:S(2)}) collective-permute-start(f32[4,416,128]{2,1,0:T(8,128)} %get-tuple-element.34), channel_id=1, source_target_pairs={{1,0},{2,1},{3,2},{4,3},{5,4},{6,5},{7,6},{8,7},{9,8},{10,9},{11,1... | collective-permute-start | bytes 2555912 | tf_op jit(solution)/shard_map/ppermute | solution.py:438
  24.6 0.1 copy.39
  24.7 0.0 copy-start.12
  24.7 0.0 copy-start.13
  24.7 2.6 %shard_map.66 = (f32[4,2,136,256]{3,2,1,0:T(8,128)}, f32[4,2,136,256]{3,2,1,0:T(8,128)}) custom-call(bf16[4,2,135,135]{3,2,1,0:T(8,128)(2,1)S(1)} %bitcast.29, bf16[4,2,135,135]{3,2,1,0:T(8,128)(2,1)S(1)} %bitcast.35), custom_call_target="tpu_custom_call" | custom-call | flops 2000000000 | bytes 2000000 | tf_op jit(solution)/shard_map/pallas_call | solution.py:395
  27.3 0.2 copy_bitcast_fusion.3
  27.5 5.1 %collective-permute-done.refs_5_ = f32[4,416,128]{2,1,0:T(8,128)S(1)} collective-permute-done((f32[4,416,128]{2,1,0:T(8,128)}, f32[4,416,128]{2,1,0:T(8,128)S(1)}, u32[]{:S(2)}, u32[]{:S(2)}) %collective-permute-start) | collective-permute-done | bytes 852000 | tf_op jit(solution)/shard_map/ppermute | solution.py:435
  32.6 4.6 %collective-permute-done.1.refs_6_ = f32[4,416,128]{2,1,0:T(8,128)S(1)} collective-permute-done((f32[4,416,128]{2,1,0:T(8,128)}, f32[4,416,128]{2,1,0:T(8,128)S(1)}, u32[]{:S(2)}, u32[]{:S(2)}) %collective-permute-start.1) | collective-permute-done | bytes 852000 | tf_op jit(solution)/shard_map/ppermute | solution.py:438
  37.2 0.0 copy-done.7
  37.2 6.6 %shard_map.67 = (f32[2,4,136,256]{3,2,1,0:T(8,128)}, f32[3,2,4,136,256]{4,3,2,1,0:T(8,128)}) custom-call(bf16[4,2,135,135]{3,2,1,0:T(8,128)(2,1)S(1)} %bitcast.30, bf16[4,2,135,135]{3,2,1,0:T(8,128)(2,1)S(1)} %get-tuple-element.56.refs_1_, bf16[4,2,135,135]{3,2,1,0:T(8,128)(2,1)S(1)} %get-tuple-element.55.refs_2_, f32[4,2,136,256]{3,2,1,0:T(8,128)S(1)} %copy-done.6, ...), custom_call_target="tpu_custom_call" | custom-call | flops 6000000000 | bytes 6000000 | tf_op jit(solution)/shard_map/pallas_call | solution.py:395
  43.8 7.4 %all-to-all-done.received = f32[8,360,128]{2,1,0:T(8,128)S(1)} async-done(((f32[8,360,128]{2,1,0:T(8,128)}), f32[8,360,128]{2,1,0:T(8,128)S(1)}, u32[]{:S(2)}, u32[]{:S(2)}) %all-to-all-start) | async-done | bytes 1474592 | tf_op jit(solution)/shard_map/all_to_all | solution.py:432
  51.2 1.8 %shard_map.69 = f32[4,216,128]{2,1,0:T(8,128)} custom-call(f32[8,360,128]{2,1,0:T(8,128)S(1)} %all-to-all-done.received), custom_call_target="tpu_custom_call" | custom-call | flops 1500000000 | bytes 1500000 | tf_op jit(solution)/shard_map/pallas_call | solution.py:395
  52.9 3.5 %all-to-all-start.1 = ((f32[4,216,128]{2,1,0:T(8,128)}), f32[4,216,128]{2,1,0:T(8,128)S(1)}, u32[]{:S(2)}, u32[]{:S(2)}) async-start(f32[4,216,128]{2,1,0:T(8,128)} %shard_map.69), calls=%async_computation.1 | async-start | bytes 884736 | tf_op jit(solution)/shard_map/all_to_all | solution.py:432
  56.4 1.9 %shard_map.68 = (f32[7,136,256]{2,1,0:T(8,128)S(1)}, f32[8,144,128]{2,1,0:T(8,128)}) custom-call(f32[8,360,128]{2,1,0:T(8,128)S(1)} %all-to-all-done.received), custom_call_target="tpu_custom_call" | custom-call | flops 2500000000 | bytes 2500000 | tf_op jit(solution)/shard_map/pallas_call | solution.py:395
  58.3 5.0 %all-to-all-done.1.received = f32[4,216,128]{2,1,0:T(8,128)S(1)} async-done(((f32[4,216,128]{2,1,0:T(8,128)}), f32[4,216,128]{2,1,0:T(8,128)S(1)}, u32[]{:S(2)}, u32[]{:S(2)}) %all-to-all-start.1) | async-done | bytes 442400 | tf_op jit(solution)/shard_map/all_to_all | solution.py:432
  63.4 1.1 shard_map.70
  64.5 12.3 %all_to_all.30.received.refs_0_ = f32[8,72,128]{2,1,0:T(8,128)S(1)} all-to-all(f32[8,72,128]{2,1,0:T(8,128)S(1)} %shard_map.70), channel_id=1, replica_groups={{0,16,32,48,64,80,96,112},{128,144,160,176,192,208,224,240},{256,272,28..., dimensions={0} | all-to-all | bytes 589824 | tf_op jit(solution)/shard_map/all_to_all | solution.py:432
  76.8 7.4 %collective-permute-start.2 = (f32[4,72,128]{2,1,0:T(8,128)S(1)}, f32[4,72,128]{2,1,0:T(8,128)S(1)}, u32[]{:S(2)}, u32[]{:S(2)}) collective-permute-start(f32[4,72,128]{2,1,0:T(8,128)S(1)} %get-tuple-element.52), channel_id=1, source_target_pairs={{0,1},{1,2},{2,3},{3,4},{4,5},{5,6},{6,7},{7,8},{8,9},{9,10},{10,1... | collective-permute-start | bytes 442376 | tf_op jit(solution)/shard_map/ppermute | solution.py:435
  84.2 2.1 %collective-permute-start.3 = (f32[4,72,128]{2,1,0:T(8,128)S(1)}, f32[4,72,128]{2,1,0:T(8,128)S(1)}, u32[]{:S(2)}, u32[]{:S(2)}) collective-permute-start(f32[4,72,128]{2,1,0:T(8,128)S(1)} %get-tuple-element.51), channel_id=1, source_target_pairs={{1,0},{2,1},{3,2},{4,3},{5,4},{6,5},{7,6},{8,7},{9,8},{10,9},{11,1... | collective-permute-start | bytes 442376 | tf_op jit(solution)/shard_map/ppermute | solution.py:438
  86.3 0.6 shard_map.71.part
  86.9 0.0 copy-start.4
  86.9 0.0 collective-permute-done.2.below.refs_1_
  86.9 3.7 %collective-permute-done.3.above.refs_2_ = f32[4,72,128]{2,1,0:T(8,128)S(1)} collective-permute-done((f32[4,72,128]{2,1,0:T(8,128)S(1)}, f32[4,72,128]{2,1,0:T(8,128)S(1)}, u32[]{:S(2)}, u32[]{:S(2)}) %collective-permute-start.3) | collective-permute-done | bytes 147488 | tf_op jit(solution)/shard_map/ppermute | solution.py:438
  90.7 0.6 shard_map.72
  91.2 12.5 %all_to_all.31.blocks = f32[8,72,128]{2,1,0:T(8,128)S(1)} all-to-all(f32[8,72,128]{2,1,0:T(8,128)S(1)} %get-tuple-element.43), channel_id=1, replica_groups={{0,16,32,48,64,80,96,112},{128,144,160,176,192,208,224,240},{256,272,28..., dimensions={0} | all-to-all | bytes 589824 | tf_op jit(solution)/shard_map/all_to_all | solution.py:432
  103.7 1.8 %shard_map.73 = f32[4,216,128]{2,1,0:T(8,128)} custom-call(f32[8,144,128]{2,1,0:T(8,128)S(1)} %copy-done.4, f32[8,72,128]{2,1,0:T(8,128)S(1)} %all_to_all.31.blocks), custom_call_target="tpu_custom_call" | custom-call | flops 1500000000 | bytes 1500000 | tf_op jit(solution)/shard_map/pallas_call | solution.py:395
  105.5 3.5 %all-to-all-start.4 = ((f32[4,216,128]{2,1,0:T(8,128)}), f32[4,216,128]{2,1,0:T(8,128)S(1)}, u32[]{:S(2)}, u32[]{:S(2)}) async-start(f32[4,216,128]{2,1,0:T(8,128)} %shard_map.73), calls=%async_computation.4 | async-start | bytes 884736 | tf_op jit(solution)/shard_map/all_to_all | solution.py:432
  109.0 1.5 %shard_map.75.states = f32[7,136,256]{2,1,0:T(8,128)S(1)} custom-call(f32[8,144,128]{2,1,0:T(8,128)S(1)} %copy-done.4, f32[8,72,128]{2,1,0:T(8,128)S(1)} %all_to_all.31.blocks), custom_call_target="tpu_custom_call" | custom-call | flops 2500000000 | bytes 2500000 | tf_op jit(solution)/shard_map/pallas_call | solution.py:395
  110.5 0.4 copy-done.1
  110.9 2.3 %shard_map.74.rest = f32[3,2,136,256]{3,2,1,0:T(8,128)} custom-call(f32[8,72,128]{2,1,0:T(8,128)S(1)} %all_to_all.30.received.refs_0_, f32[4,72,128]{2,1,0:T(8,128)S(1)} %collective-permute-done.2.below.refs_1_, f32[4,72,128]{2,1,0:T(8,128)S(1)} %collective-permute-done.3.above.refs_2_, f32[3,2,4,136,256]{4,3,2,1,0:T(8,128)S(1)} %copy-done.1), custom_call_target="tpu_custom_call" | custom-call | flops 3000000000 | bytes 3000000 | tf_op jit(solution)/shard_map/pallas_call | solution.py:395
  113.2 0.0 copy-start.3
  113.2 2.8 %all-to-all-done.4.received = f32[4,216,128]{2,1,0:T(8,128)S(1)} async-done(((f32[4,216,128]{2,1,0:T(8,128)}), f32[4,216,128]{2,1,0:T(8,128)S(1)}, u32[]{:S(2)}, u32[]{:S(2)}) %all-to-all-start.4) | async-done | bytes 442400 | tf_op jit(solution)/shard_map/all_to_all | solution.py:432
  116.0 1.1 shard_map.76
  117.1 15.5 %all_to_all.32.received = f32[8,72,128]{2,1,0:T(8,128)S(1)} all-to-all(f32[8,72,128]{2,1,0:T(8,128)S(1)} %shard_map.76), channel_id=1, replica_groups={{0,16,32,48,64,80,96,112},{128,144,160,176,192,208,224,240},{256,272,28..., dimensions={0} | all-to-all | bytes 589824 | tf_op jit(solution)/shard_map/all_to_all | solution.py:432
  132.6 1.6 %shard_map.77 = f32[2160,128]{1,0:T(8,128)} custom-call(f32[8,72,128]{2,1,0:T(8,128)S(1)} %all_to_all.32.received, f32[4,2,136,256]{3,2,1,0:T(8,128)S(1)} %copy-done.2, f32[2,136,256]{2,1,0:T(8,128)S(1)} %get-tuple-element.49.first, f32[3,2,136,256]{3,2,1,0:T(8,128)S(1)} %copy-done.3), custom_call_target="tpu_custom_call" | custom-call | flops 2000000000 | bytes 2000000 | tf_op jit(solution)/shard_map/pallas_call | solution.py:395
  (20 shorter events, 0.1 us)
Async XLA Ops:
  0.0 1.3 copy-start.8
  0.0 1.4 %copy-start.10 = (bf16[4,2,1,135,135]{4,1,3,2,0:T(2,128)(2,1)S(1)}, bf16[4,2,1,135,135]{4,1,3,2,0:T(2,128)(2,1)}, u32[]{:S(2)}) copy-start(bf16[4,2,1,135,135]{4,1,3,2,0:T(2,128)(2,1)} %param.8) | copy-start | bytes 874804
  0.0 1.5 %copy-start.11 = (bf16[4,2,1,135,135]{4,1,3,2,0:T(2,128)(2,1)S(1)}, bf16[4,2,1,135,135]{4,1,3,2,0:T(2,128)(2,1)}, u32[]{:S(2)}) copy-start(bf16[4,2,1,135,135]{4,1,3,2,0:T(2,128)(2,1)} %param.9) | copy-start | bytes 874804
  5.2 46.0 %all-to-all-start = ((f32[8,360,128]{2,1,0:T(8,128)}), f32[8,360,128]{2,1,0:T(8,128)S(1)}, u32[]{:S(2)}, u32[]{:S(2)}) async-start(f32[8,360,128]{2,1,0:T(8,128)} %shard_map.64), calls=%async_computation | async-start | bytes 2949120 | tf_op jit(solution)/shard_map/all_to_all | solution.py:432
  12.9 1.1 copy-start.9
  17.8 14.8 %collective-permute-start = (f32[4,416,128]{2,1,0:T(8,128)}, f32[4,416,128]{2,1,0:T(8,128)S(1)}, u32[]{:S(2)}, u32[]{:S(2)}) collective-permute-start(f32[4,416,128]{2,1,0:T(8,128)} %get-tuple-element.33), channel_id=1, source_target_pairs={{0,1},{1,2},{2,3},{3,4},{4,5},{5,6},{6,7},{7,8},{8,9},{9,10},{10,1... | collective-permute-start | bytes 2555912 | tf_op jit(solution)/shard_map/ppermute | solution.py:435
  22.7 14.5 %collective-permute-start.1 = (f32[4,416,128]{2,1,0:T(8,128)}, f32[4,416,128]{2,1,0:T(8,128)S(1)}, u32[]{:S(2)}, u32[]{:S(2)}) collective-permute-start(f32[4,416,128]{2,1,0:T(8,128)} %get-tuple-element.34), channel_id=1, source_target_pairs={{1,0},{2,1},{3,2},{4,3},{5,4},{6,5},{7,6},{8,7},{9,8},{10,9},{11,1... | collective-permute-start | bytes 2555912 | tf_op jit(solution)/shard_map/ppermute | solution.py:438
  24.7 2.6 %copy-start.12 = (bf16[4,2,1,135,135]{4,1,3,2,0:T(2,128)(2,1)S(1)}, bf16[4,2,1,135,135]{4,1,3,2,0:T(2,128)(2,1)}, u32[]{:S(2)}) copy-start(bf16[4,2,1,135,135]{4,1,3,2,0:T(2,128)(2,1)} %param.11) | copy-start | bytes 874804
  24.7 2.6 %copy-start.13 = (bf16[4,2,1,135,135]{4,1,3,2,0:T(2,128)(2,1)S(1)}, bf16[4,2,1,135,135]{4,1,3,2,0:T(2,128)(2,1)}, u32[]{:S(2)}) copy-start(bf16[4,2,1,135,135]{4,1,3,2,0:T(2,128)(2,1)} %param.10) | copy-start | bytes 874804
  24.7 12.5 %copy-start.7 = (f32[4,2,136,256]{3,2,1,0:T(8,128)S(1)}, f32[4,2,136,256]{3,2,1,0:T(8,128)}, u32[]{:S(2)}) copy-start(f32[4,2,136,256]{3,2,1,0:T(8,128)} %get-tuple-element.32.refs_4_) | copy-start | bytes 3342340
  27.3 9.9 %copy-start.5 = (f32[4,2,136,256]{3,2,1,0:T(8,128)S(1)}, f32[4,2,136,256]{3,2,1,0:T(8,128)}, u32[]{:S(2)}) copy-start(f32[4,2,136,256]{3,2,1,0:T(8,128)} %get-tuple-element.36.refs_7_) | copy-start | bytes 3342340
  27.3 9.9 %copy-start.6 = (f32[4,2,136,256]{3,2,1,0:T(8,128)S(1)}, f32[4,2,136,256]{3,2,1,0:T(8,128)}, u32[]{:S(2)}) copy-start(f32[4,2,136,256]{3,2,1,0:T(8,128)} %get-tuple-element.31.refs_3_) | copy-start | bytes 3342340
  52.9 10.4 %all-to-all-start.1 = ((f32[4,216,128]{2,1,0:T(8,128)}), f32[4,216,128]{2,1,0:T(8,128)S(1)}, u32[]{:S(2)}, u32[]{:S(2)}) async-start(f32[4,216,128]{2,1,0:T(8,128)} %shard_map.69), calls=%async_computation.1 | async-start | bytes 884736 | tf_op jit(solution)/shard_map/all_to_all | solution.py:432
  64.5 21.9 %copy-start = (f32[2,4,136,256]{3,2,1,0:T(8,128)S(1)}, f32[2,4,136,256]{3,2,1,0:T(8,128)}, u32[]{:S(2)}) copy-start(f32[2,4,136,256]{3,2,1,0:T(8,128)} %get-tuple-element.42.plan) | copy-start | bytes 3342340
  76.8 10.2 %collective-permute-start.2 = (f32[4,72,128]{2,1,0:T(8,128)S(1)}, f32[4,72,128]{2,1,0:T(8,128)S(1)}, u32[]{:S(2)}, u32[]{:S(2)}) collective-permute-start(f32[4,72,128]{2,1,0:T(8,128)S(1)} %get-tuple-element.52), channel_id=1, source_target_pairs={{0,1},{1,2},{2,3},{3,4},{4,5},{5,6},{6,7},{7,8},{8,9},{9,10},{10,1... | collective-permute-start | bytes 442376 | tf_op jit(solution)/shard_map/ppermute | solution.py:435
  84.2 6.5 %collective-permute-start.3 = (f32[4,72,128]{2,1,0:T(8,128)S(1)}, f32[4,72,128]{2,1,0:T(8,128)S(1)}, u32[]{:S(2)}, u32[]{:S(2)}) collective-permute-start(f32[4,72,128]{2,1,0:T(8,128)S(1)} %get-tuple-element.51), channel_id=1, source_target_pairs={{1,0},{2,1},{3,2},{4,3},{5,4},{6,5},{7,6},{8,7},{9,8},{10,9},{11,1... | collective-permute-start | bytes 442376 | tf_op jit(solution)/shard_map/ppermute | solution.py:438
  86.9 16.8 %copy-start.4 = (f32[8,144,128]{2,1,0:T(8,128)S(1)}, f32[8,144,128]{2,1,0:T(8,128)}, u32[]{:S(2)}) copy-start(f32[8,144,128]{2,1,0:T(8,128)} %get-tuple-element.40.matrices) | copy-start | bytes 1769476
  105.5 10.5 %all-to-all-start.4 = ((f32[4,216,128]{2,1,0:T(8,128)}), f32[4,216,128]{2,1,0:T(8,128)S(1)}, u32[]{:S(2)}, u32[]{:S(2)}) async-start(f32[4,216,128]{2,1,0:T(8,128)} %shard_map.73), calls=%async_computation.4 | async-start | bytes 884736 | tf_op jit(solution)/shard_map/all_to_all | solution.py:432
  109.0 1.9 %copy-start.1 = (f32[3,2,4,136,256]{4,3,2,1,0:T(8,128)S(1)}, f32[3,2,4,136,256]{4,3,2,1,0:T(8,128)}, u32[]{:S(2)}) copy-start(f32[3,2,4,136,256]{4,3,2,1,0:T(8,128)} %get-tuple-element.46.refs_3_) | copy-start | bytes 10027012
  113.2 19.5 %copy-start.3 = (f32[3,2,136,256]{3,2,1,0:T(8,128)S(1)}, f32[3,2,136,256]{3,2,1,0:T(8,128)}, u32[]{:S(2)}) copy-start(f32[3,2,136,256]{3,2,1,0:T(8,128)} %shard_map.74.rest) | copy-start | bytes 2506756
  116.0 16.6 %copy-start.2 = (f32[4,2,136,256]{3,2,1,0:T(8,128)S(1)}, f32[4,2,136,256]{3,2,1,0:T(8,128)}, u32[]{:S(2)}) copy-start(f32[4,2,136,256]{3,2,1,0:T(8,128)} %get-tuple-element.48.maps) | copy-start | bytes 3342340

commit v5 on v4

--- a/solution.py
+++ b/solution.py
@@ -122,11 +122,19 @@
             maps[s, c] = float_by_float(steps[s, c, :, :full], maps[s + 1, c])
 
 
+PIECES = 2
+
+
+def piece_rows(full):
+    return -(-(full + 8) // (8 * PIECES)) * 8
+
+
 def start(inverse, before, after, source, sent, maps, values, sems):
     positions, columns, unknowns, vectors = source.shape
     full = values.shape[-2]
     room = full + 8
     peers = ROW // columns
+    piece = piece_rows(full)
     copies = []
 
     def send(ref, at, low):
@@ -144,7 +152,7 @@
             steps = [float_by_float(*steps[k : k + 2]) for k in range(0, len(steps), 2)]
         maps[c, 1] = pack_map(padded(steps[0]))
         for q in range(peers):
-            send(maps.at[c, 1], c * peers + q, room)
+            send(maps.at[c, 1, pl.ds(q % PIECES * piece, piece)], c * peers + q, room)
     for c in range(columns):
         steps = [
             (-mul(inverse[s, c], before[s, c]), mul(inverse[s, c], source[s, c]))
@@ -162,7 +170,7 @@
             pair = value[:, q // 2 * LANES : (q // 2 + 1) * LANES]
             fold = (full // 8 + 1) // 2 * 8
             values[c, q, 0:fold] = pack_slice(pair, q % 2)
-            send(values.at[c, q, pl.ds(0, fold)], c * peers + q, 2 * room)
+            send(values.at[c, q, pl.ds(0, fold)], c * peers + q, room + piece)
     for copy in copies:
         copy.wait()
 
@@ -214,19 +222,30 @@
 
 def fore_views(full, received):
     room = full + 8
-    return received.at[:, 0:room], received.at[:, 2 * room :]
-
-
-def fore_run(full, received, sent):
+    fold = (full // 8 + 1) // 2 * 8
+    return received.at[:, 0:room], received.at[:, received.shape[1] - fold :]
+
+
+def fore_run(full, received, piece, sent):
+    room = full + 8
+    piece[...] = received[:, room : room + piece.shape[1]]
     whole_run(full, range(ROW), *fore_views(full, received), sent)
 
 
-def fore_prefixes(full, received, states, later, sem):
-    room = full + 8
-    copy = pltpu.make_async_copy(received.at[:, room : 2 * room], later, sem)
-    copy.start()
+def fore_prefixes(full, received, states):
     prefixes(full, range(ROW), *fore_views(full, received), states)
-    copy.wait()
+
+
+def fore_enter(full, row, place, own, other, joined, states, sent, later, sems):
+    rows = own.shape[1]
+    copies = []
+    for d, block in enumerate((own, other)):
+        at = pl.multiple_of((place[0] + d) % PIECES * rows, 8)
+        copies.append(pltpu.make_async_copy(block, later.at[:, pl.ds(at, rows)], sems.at[d]))
+        copies[-1].start()
+    enter(full, False, row, joined, states, sent)
+    for copy in copies:
+        copy.wait()
 
 
 def enter(full, backward, row, received, states, sent):
@@ -273,44 +292,62 @@
     return jnp.concatenate(parts, axis=1)
 
 
-def couple(inverse, lower, upper, head, tail, below, above, steps, plan, more):
+def couple(inverse, lower, upper, head, tail, steps, plan, more):
+    positions, columns, unknowns, _ = inverse.shape
+    forward = (head, tail)
+
+    def parts(s, c):
+        near = upper if c == 0 else lower
+        by_near = mul(inverse[s, c], near[s, c])
+        return [
+            forward[c][s, 0, :unknowns],
+            -float_by_float(by_near, forward[1 - c][s, 0, :unknowns]),
+            forward[c][s, 1, :unknowns]
+            - float_by_float(by_near, forward[1 - c][s, 1, :unknowns]),
+        ]
+
+    accumulate(parts, steps, unknowns, plan, more)
+
+
+def couple_far(inverse, lower, upper, below, above, steps, plan, more):
     positions, columns, unknowns, _ = inverse.shape
     full = plan.shape[-2]
     room = full + 8
-    forward = (head, tail)
     halo = (below, above)
-    for c in range(columns):
-        near, far = (upper, lower) if c == 0 else (lower, upper)
+
+    def parts(s, c):
+        far = lower if c == 0 else upper
+        by_far = -mul(inverse[s, c], far[s, c])
+        value = jnp.concatenate(
+            [halo[c][s, room : room + full], halo[c][s, room + full :]], axis=1
+        )
+        return [
+            float_by_float(by_far, unpack_map(halo[c][s, 0:room])[:unknowns]),
+            float_by_float(by_far, value[:unknowns]),
+        ]
+
+    accumulate(parts, steps, unknowns, plan, more)
+
+
+def accumulate(parts, steps, unknowns, plan, more):
+    for c in range(plan.shape[0]):
         kept = None
-        for s in range(positions - 1, -1, -1):
-            by_near = mul(inverse[s, c], near[s, c])
-            by_far = mul(inverse[s, c], far[s, c])
-            far_map = unpack_map(halo[c][s, 0:room])
-            far_value = jnp.concatenate(
-                [halo[c][s, room : room + full], halo[c][s, room + full :]], axis=1
-            )
-            parts = [
-                forward[c][s, 0, :unknowns],
-                -float_by_float(by_near, forward[1 - c][s, 0, :unknowns]),
-                -float_by_float(by_far, far_map[:unknowns]),
-                forward[c][s, 1, :unknowns]
-                - float_by_float(by_near, forward[1 - c][s, 1, :unknowns])
-                - float_by_float(by_far, far_value[:unknowns]),
-            ]
+        for s in range(more.shape[0], -1, -1):
+            new = parts(s, c)
             if kept is not None:
                 step = steps[s, c, :unknowns, :unknowns]
-                parts = [part + float_by_float(step, old) for part, old in zip(parts, kept)]
-            kept = parts
-            for k in range(4):
-                put(*((plan, (c, k)) if s == 0 else (more, (s - 1, c, k))), kept[k])
-
-
-def near_part(received, plan, part):
+                new = [part + float_by_float(step, old) for part, old in zip(new, kept)]
+            kept = new
+            for k, value in enumerate(kept):
+                put(*((plan, (c, k)) if s == 0 else (more, (s - 1, c, k))), value)
+
+
+def near_part(received, plan, far_plan, part):
     columns, full, _ = part.shape
     peers = ROW // columns
     entering = [unpack_columns(full, received, c * peers, peers) for c in range(columns)]
     for c in range(columns):
-        part[c] = plan[c, 3] + (
+        part[c] = (plan[c, 2] + far_plan[c, 1]) + (
             float_by_float(plan[c, 0, :, :full], entering[c])
             + float_by_float(plan[c, 1, :, :full], entering[1 - c])
         )
@@ -322,26 +359,31 @@
     halo = (below, above)
     for c in range(columns):
         entering = unpack_columns(full, halo[c], 0, peers)
-        value = part[c] + float_by_float(plan[c, 2, :, :full], entering)
+        value = part[c] + float_by_float(plan[c, 0, :, :full], entering)
         values[c] = value
         for q in range(peers):
             pair = value[:, q // 2 * LANES : (q // 2 + 1) * LANES]
             sent[c * peers + q] = pack_slice(pair, q % 2)
 
 
-def levels(received, below, above, more, values):
+def levels(received, below, above, more, far_more, values):
     others, columns, full, _ = values.shape
     peers = ROW // columns
     entering = [unpack_columns(full, received, c * peers, peers) for c in range(columns)]
     halo = [unpack_columns(full, got, 0, peers) for got in (below, above)]
     for c in range(columns):
         total = None
-        for k, value in enumerate((entering[c], entering[1 - c], halo[c])):
-            stack = jnp.concatenate([more[s, c, k, :, :full] for s in range(others)], axis=0)
+        for maps, k, value in (
+            (more, 0, entering[c]),
+            (more, 1, entering[1 - c]),
+            (far_more, 0, halo[c]),
+        ):
+            stack = jnp.concatenate([maps[s, c, k, :, :full] for s in range(others)], axis=0)
             product = float_by_float(stack, value)
             total = product if total is None else total + product
         for s in range(others):
-            values[s, c] = more[s, c, 3] + total[s * full : (s + 1) * full]
+            value = more[s, c, 2] + far_more[s, c, 1]
+            values[s, c] = value + total[s * full : (s + 1) * full]
 
 
 def finish(received, maps, first, rest, result, out, sems):
@@ -418,6 +460,8 @@
     room = full + 8
     fold = (full // 8 + 1) // 2 * 8
     peers = ROW // columns
+    piece = piece_rows(full)
+    place = (lax.axis_index("sweep") % ROW).astype(jnp.int32).reshape(1)
     count = lax.axis_size("sweep")
     rows = count // ROW
     inside = [[r * ROW + i for i in range(ROW)] for r in range(rows)]
@@ -437,21 +481,9 @@
     def from_above(x):
         return lax.ppermute(x, "cross", [(i + 1, i) for i in range(ends)])
 
-    def settle(backward, joined, states):
-        (sent,) = call(
-            functools.partial(enter, full, backward),
-            [(ROW, fold, LANES)],
-            row,
-            joined,
-            states,
-            us=1,
-            smem=(0,),
-        )
-        return exchange(sent, inside)
-
     (sent,) = call(
         start,
-        [(ROW, 2 * room + fold, LANES)],
+        [(ROW, room + piece + fold, LANES)],
         inverse,
         before,
         after,
@@ -477,46 +509,75 @@
     below, above = from_below(second), from_above(first)
     plan, more = call(
         couple,
-        [(columns, 4, full, vectors), (positions - 1, columns, 4, full, vectors)],
+        [(columns, 3, full, vectors), (positions - 1, columns, 3, full, vectors)],
         inverse,
         lower,
         upper,
         head,
         tail,
+        back_steps,
+        us=4,
+        kept=2,
+    )
+    far_plan, far_more = call(
+        couple_far,
+        [(columns, 2, full, vectors), (positions - 1, columns, 2, full, vectors)],
+        inverse,
+        lower,
+        upper,
         below,
         above,
         back_steps,
-        us=6,
+        us=3,
         kept=2,
     )
-    received, plan, more = lax.optimization_barrier((received, plan, more))
-    (sent,) = call(
-        functools.partial(fore_run, full), [(rows, room + fold, LANES)], received, us=1.5
-    )
+    received, plan, more, far_plan, far_more = lax.optimization_barrier(
+        (received, plan, more, far_plan, far_more)
+    )
+    own, sent = call(
+        functools.partial(fore_run, full),
+        [(ROW, piece, LANES), (rows, room + fold, LANES)],
+        received,
+        us=1.5,
+    )
+
     joined = exchange(sent, across)
-    states, later = call(
+    other = lax.ppermute(own, "sweep", [(i, i ^ 1) for i in range(count)])
+    (states,) = call(
         functools.partial(fore_prefixes, full),
-        [(ROW - 1, full, 2 * LANES), (ROW, room, LANES)],
+        [(ROW - 1, full, 2 * LANES)],
         received,
-        us=2.5,
+        us=2,
+    )
+    sent, later = call(
+        functools.partial(fore_enter, full),
+        [(ROW, fold, LANES), (ROW, room, LANES)],
+        row,
+        place,
+        own,
+        other,
+        joined,
+        states,
+        us=1,
+        smem=(0, 1),
         direct=1,
-        scratch=[pltpu.SemaphoreType.DMA],
-    )
-    entering = settle(False, joined, states)
+        scratch=[pltpu.SemaphoreType.DMA((PIECES,))],
+    )
+    entering = exchange(sent, inside)
     below, above = from_below(entering[peers:]), from_above(entering[:peers])
-    (part,) = call(near_part, [(columns, full, vectors)], entering, plan, us=0.6)
+    (part,) = call(near_part, [(columns, full, vectors)], entering, plan, far_plan, us=0.6)
     sent, first = call(
         far_part,
         [(ROW, fold, LANES), (columns, full, vectors)],
         below,
         above,
-        plan,
+        far_plan,
         part,
         us=0.6,
     )
     received = exchange(sent, inside)
     received, more = lax.optimization_barrier((received, more))
-    (values,) = call(levels, [others], entering, below, above, more, us=3, kept=1)
+    (values,) = call(levels, [others], entering, below, above, more, far_more, us=3, kept=1)
     order = range(ROW - 1, -1, -1)
     (sent,) = call(
         functools.partial(whole_run, full, order),
@@ -534,7 +595,16 @@
         us=2.5,
     )
     joined, values = lax.optimization_barrier((joined, values))
-    entering = settle(True, joined, states)
+    (sent,) = call(
+        functools.partial(enter, full, True),
+        [(ROW, fold, LANES)],
+        row,
+        joined,
+        states,
+        us=1,
+        smem=(0,),
+    )
+    entering = exchange(sent, inside)
     lines = positions * columns * unknowns * 2
     (update,) = call(
         finish,

time: 137 us -> 136 us (level)
  waiting for transfers between devices: 28.7 us -> 19.3 us
  starting transfers between devices: 30.9 us -> 34.6 us
  blocking collectives: 40.2 us -> 42.7 us
  Pallas kernels: 30.5 us -> 32.6 us
    all_to_all x3, waiting for transfers between devices: 15.2 us -> 5.54 us  [exchange(): return lax.all_to_all(x, 'sweep', 0, 0, axis_index_groups=groups)]
    ppermute x0 -> x1, waiting for transfers between devices: none -> 6.21 us  [shards(): other = lax.ppermute(own, 'sweep', [(i, i ^ 1) for i in range(count)])]
    ppermute x2, waiting for transfers between devices: 5.11 us -> 0.01 us  [from_below(): return lax.ppermute(x, 'cross', [(i, i + 1) for i in range(ends)])]
    all_to_all x3, starting transfers between devices: 14.6 us -> 17.6 us  [exchange(): return lax.all_to_all(x, 'sweep', 0, 0, axis_index_groups=groups)]
    all_to_all x3, blocking collectives: 40.2 us -> 42.7 us  [exchange(): return lax.all_to_all(x, 'sweep', 0, 0, axis_index_groups=groups)]
    pallas_call x14 -> x15, Pallas kernels: 30.5 us -> 32.6 us  [call(): pl.pallas_call(with_copies if kept else kernel, out_shape=[jax.ShapeDtype...]
    ppermute x0 -> x1, starting transfers between devices: none -> 1.91 us  [shards(): other = lax.ppermute(own, 'sweep', [(i, i ^ 1) for i in range(count)])]
    unnamed x30 -> x34, local copies, waits for them, and re-layouts: 2.99 us -> 3.67 us
  transfers between devices with their start and end apart: 7 -> 8, of which waited for: 6 -> 5; matrix products, arithmetic and copies ran while one was open for 0% -> 0% of each run, Pallas kernels for 14% -> 16%
where the time goes in v5:
time: 136 us; the launch traced here: 134 us
  blocking collectives  42.7 us (31%)
  starting transfers between devices  34.6 us (25%)
  Pallas kernels  32.6 us (24%)
  waiting for transfers between devices  19.3 us (14%)
  local copies, waits for them, and re-layouts  4.33 us (3%)
    all_to_all x3, blocking collectives, exchange(): return lax.all_to_all(x, 'sweep', 0, 0, axis_index_groups=groups)  42.7 us
    pallas_call x15, Pallas kernels, call(): pl.pallas_call(with_copies if kept else kernel, out_shape=[jax.ShapeDtype...  32.6 us
    all_to_all x3, starting transfers between devices, exchange(): return lax.all_to_all(x, 'sweep', 0, 0, axis_index_groups=groups)  17.6 us
    ppermute x2, starting transfers between devices, from_below(): return lax.ppermute(x, 'cross', [(i, i + 1) for i in range(ends)])  11.2 us
    ppermute x2, waiting for transfers between devices, from_above(): return lax.ppermute(x, 'cross', [(i + 1, i) for i in range(ends)])  7.54 us
    ppermute x1, waiting for transfers between devices, shards(): other = lax.ppermute(own, 'sweep', [(i, i ^ 1) for i in range(count)])  6.21 us
    all_to_all x3, waiting for transfers between devices, exchange(): return lax.all_to_all(x, 'sweep', 0, 0, axis_index_groups=groups)  5.54 us
    ppermute x2, starting transfers between devices, from_above(): return lax.ppermute(x, 'cross', [(i + 1, i) for i in range(ends)])  3.84 us
  transfers between devices with their start and end apart: 8, of which 5 were waited for; matrix products, arithmetic and copies ran while one was open for 0% of the time, Pallas kernels for 16%

profile of v5, /device:TPU:1, one launch (start us, length us, event | category | flops | bytes accessed | tf_op | source)
XLA Modules:
  0.0 134.0 jit_solution(6785996950757526586)
XLA Ops:
  0.0 1.3 copy.44
  1.3 0.1 copy.43
  1.4 0.0 copy-done.13
  1.4 0.2 copy-done.11
  1.6 0.2 copy_bitcast_fusion.7
  1.7 3.5 %shard_map.64 = f32[8,288,128]{2,1,0:T(8,128)} custom-call(bf16[4,2,135,135]{3,2,1,0:T(8,128)(2,1)S(1)} %bitcast.33, bf16[4,2,135,135]{3,2,1,0:T(8,128)(2,1)S(1)} %get-tuple-element.66.before, bf16[4,2,135,135]{3,2,1,0:T(8,128)(2,1)S(1)} %get-tuple-element.65.after, bf16[4,2,135,256]{3,2,1,0:T(8,128)(2,1)S(1)} %bitcast.34), custom_call_target="tpu_custom_call" | custom-call | flops 4000000000 | bytes 4000000 | tf_op jit(solution)/shard_map/pallas_call | solution.py:437
  5.2 0.0 copy-start.10
  5.2 7.8 %all-to-all-start = ((f32[8,288,128]{2,1,0:T(8,128)}), f32[8,288,128]{2,1,0:T(8,128)S(1)}, u32[]{:S(2)}, u32[]{:S(2)}) async-start(f32[8,288,128]{2,1,0:T(8,128)} %shard_map.64), calls=%async_computation | async-start | bytes 2359296 | tf_op jit(solution)/shard_map/all_to_all | solution.py:476
  13.0 0.1 copy.42
  13.1 0.1 copy.41
  13.2 0.1 copy.40
  13.3 3.8 %shard_map.65 = (f32[4,416,128]{2,1,0:T(8,128)}, f32[4,416,128]{2,1,0:T(8,128)}, f32[4,2,136,256]{3,2,1,0:T(8,128)}, f32[4,2,136,256]{3,2,1,0:T(8,128)}) custom-call(bf16[4,2,135,135]{3,2,1,0:T(8,128)(2,1)S(1)} %bitcast.29, bf16[4,2,135,135]{3,2,1,0:T(8,128)(2,1)S(1)} %bitcast.35, bf16[4,2,135,256]{3,2,1,0:T(8,128)(2,1)S(1)} %bitcast.36), custom_call_target="tpu_custom_call" | custom-call | flops 3000000000 | bytes 3000000 | tf_op jit(solution)/shard_map/pallas_call | solution.py:437
  17.0 4.8 %collective-permute-start = (f32[4,416,128]{2,1,0:T(8,128)}, f32[4,416,128]{2,1,0:T(8,128)S(1)}, u32[]{:S(2)}, u32[]{:S(2)}) collective-permute-start(f32[4,416,128]{2,1,0:T(8,128)} %get-tuple-element.43), channel_id=1, source_target_pairs={{0,1},{1,2},{2,3},{3,4},{4,5},{5,6},{6,7},{7,8},{8,9},{9,10},{10,1... | collective-permute-start | bytes 2555912 | tf_op jit(solution)/shard_map/ppermute | solution.py:479
  21.9 1.9 %collective-permute-start.1 = (f32[4,416,128]{2,1,0:T(8,128)}, f32[4,416,128]{2,1,0:T(8,128)S(1)}, u32[]{:S(2)}, u32[]{:S(2)}) collective-permute-start(f32[4,416,128]{2,1,0:T(8,128)} %get-tuple-element.44), channel_id=1, source_target_pairs={{1,0},{2,1},{3,2},{4,3},{5,4},{6,5},{7,6},{8,7},{9,8},{10,9},{11,1... | collective-permute-start | bytes 2555912 | tf_op jit(solution)/shard_map/ppermute | solution.py:482
  23.8 0.1 copy.39
  23.9 0.0 copy-start.14
  23.9 0.0 copy-start.15
  23.9 2.5 %shard_map.66 = (f32[4,2,136,256]{3,2,1,0:T(8,128)}, f32[4,2,136,256]{3,2,1,0:T(8,128)}) custom-call(bf16[4,2,135,135]{3,2,1,0:T(8,128)(2,1)S(1)} %bitcast.30, bf16[4,2,135,135]{3,2,1,0:T(8,128)(2,1)S(1)} %bitcast.37), custom_call_target="tpu_custom_call" | custom-call | flops 2000000000 | bytes 2000000 | tf_op jit(solution)/shard_map/pallas_call | solution.py:437
  26.5 0.2 copy_bitcast_fusion.3
  26.6 1.1 copy-done.7
  27.7 0.3 copy-done.8
  28.0 4.7 %shard_map.67 = (f32[2,3,136,256]{3,2,1,0:T(8,128)}, f32[3,2,3,136,256]{4,3,2,1,0:T(8,128)}) custom-call(bf16[4,2,135,135]{3,2,1,0:T(8,128)(2,1)S(1)} %bitcast.31, bf16[4,2,135,135]{3,2,1,0:T(8,128)(2,1)S(1)} %get-tuple-element.68.refs_1_, bf16[4,2,135,135]{3,2,1,0:T(8,128)(2,1)S(1)} %get-tuple-element.67.refs_2_, f32[4,2,136,256]{3,2,1,0:T(8,128)S(1)} %copy-done.8, ...), custom_call_target="tpu_custom_call" | custom-call | flops 4000000000 | bytes 4000000 | tf_op jit(solution)/shard_map/pallas_call | solution.py:437
  32.8 3.6 %collective-permute-done.1.refs_4_ = f32[4,416,128]{2,1,0:T(8,128)S(1)} collective-permute-done((f32[4,416,128]{2,1,0:T(8,128)}, f32[4,416,128]{2,1,0:T(8,128)S(1)}, u32[]{:S(2)}, u32[]{:S(2)}) %collective-permute-start.1) | collective-permute-done | bytes 852000 | tf_op jit(solution)/shard_map/ppermute | solution.py:482
  36.4 4.3 %shard_map.68 = (f32[2,2,136,256]{3,2,1,0:T(8,128)}, f32[3,2,2,136,256]{4,3,2,1,0:T(8,128)}) custom-call(bf16[4,2,135,135]{3,2,1,0:T(8,128)(2,1)S(1)} %bitcast.32, bf16[4,2,135,135]{3,2,1,0:T(8,128)(2,1)S(1)} %get-tuple-element.68.refs_1_, bf16[4,2,135,135]{3,2,1,0:T(8,128)(2,1)S(1)} %get-tuple-element.67.refs_2_, ...), custom_call_target="tpu_custom_call" | custom-call | flops 3000000000 | bytes 3000000 | tf_op jit(solution)/shard_map/pallas_call | solution.py:437
  40.7 2.6 %all-to-all-done.received = f32[8,288,128]{2,1,0:T(8,128)S(1)} async-done(((f32[8,288,128]{2,1,0:T(8,128)}), f32[8,288,128]{2,1,0:T(8,128)S(1)}, u32[]{:S(2)}, u32[]{:S(2)}) %all-to-all-start) | async-done | bytes 1179680 | tf_op jit(solution)/shard_map/all_to_all | solution.py:476
  43.3 1.8 %shard_map.69 = (f32[8,72,128]{2,1,0:T(8,128)S(1)}, f32[4,216,128]{2,1,0:T(8,128)}) custom-call(f32[8,288,128]{2,1,0:T(8,128)S(1)} %all-to-all-done.received), custom_call_target="tpu_custom_call" | custom-call | flops 1500000000 | bytes 1500000 | tf_op jit(solution)/shard_map/pallas_call | solution.py:437
  45.0 5.8 %all-to-all-start.1 = ((f32[4,216,128]{2,1,0:T(8,128)}), f32[4,216,128]{2,1,0:T(8,128)S(1)}, u32[]{:S(2)}, u32[]{:S(2)}) async-start(f32[4,216,128]{2,1,0:T(8,128)} %get-tuple-element.49), calls=%async_computation.1 | async-start | bytes 884736 | tf_op jit(solution)/shard_map/all_to_all | solution.py:476
  50.8 1.9 %collective-permute-start.2 = (f32[8,72,128]{2,1,0:T(8,128)S(1)}, f32[8,72,128]{2,1,0:T(8,128)S(1)}, u32[]{:S(2)}, u32[]{:S(2)}) collective-permute-start(f32[8,72,128]{2,1,0:T(8,128)S(1)} %get-tuple-element.48.own), channel_id=1, source_target_pairs={{0,16},{16,0},{32,48},{48,32},{64,80},{80,64},{96,112},{112,96},{1... | collective-permute-start | bytes 884744 | tf_op jit(solution)/shard_map/ppermute | solution.py:545
  52.8 1.5 %shard_map.70.states = f32[7,136,256]{2,1,0:T(8,128)S(1)} custom-call(f32[8,288,128]{2,1,0:T(8,128)S(1)} %all-to-all-done.received), custom_call_target="tpu_custom_call" | custom-call | flops 2000000000 | bytes 2000000 | tf_op jit(solution)/shard_map/pallas_call | solution.py:437
  54.3 6.2 %collective-permute-done.2.other = f32[8,72,128]{2,1,0:T(8,128)S(1)} collective-permute-done((f32[8,72,128]{2,1,0:T(8,128)S(1)}, f32[8,72,128]{2,1,0:T(8,128)S(1)}, u32[]{:S(2)}, u32[]{:S(2)}) %collective-permute-start.2) | collective-permute-done | bytes 294944 | tf_op jit(solution)/shard_map/ppermute | solution.py:545
  60.5 1.3 shard_map.71
  61.8 14.7 %all_to_all.30.received.refs_0_ = f32[8,72,128]{2,1,0:T(8,128)S(1)} all-to-all(f32[8,72,128]{2,1,0:T(8,128)S(1)} %get-tuple-element.51), channel_id=1, replica_groups={{0,16,32,48,64,80,96,112},{128,144,160,176,192,208,224,240},{256,272,28..., dimensions={0} | all-to-all | bytes 589824 | tf_op jit(solution)/shard_map/all_to_all | solution.py:476
  76.5 6.4 %collective-permute-start.3 = (f32[4,72,128]{2,1,0:T(8,128)S(1)}, f32[4,72,128]{2,1,0:T(8,128)S(1)}, u32[]{:S(2)}, u32[]{:S(2)}) collective-permute-start(f32[4,72,128]{2,1,0:T(8,128)S(1)} %get-tuple-element.64), channel_id=1, source_target_pairs={{0,1},{1,2},{2,3},{3,4},{4,5},{5,6},{6,7},{7,8},{8,9},{9,10},{10,1... | collective-permute-start | bytes 442376 | tf_op jit(solution)/shard_map/ppermute | solution.py:479
  83.0 1.9 %collective-permute-start.4 = (f32[4,72,128]{2,1,0:T(8,128)S(1)}, f32[4,72,128]{2,1,0:T(8,128)S(1)}, u32[]{:S(2)}, u32[]{:S(2)}) collective-permute-start(f32[4,72,128]{2,1,0:T(8,128)S(1)} %get-tuple-element.63), channel_id=1, source_target_pairs={{1,0},{2,1},{3,2},{4,3},{5,4},{6,5},{7,6},{8,7},{9,8},{10,9},{11,1... | collective-permute-start | bytes 442376 | tf_op jit(solution)/shard_map/ppermute | solution.py:482
  84.9 0.6 shard_map.72.part
  85.5 3.9 %collective-permute-done.4.above.refs_2_ = f32[4,72,128]{2,1,0:T(8,128)S(1)} collective-permute-done((f32[4,72,128]{2,1,0:T(8,128)S(1)}, f32[4,72,128]{2,1,0:T(8,128)S(1)}, u32[]{:S(2)}, u32[]{:S(2)}) %collective-permute-start.4) | collective-permute-done | bytes 147488 | tf_op jit(solution)/shard_map/ppermute | solution.py:482
  89.4 0.6 shard_map.73
  90.0 12.5 %all_to_all.31.blocks = f32[8,72,128]{2,1,0:T(8,128)S(1)} all-to-all(f32[8,72,128]{2,1,0:T(8,128)S(1)} %get-tuple-element.54), channel_id=1, replica_groups={{0,16,32,48,64,80,96,112},{128,144,160,176,192,208,224,240},{256,272,28..., dimensions={0} | all-to-all | bytes 589824 | tf_op jit(solution)/shard_map/all_to_all | solution.py:476
  102.5 1.8 %shard_map.74 = f32[4,216,128]{2,1,0:T(8,128)} custom-call(f32[8,144,128]{2,1,0:T(8,128)S(1)} %copy-done.2, f32[8,72,128]{2,1,0:T(8,128)S(1)} %all_to_all.31.blocks), custom_call_target="tpu_custom_call" | custom-call | flops 1500000000 | bytes 1500000 | tf_op jit(solution)/shard_map/pallas_call | solution.py:437
  104.3 4.0 %all-to-all-start.4 = ((f32[4,216,128]{2,1,0:T(8,128)}), f32[4,216,128]{2,1,0:T(8,128)S(1)}, u32[]{:S(2)}, u32[]{:S(2)}) async-start(f32[4,216,128]{2,1,0:T(8,128)} %shard_map.74), calls=%async_computation.4 | async-start | bytes 884736 | tf_op jit(solution)/shard_map/all_to_all | solution.py:476
  108.3 1.5 %shard_map.76.states = f32[7,136,256]{2,1,0:T(8,128)S(1)} custom-call(f32[8,144,128]{2,1,0:T(8,128)S(1)} %copy-done.2, f32[8,72,128]{2,1,0:T(8,128)S(1)} %all_to_all.31.blocks), custom_call_target="tpu_custom_call" | custom-call | flops 2500000000 | bytes 2500000 | tf_op jit(solution)/shard_map/pallas_call | solution.py:437
  109.8 0.2 copy-done.3
  110.0 0.5 copy-done.6
  110.5 2.3 %shard_map.75.rest = f32[3,2,136,256]{3,2,1,0:T(8,128)} custom-call(f32[8,72,128]{2,1,0:T(8,128)S(1)} %all_to_all.30.received.refs_0_, f32[4,72,128]{2,1,0:T(8,128)S(1)} %collective-permute-done.3.below.refs_1_, f32[4,72,128]{2,1,0:T(8,128)S(1)} %collective-permute-done.4.above.refs_2_, f32[3,2,3,136,256]{4,3,2,1,0:T(8,128)S(1)} %copy-done.3, ...), custom_call_target="tpu_custom_call" | custom-call | flops 3000000000 | bytes 3000000 | tf_op jit(solution)/shard_map/pallas_call | solution.py:437
  112.7 2.9 %all-to-all-done.4.received = f32[4,216,128]{2,1,0:T(8,128)S(1)} async-done(((f32[4,216,128]{2,1,0:T(8,128)}), f32[4,216,128]{2,1,0:T(8,128)S(1)}, u32[]{:S(2)}, u32[]{:S(2)}) %all-to-all-start.4) | async-done | bytes 442400 | tf_op jit(solution)/shard_map/all_to_all | solution.py:476
  115.7 1.1 shard_map.77
  116.8 15.5 %all_to_all.32.received = f32[8,72,128]{2,1,0:T(8,128)S(1)} all-to-all(f32[8,72,128]{2,1,0:T(8,128)S(1)} %shard_map.77), channel_id=1, replica_groups={{0,16,32,48,64,80,96,112},{128,144,160,176,192,208,224,240},{256,272,28..., dimensions={0} | all-to-all | bytes 589824 | tf_op jit(solution)/shard_map/all_to_all | solution.py:476
  132.3 1.6 %shard_map.78 = f32[2160,128]{1,0:T(8,128)} custom-call(f32[8,72,128]{2,1,0:T(8,128)S(1)} %all_to_all.32.received, f32[4,2,136,256]{3,2,1,0:T(8,128)S(1)} %copy-done.4, f32[2,136,256]{2,1,0:T(8,128)S(1)} %get-tuple-element.61.first, f32[3,2,136,256]{3,2,1,0:T(8,128)S(1)} %copy-done.5), custom_call_target="tpu_custom_call" | custom-call | flops 2000000000 | bytes 2000000 | tf_op jit(solution)/shard_map/pallas_call | solution.py:437
  (27 shorter events, 0.1 us)
Async XLA Ops:
  0.0 1.3 copy-start.12
  0.0 1.4 %copy-start.13 = (bf16[4,2,1,135,135]{4,1,3,2,0:T(2,128)(2,1)S(1)}, bf16[4,2,1,135,135]{4,1,3,2,0:T(2,128)(2,1)}, u32[]{:S(2)}) copy-start(bf16[4,2,1,135,135]{4,1,3,2,0:T(2,128)(2,1)} %param.9) | copy-start | bytes 874804
  0.0 1.5 %copy-start.11 = (bf16[4,2,1,135,135]{4,1,3,2,0:T(2,128)(2,1)S(1)}, bf16[4,2,1,135,135]{4,1,3,2,0:T(2,128)(2,1)}, u32[]{:S(2)}) copy-start(bf16[4,2,1,135,135]{4,1,3,2,0:T(2,128)(2,1)} %param.8) | copy-start | bytes 874804
  5.2 7.8 %copy-start.10 = (bf16[4,2,1,135,135]{4,1,3,2,0:T(2,128)(2,1)S(1)}, bf16[4,2,1,135,135]{4,1,3,2,0:T(2,128)(2,1)}, u32[]{:S(2)}) copy-start(bf16[4,2,1,135,135]{4,1,3,2,0:T(2,128)(2,1)} %param.7) | copy-start | bytes 874804
  5.2 38.1 %all-to-all-start = ((f32[8,288,128]{2,1,0:T(8,128)}), f32[8,288,128]{2,1,0:T(8,128)S(1)}, u32[]{:S(2)}, u32[]{:S(2)}) async-start(f32[8,288,128]{2,1,0:T(8,128)} %shard_map.64), calls=%async_computation | async-start | bytes 2359296 | tf_op jit(solution)/shard_map/all_to_all | solution.py:476
  17.0 15.7 %collective-permute-start = (f32[4,416,128]{2,1,0:T(8,128)}, f32[4,416,128]{2,1,0:T(8,128)S(1)}, u32[]{:S(2)}, u32[]{:S(2)}) collective-permute-start(f32[4,416,128]{2,1,0:T(8,128)} %get-tuple-element.43), channel_id=1, source_target_pairs={{0,1},{1,2},{2,3},{3,4},{4,5},{5,6},{6,7},{7,8},{8,9},{9,10},{10,1... | collective-permute-start | bytes 2555912 | tf_op jit(solution)/shard_map/ppermute | solution.py:479
  21.9 14.5 %collective-permute-start.1 = (f32[4,416,128]{2,1,0:T(8,128)}, f32[4,416,128]{2,1,0:T(8,128)S(1)}, u32[]{:S(2)}, u32[]{:S(2)}) collective-permute-start(f32[4,416,128]{2,1,0:T(8,128)} %get-tuple-element.44), channel_id=1, source_target_pairs={{1,0},{2,1},{3,2},{4,3},{5,4},{6,5},{7,6},{8,7},{9,8},{10,9},{11,1... | collective-permute-start | bytes 2555912 | tf_op jit(solution)/shard_map/ppermute | solution.py:482
  23.9 2.5 %copy-start.14 = (bf16[4,2,1,135,135]{4,1,3,2,0:T(2,128)(2,1)S(1)}, bf16[4,2,1,135,135]{4,1,3,2,0:T(2,128)(2,1)}, u32[]{:S(2)}) copy-start(bf16[4,2,1,135,135]{4,1,3,2,0:T(2,128)(2,1)} %param.11) | copy-start | bytes 874804
  23.9 2.5 %copy-start.15 = (bf16[4,2,1,135,135]{4,1,3,2,0:T(2,128)(2,1)S(1)}, bf16[4,2,1,135,135]{4,1,3,2,0:T(2,128)(2,1)}, u32[]{:S(2)}) copy-start(bf16[4,2,1,135,135]{4,1,3,2,0:T(2,128)(2,1)} %param.10) | copy-start | bytes 874804
  23.9 2.7 %copy-start.9 = (f32[4,2,136,256]{3,2,1,0:T(8,128)S(1)}, f32[4,2,136,256]{3,2,1,0:T(8,128)}, u32[]{:S(2)}) copy-start(f32[4,2,136,256]{3,2,1,0:T(8,128)} %get-tuple-element.38.refs_4_) | copy-start | bytes 3342340
  26.4 1.2 copy-start.7
  26.5 1.6 %copy-start.8 = (f32[4,2,136,256]{3,2,1,0:T(8,128)S(1)}, f32[4,2,136,256]{3,2,1,0:T(8,128)}, u32[]{:S(2)}) copy-start(f32[4,2,136,256]{3,2,1,0:T(8,128)} %get-tuple-element.37.refs_3_) | copy-start | bytes 3342340
  45.0 15.4 %all-to-all-start.1 = ((f32[4,216,128]{2,1,0:T(8,128)}), f32[4,216,128]{2,1,0:T(8,128)S(1)}, u32[]{:S(2)}, u32[]{:S(2)}) async-start(f32[4,216,128]{2,1,0:T(8,128)} %get-tuple-element.49), calls=%async_computation.1 | async-start | bytes 884736 | tf_op jit(solution)/shard_map/all_to_all | solution.py:476
  50.8 9.6 %collective-permute-start.2 = (f32[8,72,128]{2,1,0:T(8,128)S(1)}, f32[8,72,128]{2,1,0:T(8,128)S(1)}, u32[]{:S(2)}, u32[]{:S(2)}) collective-permute-start(f32[8,72,128]{2,1,0:T(8,128)S(1)} %get-tuple-element.48.own), channel_id=1, source_target_pairs={{0,16},{16,0},{32,48},{48,32},{64,80},{80,64},{96,112},{112,96},{1... | collective-permute-start | bytes 884744 | tf_op jit(solution)/shard_map/ppermute | solution.py:545
  60.5 24.4 %copy-start.1 = (f32[2,2,136,256]{3,2,1,0:T(8,128)S(1)}, f32[2,2,136,256]{3,2,1,0:T(8,128)}, u32[]{:S(2)}) copy-start(f32[2,2,136,256]{3,2,1,0:T(8,128)} %get-tuple-element.52.far_plan.plan) | copy-start | bytes 1671172
  61.8 23.1 %copy-start = (f32[2,3,136,256]{3,2,1,0:T(8,128)S(1)}, f32[2,3,136,256]{3,2,1,0:T(8,128)}, u32[]{:S(2)}) copy-start(f32[2,3,136,256]{3,2,1,0:T(8,128)} %get-tuple-element.53.plan) | copy-start | bytes 2506756
  76.5 9.0 %collective-permute-start.3 = (f32[4,72,128]{2,1,0:T(8,128)S(1)}, f32[4,72,128]{2,1,0:T(8,128)S(1)}, u32[]{:S(2)}, u32[]{:S(2)}) collective-permute-start(f32[4,72,128]{2,1,0:T(8,128)S(1)} %get-tuple-element.64), channel_id=1, source_target_pairs={{0,1},{1,2},{2,3},{3,4},{4,5},{5,6},{6,7},{7,8},{8,9},{9,10},{10,1... | collective-permute-start | bytes 442376 | tf_op jit(solution)/shard_map/ppermute | solution.py:479
  83.0 6.5 %collective-permute-start.4 = (f32[4,72,128]{2,1,0:T(8,128)S(1)}, f32[4,72,128]{2,1,0:T(8,128)S(1)}, u32[]{:S(2)}, u32[]{:S(2)}) collective-permute-start(f32[4,72,128]{2,1,0:T(8,128)S(1)} %get-tuple-element.63), channel_id=1, source_target_pairs={{1,0},{2,1},{3,2},{4,3},{5,4},{6,5},{7,6},{8,7},{9,8},{10,9},{11,1... | collective-permute-start | bytes 442376 | tf_op jit(solution)/shard_map/ppermute | solution.py:482
  85.5 17.0 %copy-start.2 = (f32[8,144,128]{2,1,0:T(8,128)S(1)}, f32[8,144,128]{2,1,0:T(8,128)}, u32[]{:S(2)}) copy-start(f32[8,144,128]{2,1,0:T(8,128)} %get-tuple-element.50.matrices) | copy-start | bytes 1769476
  104.3 11.4 %all-to-all-start.4 = ((f32[4,216,128]{2,1,0:T(8,128)}), f32[4,216,128]{2,1,0:T(8,128)S(1)}, u32[]{:S(2)}, u32[]{:S(2)}) async-start(f32[4,216,128]{2,1,0:T(8,128)} %shard_map.74), calls=%async_computation.4 | async-start | bytes 884736 | tf_op jit(solution)/shard_map/all_to_all | solution.py:476
  108.3 1.7 %copy-start.3 = (f32[3,2,3,136,256]{4,3,2,1,0:T(8,128)S(1)}, f32[3,2,3,136,256]{4,3,2,1,0:T(8,128)}, u32[]{:S(2)}) copy-start(f32[3,2,3,136,256]{4,3,2,1,0:T(8,128)} %get-tuple-element.57.refs_3_) | copy-start | bytes 7520260
  108.3 2.2 %copy-start.6 = (f32[3,2,2,136,256]{4,3,2,1,0:T(8,128)S(1)}, f32[3,2,2,136,256]{4,3,2,1,0:T(8,128)}, u32[]{:S(2)}) copy-start(f32[3,2,2,136,256]{4,3,2,1,0:T(8,128)} %get-tuple-element.58.refs_4_) | copy-start | bytes 5013508
  112.7 19.5 %copy-start.5 = (f32[3,2,136,256]{3,2,1,0:T(8,128)S(1)}, f32[3,2,136,256]{3,2,1,0:T(8,128)}, u32[]{:S(2)}) copy-start(f32[3,2,136,256]{3,2,1,0:T(8,128)} %shard_map.75.rest) | copy-start | bytes 2506756
  115.7 16.6 %copy-start.4 = (f32[4,2,136,256]{3,2,1,0:T(8,128)S(1)}, f32[4,2,136,256]{3,2,1,0:T(8,128)}, u32[]{:S(2)}) copy-start(f32[4,2,136,256]{3,2,1,0:T(8,128)} %get-tuple-element.60.maps) | copy-start | bytes 3342340

commit v6 on v5

--- a/solution.py
+++ b/solution.py
@@ -129,7 +129,7 @@
     return -(-(full + 8) // (8 * PIECES)) * 8
 
 
-def start(inverse, before, after, source, sent, maps, values, sems):
+def start(turn, inverse, before, after, source, sent, maps, values, sems):
     positions, columns, unknowns, vectors = source.shape
     full = values.shape[-2]
     room = full + 8
@@ -138,7 +138,7 @@
     copies = []
 
     def send(ref, at, low):
-        there = sent.at[at, pl.ds(low, ref.shape[0])]
+        there = sent.at[(turn[0] + at) % ROW, pl.ds(low, ref.shape[0])]
         copies.append(pltpu.make_async_copy(ref, there, sems.at[len(copies)]))
         copies[-1].start()
 
@@ -281,13 +281,16 @@
         sent[at] = pack_slice(every[k * full : (k + 1) * full], 0)
 
 
-def unpack_columns(full, received, first, count):
+def unpack_columns(full, received, first, count, turn=None):
+    def block(at):
+        return received[at if turn is None else (turn[0] + at) % ROW]
+
     parts = []
     for h in range(count // 2):
         at = first + 2 * h
         parts.append(
-            unpack_slice(received[at], full, 0)
-            + pltpu.roll(unpack_slice(received[at + 1], full, 0), 64, 1)
+            unpack_slice(block(at), full, 0)
+            + pltpu.roll(unpack_slice(block(at + 1), full, 0), 64, 1)
         )
     return jnp.concatenate(parts, axis=1)
 
@@ -342,10 +345,17 @@
                 put(*((plan, (c, k)) if s == 0 else (more, (s - 1, c, k))), value)
 
 
-def near_part(received, plan, far_plan, part):
+def by_column(turn, received, *outs):
+    for c, out in enumerate(outs):
+        peers = out.shape[0]
+        for q in range(peers):
+            out[q] = received[(turn[0] + c * peers + q) % ROW]
+
+
+def near_part(turn, received, plan, far_plan, part):
     columns, full, _ = part.shape
     peers = ROW // columns
-    entering = [unpack_columns(full, received, c * peers, peers) for c in range(columns)]
+    entering = [unpack_columns(full, received, c * peers, peers, turn) for c in range(columns)]
     for c in range(columns):
         part[c] = (plan[c, 2] + far_plan[c, 1]) + (
             float_by_float(plan[c, 0, :, :full], entering[c])
@@ -353,7 +363,7 @@
         )
 
 
-def far_part(below, above, plan, part, sent, values):
+def far_part(turn, below, above, plan, part, sent, values):
     columns, full, _ = part.shape
     peers = ROW // columns
     halo = (below, above)
@@ -363,13 +373,13 @@
         values[c] = value
         for q in range(peers):
             pair = value[:, q // 2 * LANES : (q // 2 + 1) * LANES]
-            sent[c * peers + q] = pack_slice(pair, q % 2)
-
-
-def levels(received, below, above, more, far_more, values):
+            sent[(turn[0] + c * peers + q) % ROW] = pack_slice(pair, q % 2)
+
+
+def levels(turn, received, below, above, more, far_more, values):
     others, columns, full, _ = values.shape
     peers = ROW // columns
-    entering = [unpack_columns(full, received, c * peers, peers) for c in range(columns)]
+    entering = [unpack_columns(full, received, c * peers, peers, turn) for c in range(columns)]
     halo = [unpack_columns(full, got, 0, peers) for got in (below, above)]
     for c in range(columns):
         total = None
@@ -386,12 +396,12 @@
             values[s, c] = value + total[s * full : (s + 1) * full]
 
 
-def finish(received, maps, first, rest, result, out, sems):
+def finish(turn, received, maps, first, rest, result, out, sems):
     positions, columns, full, vectors = maps.shape
     peers = ROW // columns
     total = result.shape[0]
     unknowns = total // (2 * positions * columns)
-    entering = [unpack_columns(full, received, c * peers, peers) for c in range(columns)]
+    entering = [unpack_columns(full, received, c * peers, peers, turn) for c in range(columns)]
     copies = []
     for part in range(2):
         levels = range(part * positions // 2, (part + 1) * positions // 2)
@@ -461,7 +471,8 @@
     fold = (full // 8 + 1) // 2 * 8
     peers = ROW // columns
     piece = piece_rows(full)
-    place = (lax.axis_index("sweep") % ROW).astype(jnp.int32).reshape(1)
+    turn = (lax.axis_index("cross") % 2).astype(jnp.int32).reshape(1)
+    place = (lax.axis_index("sweep").astype(jnp.int32).reshape(1) + ROW - turn) % ROW
     count = lax.axis_size("sweep")
     rows = count // ROW
     inside = [[r * ROW + i for i in range(ROW)] for r in range(rows)]
@@ -484,11 +495,13 @@
     (sent,) = call(
         start,
         [(ROW, room + piece + fold, LANES)],
+        turn,
         inverse,
         before,
         after,
         source,
         us=4,
+        smem=(0,),
         direct=1,
         scratch=[
             pltpu.VMEM((columns, 2, room, LANES), F32),
@@ -542,7 +555,16 @@
     )
 
     joined = exchange(sent, across)
-    other = lax.ppermute(own, "sweep", [(i, i ^ 1) for i in range(count)])
+    wide = ends + 1
+    other = lax.ppermute(
+        own,
+        ("sweep", "cross"),
+        [
+            (i * wide + c, (i // ROW * ROW + (((i - c % 2) % ROW ^ 1) + c % 2) % ROW) * wide + c)
+            for i in range(count)
+            for c in range(wide)
+        ],
+    )
     (states,) = call(
         functools.partial(fore_prefixes, full),
         [(ROW - 1, full, 2 * LANES)],
@@ -564,20 +586,39 @@
         scratch=[pltpu.SemaphoreType.DMA((PIECES,))],
     )
     entering = exchange(sent, inside)
-    below, above = from_below(entering[peers:]), from_above(entering[:peers])
-    (part,) = call(near_part, [(columns, full, vectors)], entering, plan, far_plan, us=0.6)
+    lower_column, upper_column = call(
+        by_column, [(peers, fold, LANES)] * columns, turn, entering, us=0.1, smem=(0,)
+    )
+    below, above = from_below(upper_column), from_above(lower_column)
+    (part,) = call(
+        near_part, [(columns, full, vectors)], turn, entering, plan, far_plan, us=0.6, smem=(0,)
+    )
     sent, first = call(
         far_part,
         [(ROW, fold, LANES), (columns, full, vectors)],
+        turn,
         below,
         above,
         far_plan,
         part,
         us=0.6,
+        smem=(0,),
     )
     received = exchange(sent, inside)
     received, more = lax.optimization_barrier((received, more))
-    (values,) = call(levels, [others], entering, below, above, more, far_more, us=3, kept=1)
+    (values,) = call(
+        levels,
+        [others],
+        turn,
+        entering,
+        below,
+        above,
+        more,
+        far_more,
+        us=3,
+        smem=(0,),
+        kept=1,
+    )
     order = range(ROW - 1, -1, -1)
     (sent,) = call(
         functools.partial(whole_run, full, order),
@@ -609,11 +650,13 @@
     (update,) = call(
         finish,
         [(lines, LANES)],
+        turn,
         entering,
         back_maps,
         first,
         values,
         us=2,
+        smem=(0,),
         direct=1,
         scratch=[pltpu.VMEM((lines + 16, LANES), F32), pltpu.SemaphoreType.DMA((2,))],
     )

time: 136 us -> 134 us (0.985)
    pallas_call x15 -> x16, Pallas kernels: 32.6 us -> 32.8 us  [call(): pl.pallas_call(with_copies if kept else kernel, out_shape=[jax.ShapeDtype...]
where the time goes in v6:
time: 134 us; the launch traced here: 132 us
  blocking collectives  41.9 us (31%)
  starting transfers between devices  34.2 us (26%)
  Pallas kernels  32.8 us (24%)
  waiting for transfers between devices  18.5 us (14%)
  local copies, waits for them, and re-layouts  4.31 us (3%)
    all_to_all x3, blocking collectives, exchange(): return lax.all_to_all(x, 'sweep', 0, 0, axis_index_groups=groups)  41.9 us
    pallas_call x16, Pallas kernels, call(): pl.pallas_call(with_copies if kept else kernel, out_shape=[jax.ShapeDtype...  32.8 us
    all_to_all x3, starting transfers between devices, exchange(): return lax.all_to_all(x, 'sweep', 0, 0, axis_index_groups=groups)  17.4 us
    ppermute x2, starting transfers between devices, from_below(): return lax.ppermute(x, 'cross', [(i, i + 1) for i in range(ends)])  11 us
    ppermute x2, waiting for transfers between devices, from_above(): return lax.ppermute(x, 'cross', [(i + 1, i) for i in range(ends)])  7.54 us
    ppermute x1, waiting for transfers between devices, shards(): lax.ppermute(own, ('sweep', 'cross'), [(i * wide + c, (i // ROW * ROW + (...  5.53 us
    all_to_all x3, waiting for transfers between devices, exchange(): return lax.all_to_all(x, 'sweep', 0, 0, axis_index_groups=groups)  5.42 us
    ppermute x2, starting transfers between devices, from_above(): return lax.ppermute(x, 'cross', [(i + 1, i) for i in range(ends)])  3.84 us
  transfers between devices with their start and end apart: 8, of which 5 were waited for; matrix products, arithmetic and copies ran while one was open for 0% of the time, Pallas kernels for 16%

profile of v6, /device:TPU:1, one launch (start us, length us, event | category | flops | bytes accessed | tf_op | source)
XLA Modules:
  0.0 132.2 jit_solution(6484111298622317523)
XLA Ops:
  0.0 1.3 copy.44
  1.3 0.1 copy.43
  1.4 0.0 copy-done.11
  1.4 0.2 copy-done.13
  1.6 0.2 copy_bitcast_fusion.7
  1.7 3.5 %shard_map.64 = f32[8,288,128]{2,1,0:T(8,128)} custom-call(s32[1]{0:T(128)} %bitcast.turn.refs_0_, bf16[4,2,135,135]{3,2,1,0:T(8,128)(2,1)S(1)} %bitcast.34, bf16[4,2,135,135]{3,2,1,0:T(8,128)(2,1)S(1)} %get-tuple-element.68.before, bf16[4,2,135,135]{3,2,1,0:T(8,128)(2,1)S(1)} %get-tuple-element.67.after, bf16[4,2,135,256]{3,2,1,0:T(8,128)(2,1)S(1)} %bitcast.35), custom_call_target="tpu_custom_call" | custom-call | flops 4000000000 | bytes 4000000 | tf_op jit(solution)/shard_map/pallas_call | solution.py:447
  5.2 0.0 copy-start.10
  5.2 7.8 %all-to-all-start = ((f32[8,288,128]{2,1,0:T(8,128)}), f32[8,288,128]{2,1,0:T(8,128)S(1)}, u32[]{:S(2)}, u32[]{:S(2)}) async-start(f32[8,288,128]{2,1,0:T(8,128)} %shard_map.64), calls=%async_computation | async-start | bytes 2359296 | tf_op jit(solution)/shard_map/all_to_all | solution.py:487
  13.0 0.1 copy.42
  13.1 0.1 copy.41
  13.2 0.1 copy.40
  13.3 3.8 %shard_map.65 = (f32[4,416,128]{2,1,0:T(8,128)}, f32[4,416,128]{2,1,0:T(8,128)}, f32[4,2,136,256]{3,2,1,0:T(8,128)}, f32[4,2,136,256]{3,2,1,0:T(8,128)}) custom-call(bf16[4,2,135,135]{3,2,1,0:T(8,128)(2,1)S(1)} %bitcast.30, bf16[4,2,135,135]{3,2,1,0:T(8,128)(2,1)S(1)} %bitcast.36, bf16[4,2,135,256]{3,2,1,0:T(8,128)(2,1)S(1)} %bitcast.37), custom_call_target="tpu_custom_call" | custom-call | flops 3000000000 | bytes 3000000 | tf_op jit(solution)/shard_map/pallas_call | solution.py:447
  17.1 4.9 %collective-permute-start = (f32[4,416,128]{2,1,0:T(8,128)}, f32[4,416,128]{2,1,0:T(8,128)S(1)}, u32[]{:S(2)}, u32[]{:S(2)}) collective-permute-start(f32[4,416,128]{2,1,0:T(8,128)} %get-tuple-element.45), channel_id=1, source_target_pairs={{0,1},{1,2},{2,3},{3,4},{4,5},{5,6},{6,7},{7,8},{8,9},{9,10},{10,1... | collective-permute-start | bytes 2555912 | tf_op jit(solution)/shard_map/ppermute | solution.py:490
  21.9 1.9 %collective-permute-start.1 = (f32[4,416,128]{2,1,0:T(8,128)}, f32[4,416,128]{2,1,0:T(8,128)S(1)}, u32[]{:S(2)}, u32[]{:S(2)}) collective-permute-start(f32[4,416,128]{2,1,0:T(8,128)} %get-tuple-element.46), channel_id=1, source_target_pairs={{1,0},{2,1},{3,2},{4,3},{5,4},{6,5},{7,6},{8,7},{9,8},{10,9},{11,1... | collective-permute-start | bytes 2555912 | tf_op jit(solution)/shard_map/ppermute | solution.py:493
  23.8 0.1 copy.39
  23.9 0.0 copy-start.14
  24.0 2.5 %shard_map.66 = (f32[4,2,136,256]{3,2,1,0:T(8,128)}, f32[4,2,136,256]{3,2,1,0:T(8,128)}) custom-call(bf16[4,2,135,135]{3,2,1,0:T(8,128)(2,1)S(1)} %bitcast.31, bf16[4,2,135,135]{3,2,1,0:T(8,128)(2,1)S(1)} %bitcast.38), custom_call_target="tpu_custom_call" | custom-call | flops 2000000000 | bytes 2000000 | tf_op jit(solution)/shard_map/pallas_call | solution.py:447
  26.5 0.2 copy_bitcast_fusion.3
  26.7 1.1 copy-done.7
  27.7 0.3 copy-done.8
  28.1 4.7 %shard_map.67 = (f32[2,3,136,256]{3,2,1,0:T(8,128)}, f32[3,2,3,136,256]{4,3,2,1,0:T(8,128)}) custom-call(bf16[4,2,135,135]{3,2,1,0:T(8,128)(2,1)S(1)} %bitcast.32, bf16[4,2,135,135]{3,2,1,0:T(8,128)(2,1)S(1)} %get-tuple-element.70.refs_1_, bf16[4,2,135,135]{3,2,1,0:T(8,128)(2,1)S(1)} %get-tuple-element.69.refs_2_, f32[4,2,136,256]{3,2,1,0:T(8,128)S(1)} %copy-done.8, ...), custom_call_target="tpu_custom_call" | custom-call | flops 4000000000 | bytes 4000000 | tf_op jit(solution)/shard_map/pallas_call | solution.py:447
  32.8 3.6 %collective-permute-done.1.refs_4_ = f32[4,416,128]{2,1,0:T(8,128)S(1)} collective-permute-done((f32[4,416,128]{2,1,0:T(8,128)}, f32[4,416,128]{2,1,0:T(8,128)S(1)}, u32[]{:S(2)}, u32[]{:S(2)}) %collective-permute-start.1) | collective-permute-done | bytes 852000 | tf_op jit(solution)/shard_map/ppermute | solution.py:493
  36.4 4.3 %shard_map.68 = (f32[2,2,136,256]{3,2,1,0:T(8,128)}, f32[3,2,2,136,256]{4,3,2,1,0:T(8,128)}) custom-call(bf16[4,2,135,135]{3,2,1,0:T(8,128)(2,1)S(1)} %bitcast.33, bf16[4,2,135,135]{3,2,1,0:T(8,128)(2,1)S(1)} %get-tuple-element.70.refs_1_, bf16[4,2,135,135]{3,2,1,0:T(8,128)(2,1)S(1)} %get-tuple-element.69.refs_2_, ...), custom_call_target="tpu_custom_call" | custom-call | flops 3000000000 | bytes 3000000 | tf_op jit(solution)/shard_map/pallas_call | solution.py:447
  40.8 2.5 %all-to-all-done.received = f32[8,288,128]{2,1,0:T(8,128)S(1)} async-done(((f32[8,288,128]{2,1,0:T(8,128)}), f32[8,288,128]{2,1,0:T(8,128)S(1)}, u32[]{:S(2)}, u32[]{:S(2)}) %all-to-all-start) | async-done | bytes 1179680 | tf_op jit(solution)/shard_map/all_to_all | solution.py:487
  43.3 1.8 %shard_map.69 = (f32[8,72,128]{2,1,0:T(8,128)S(1)}, f32[4,216,128]{2,1,0:T(8,128)}) custom-call(f32[8,288,128]{2,1,0:T(8,128)S(1)} %all-to-all-done.received), custom_call_target="tpu_custom_call" | custom-call | flops 1500000000 | bytes 1500000 | tf_op jit(solution)/shard_map/pallas_call | solution.py:447
  45.1 5.8 %all-to-all-start.1 = ((f32[4,216,128]{2,1,0:T(8,128)}), f32[4,216,128]{2,1,0:T(8,128)S(1)}, u32[]{:S(2)}, u32[]{:S(2)}) async-start(f32[4,216,128]{2,1,0:T(8,128)} %get-tuple-element.51), calls=%async_computation.1 | async-start | bytes 884736 | tf_op jit(solution)/shard_map/all_to_all | solution.py:487
  50.9 1.9 %collective-permute-start.2 = (f32[8,72,128]{2,1,0:T(8,128)S(1)}, f32[8,72,128]{2,1,0:T(8,128)S(1)}, u32[]{:S(2)}, u32[]{:S(2)}) collective-permute-start(f32[8,72,128]{2,1,0:T(8,128)S(1)} %get-tuple-element.50.own), channel_id=1, source_target_pairs={{0,16},{1,113},{2,18},{3,115},{4,20},{5,117},{6,22},{7,119},{8,24}... | collective-permute-start | bytes 884744 | tf_op jit(solution)/shard_map/ppermute | solution.py:559
  52.8 1.5 %shard_map.70.states = f32[7,136,256]{2,1,0:T(8,128)S(1)} custom-call(f32[8,288,128]{2,1,0:T(8,128)S(1)} %all-to-all-done.received), custom_call_target="tpu_custom_call" | custom-call | flops 2000000000 | bytes 2000000 | tf_op jit(solution)/shard_map/pallas_call | solution.py:447
  54.3 5.5 %collective-permute-done.2.other = f32[8,72,128]{2,1,0:T(8,128)S(1)} collective-permute-done((f32[8,72,128]{2,1,0:T(8,128)S(1)}, f32[8,72,128]{2,1,0:T(8,128)S(1)}, u32[]{:S(2)}, u32[]{:S(2)}) %collective-permute-start.2) | collective-permute-done | bytes 294944 | tf_op jit(solution)/shard_map/ppermute | solution.py:559
  59.8 1.3 shard_map.71
  61.1 14.0 %all_to_all.30.received.refs_1_ = f32[8,72,128]{2,1,0:T(8,128)S(1)} all-to-all(f32[8,72,128]{2,1,0:T(8,128)S(1)} %get-tuple-element.53), channel_id=1, replica_groups={{0,16,32,48,64,80,96,112},{128,144,160,176,192,208,224,240},{256,272,28..., dimensions={0} | all-to-all | bytes 589824 | tf_op jit(solution)/shard_map/all_to_all | solution.py:487
  75.1 6.2 %collective-permute-start.3 = (f32[4,72,128]{2,1,0:T(8,128)S(1)}, f32[4,72,128]{2,1,0:T(8,128)S(1)}, u32[]{:S(2)}, u32[]{:S(2)}) collective-permute-start(f32[4,72,128]{2,1,0:T(8,128)S(1)} %get-tuple-element.54), channel_id=1, source_target_pairs={{0,1},{1,2},{2,3},{3,4},{4,5},{5,6},{6,7},{7,8},{8,9},{9,10},{10,1... | collective-permute-start | bytes 442376 | tf_op jit(solution)/shard_map/ppermute | solution.py:490
  81.3 1.9 %collective-permute-start.4 = (f32[4,72,128]{2,1,0:T(8,128)S(1)}, f32[4,72,128]{2,1,0:T(8,128)S(1)}, u32[]{:S(2)}, u32[]{:S(2)}) collective-permute-start(f32[4,72,128]{2,1,0:T(8,128)S(1)} %get-tuple-element.55), channel_id=1, source_target_pairs={{1,0},{2,1},{3,2},{4,3},{5,4},{6,5},{7,6},{8,7},{9,8},{10,9},{11,1... | collective-permute-start | bytes 442376 | tf_op jit(solution)/shard_map/ppermute | solution.py:493
  83.2 0.6 shard_map.73.part
  83.8 0.0 copy-start.2
  83.9 3.9 %collective-permute-done.4.above.refs_3_ = f32[4,72,128]{2,1,0:T(8,128)S(1)} collective-permute-done((f32[4,72,128]{2,1,0:T(8,128)S(1)}, f32[4,72,128]{2,1,0:T(8,128)S(1)}, u32[]{:S(2)}, u32[]{:S(2)}) %collective-permute-start.4) | collective-permute-done | bytes 147488 | tf_op jit(solution)/shard_map/ppermute | solution.py:493
  87.7 0.6 shard_map.74
  88.3 12.5 %all_to_all.31.blocks = f32[8,72,128]{2,1,0:T(8,128)S(1)} all-to-all(f32[8,72,128]{2,1,0:T(8,128)S(1)} %get-tuple-element.58), channel_id=1, replica_groups={{0,16,32,48,64,80,96,112},{128,144,160,176,192,208,224,240},{256,272,28..., dimensions={0} | all-to-all | bytes 589824 | tf_op jit(solution)/shard_map/all_to_all | solution.py:487
  100.8 1.8 %shard_map.75 = f32[4,216,128]{2,1,0:T(8,128)} custom-call(f32[8,144,128]{2,1,0:T(8,128)S(1)} %copy-done.2, f32[8,72,128]{2,1,0:T(8,128)S(1)} %all_to_all.31.blocks), custom_call_target="tpu_custom_call" | custom-call | flops 1500000000 | bytes 1500000 | tf_op jit(solution)/shard_map/pallas_call | solution.py:447
  102.6 3.9 %all-to-all-start.4 = ((f32[4,216,128]{2,1,0:T(8,128)}), f32[4,216,128]{2,1,0:T(8,128)S(1)}, u32[]{:S(2)}, u32[]{:S(2)}) async-start(f32[4,216,128]{2,1,0:T(8,128)} %shard_map.75), calls=%async_computation.4 | async-start | bytes 884736 | tf_op jit(solution)/shard_map/all_to_all | solution.py:487
  106.4 1.5 %shard_map.77.states = f32[7,136,256]{2,1,0:T(8,128)S(1)} custom-call(f32[8,144,128]{2,1,0:T(8,128)S(1)} %copy-done.2, f32[8,72,128]{2,1,0:T(8,128)S(1)} %all_to_all.31.blocks), custom_call_target="tpu_custom_call" | custom-call | flops 2500000000 | bytes 2500000 | tf_op jit(solution)/shard_map/pallas_call | solution.py:447
  107.9 0.2 copy-done.3
  108.1 0.5 copy-done.6
  108.6 2.3 %shard_map.76.rest = f32[3,2,136,256]{3,2,1,0:T(8,128)} custom-call(s32[1]{0:T(128)} %bitcast.turn.refs_0_, f32[8,72,128]{2,1,0:T(8,128)S(1)} %all_to_all.30.received.refs_1_, f32[4,72,128]{2,1,0:T(8,128)S(1)} %collective-permute-done.3.below.refs_2_, f32[4,72,128]{2,1,0:T(8,128)S(1)} %collective-permute-done.4.above.refs_3_, ...), custom_call_target="tpu_custom_call" | custom-call | flops 3000000000 | bytes 3000000 | tf_op jit(solution)/shard_map/pallas_call | solution.py:447
  110.9 2.9 %all-to-all-done.4.received = f32[4,216,128]{2,1,0:T(8,128)S(1)} async-done(((f32[4,216,128]{2,1,0:T(8,128)}), f32[4,216,128]{2,1,0:T(8,128)S(1)}, u32[]{:S(2)}, u32[]{:S(2)}) %all-to-all-start.4) | async-done | bytes 442400 | tf_op jit(solution)/shard_map/all_to_all | solution.py:487
  113.8 1.1 shard_map.78
  114.9 15.5 %all_to_all.32.received = f32[8,72,128]{2,1,0:T(8,128)S(1)} all-to-all(f32[8,72,128]{2,1,0:T(8,128)S(1)} %shard_map.78), channel_id=1, replica_groups={{0,16,32,48,64,80,96,112},{128,144,160,176,192,208,224,240},{256,272,28..., dimensions={0} | all-to-all | bytes 589824 | tf_op jit(solution)/shard_map/all_to_all | solution.py:487
  130.4 1.6 %shard_map.79 = f32[2160,128]{1,0:T(8,128)} custom-call(s32[1]{0:T(128)} %bitcast.turn.refs_0_, f32[8,72,128]{2,1,0:T(8,128)S(1)} %all_to_all.32.received, f32[4,2,136,256]{3,2,1,0:T(8,128)S(1)} %copy-done.4, f32[2,136,256]{2,1,0:T(8,128)S(1)} %get-tuple-element.65.first, f32[3,2,136,256]{3,2,1,0:T(8,128)S(1)} %copy-done.5), custom_call_target="tpu_custom_call" | custom-call | flops 2000000000 | bytes 2000000 | tf_op jit(solution)/shard_map/pallas_call | solution.py:447
  (27 shorter events, 0.1 us)
Async XLA Ops:
  0.0 1.3 copy-start.12
  0.0 1.4 %copy-start.11 = (bf16[4,2,1,135,135]{4,1,3,2,0:T(2,128)(2,1)S(1)}, bf16[4,2,1,135,135]{4,1,3,2,0:T(2,128)(2,1)}, u32[]{:S(2)}) copy-start(bf16[4,2,1,135,135]{4,1,3,2,0:T(2,128)(2,1)} %param.8) | copy-start | bytes 874804
  0.0 1.5 %copy-start.13 = (bf16[4,2,1,135,135]{4,1,3,2,0:T(2,128)(2,1)S(1)}, bf16[4,2,1,135,135]{4,1,3,2,0:T(2,128)(2,1)}, u32[]{:S(2)}) copy-start(bf16[4,2,1,135,135]{4,1,3,2,0:T(2,128)(2,1)} %param.9) | copy-start | bytes 874804
  5.2 7.8 %copy-start.10 = (bf16[4,2,1,135,135]{4,1,3,2,0:T(2,128)(2,1)S(1)}, bf16[4,2,1,135,135]{4,1,3,2,0:T(2,128)(2,1)}, u32[]{:S(2)}) copy-start(bf16[4,2,1,135,135]{4,1,3,2,0:T(2,128)(2,1)} %param.7) | copy-start | bytes 874804
  5.2 38.0 %all-to-all-start = ((f32[8,288,128]{2,1,0:T(8,128)}), f32[8,288,128]{2,1,0:T(8,128)S(1)}, u32[]{:S(2)}, u32[]{:S(2)}) async-start(f32[8,288,128]{2,1,0:T(8,128)} %shard_map.64), calls=%async_computation | async-start | bytes 2359296 | tf_op jit(solution)/shard_map/all_to_all | solution.py:487
  17.1 15.7 %collective-permute-start = (f32[4,416,128]{2,1,0:T(8,128)}, f32[4,416,128]{2,1,0:T(8,128)S(1)}, u32[]{:S(2)}, u32[]{:S(2)}) collective-permute-start(f32[4,416,128]{2,1,0:T(8,128)} %get-tuple-element.45), channel_id=1, source_target_pairs={{0,1},{1,2},{2,3},{3,4},{4,5},{5,6},{6,7},{7,8},{8,9},{9,10},{10,1... | collective-permute-start | bytes 2555912 | tf_op jit(solution)/shard_map/ppermute | solution.py:490
  21.9 14.5 %collective-permute-start.1 = (f32[4,416,128]{2,1,0:T(8,128)}, f32[4,416,128]{2,1,0:T(8,128)S(1)}, u32[]{:S(2)}, u32[]{:S(2)}) collective-permute-start(f32[4,416,128]{2,1,0:T(8,128)} %get-tuple-element.46), channel_id=1, source_target_pairs={{1,0},{2,1},{3,2},{4,3},{5,4},{6,5},{7,6},{8,7},{9,8},{10,9},{11,1... | collective-permute-start | bytes 2555912 | tf_op jit(solution)/shard_map/ppermute | solution.py:493
  23.9 2.6 %copy-start.14 = (bf16[4,2,1,135,135]{4,1,3,2,0:T(2,128)(2,1)S(1)}, bf16[4,2,1,135,135]{4,1,3,2,0:T(2,128)(2,1)}, u32[]{:S(2)}) copy-start(bf16[4,2,1,135,135]{4,1,3,2,0:T(2,128)(2,1)} %param.11) | copy-start | bytes 874804
  23.9 2.6 %copy-start.15 = (bf16[4,2,1,135,135]{4,1,3,2,0:T(2,128)(2,1)S(1)}, bf16[4,2,1,135,135]{4,1,3,2,0:T(2,128)(2,1)}, u32[]{:S(2)}) copy-start(bf16[4,2,1,135,135]{4,1,3,2,0:T(2,128)(2,1)} %param.10) | copy-start | bytes 874804
  23.9 2.7 %copy-start.9 = (f32[4,2,136,256]{3,2,1,0:T(8,128)S(1)}, f32[4,2,136,256]{3,2,1,0:T(8,128)}, u32[]{:S(2)}) copy-start(f32[4,2,136,256]{3,2,1,0:T(8,128)} %get-tuple-element.40.refs_4_) | copy-start | bytes 3342340
  26.5 1.2 copy-start.7
  26.5 1.6 %copy-start.8 = (f32[4,2,136,256]{3,2,1,0:T(8,128)S(1)}, f32[4,2,136,256]{3,2,1,0:T(8,128)}, u32[]{:S(2)}) copy-start(f32[4,2,136,256]{3,2,1,0:T(8,128)} %get-tuple-element.39.refs_3_) | copy-start | bytes 3342340
  45.1 14.8 %all-to-all-start.1 = ((f32[4,216,128]{2,1,0:T(8,128)}), f32[4,216,128]{2,1,0:T(8,128)S(1)}, u32[]{:S(2)}, u32[]{:S(2)}) async-start(f32[4,216,128]{2,1,0:T(8,128)} %get-tuple-element.51), calls=%async_computation.1 | async-start | bytes 884736 | tf_op jit(solution)/shard_map/all_to_all | solution.py:487
  50.9 9.0 %collective-permute-start.2 = (f32[8,72,128]{2,1,0:T(8,128)S(1)}, f32[8,72,128]{2,1,0:T(8,128)S(1)}, u32[]{:S(2)}, u32[]{:S(2)}) collective-permute-start(f32[8,72,128]{2,1,0:T(8,128)S(1)} %get-tuple-element.50.own), channel_id=1, source_target_pairs={{0,16},{1,113},{2,18},{3,115},{4,20},{5,117},{6,22},{7,119},{8,24}... | collective-permute-start | bytes 884744 | tf_op jit(solution)/shard_map/ppermute | solution.py:559
  59.8 23.4 %copy-start = (f32[2,3,136,256]{3,2,1,0:T(8,128)S(1)}, f32[2,3,136,256]{3,2,1,0:T(8,128)}, u32[]{:S(2)}) copy-start(f32[2,3,136,256]{3,2,1,0:T(8,128)} %get-tuple-element.57.plan) | copy-start | bytes 2506756
  59.8 23.4 %copy-start.1 = (f32[2,2,136,256]{3,2,1,0:T(8,128)S(1)}, f32[2,2,136,256]{3,2,1,0:T(8,128)}, u32[]{:S(2)}) copy-start(f32[2,2,136,256]{3,2,1,0:T(8,128)} %get-tuple-element.56.far_plan.plan) | copy-start | bytes 1671172
  75.1 8.7 %collective-permute-start.3 = (f32[4,72,128]{2,1,0:T(8,128)S(1)}, f32[4,72,128]{2,1,0:T(8,128)S(1)}, u32[]{:S(2)}, u32[]{:S(2)}) collective-permute-start(f32[4,72,128]{2,1,0:T(8,128)S(1)} %get-tuple-element.54), channel_id=1, source_target_pairs={{0,1},{1,2},{2,3},{3,4},{4,5},{5,6},{6,7},{7,8},{8,9},{9,10},{10,1... | collective-permute-start | bytes 442376 | tf_op jit(solution)/shard_map/ppermute | solution.py:490
  81.3 6.5 %collective-permute-start.4 = (f32[4,72,128]{2,1,0:T(8,128)S(1)}, f32[4,72,128]{2,1,0:T(8,128)S(1)}, u32[]{:S(2)}, u32[]{:S(2)}) collective-permute-start(f32[4,72,128]{2,1,0:T(8,128)S(1)} %get-tuple-element.55), channel_id=1, source_target_pairs={{1,0},{2,1},{3,2},{4,3},{5,4},{6,5},{7,6},{8,7},{9,8},{10,9},{11,1... | collective-permute-start | bytes 442376 | tf_op jit(solution)/shard_map/ppermute | solution.py:493
  83.8 17.0 %copy-start.2 = (f32[8,144,128]{2,1,0:T(8,128)S(1)}, f32[8,144,128]{2,1,0:T(8,128)}, u32[]{:S(2)}) copy-start(f32[8,144,128]{2,1,0:T(8,128)} %get-tuple-element.52.matrices) | copy-start | bytes 1769476
  102.6 11.2 %all-to-all-start.4 = ((f32[4,216,128]{2,1,0:T(8,128)}), f32[4,216,128]{2,1,0:T(8,128)S(1)}, u32[]{:S(2)}, u32[]{:S(2)}) async-start(f32[4,216,128]{2,1,0:T(8,128)} %shard_map.75), calls=%async_computation.4 | async-start | bytes 884736 | tf_op jit(solution)/shard_map/all_to_all | solution.py:487
  106.4 1.7 %copy-start.3 = (f32[3,2,3,136,256]{4,3,2,1,0:T(8,128)S(1)}, f32[3,2,3,136,256]{4,3,2,1,0:T(8,128)}, u32[]{:S(2)}) copy-start(f32[3,2,3,136,256]{4,3,2,1,0:T(8,128)} %get-tuple-element.61.refs_4_) | copy-start | bytes 7520260
  106.4 2.2 %copy-start.6 = (f32[3,2,2,136,256]{4,3,2,1,0:T(8,128)S(1)}, f32[3,2,2,136,256]{4,3,2,1,0:T(8,128)}, u32[]{:S(2)}) copy-start(f32[3,2,2,136,256]{4,3,2,1,0:T(8,128)} %get-tuple-element.62.refs_5_) | copy-start | bytes 5013508
  110.9 19.5 %copy-start.5 = (f32[3,2,136,256]{3,2,1,0:T(8,128)S(1)}, f32[3,2,136,256]{3,2,1,0:T(8,128)}, u32[]{:S(2)}) copy-start(f32[3,2,136,256]{3,2,1,0:T(8,128)} %shard_map.76.rest) | copy-start | bytes 2506756
  113.8 16.6 %copy-start.4 = (f32[4,2,136,256]{3,2,1,0:T(8,128)S(1)}, f32[4,2,136,256]{3,2,1,0:T(8,128)}, u32[]{:S(2)}) copy-start(f32[4,2,136,256]{3,2,1,0:T(8,128)} %get-tuple-element.64.maps) | copy-start | bytes 3342340

commit v7 on v6

--- a/solution.py
+++ b/solution.py
@@ -146,13 +146,6 @@
         rows, lanes = full - value.shape[0], 2 * LANES - value.shape[1]
         return jnp.pad(value, ((0, rows), (0, lanes)))
 
-    for c in range(columns):
-        steps = [-mul(inverse[s, c], after[s, c]) for s in range(positions)]
-        while len(steps) > 1:
-            steps = [float_by_float(*steps[k : k + 2]) for k in range(0, len(steps), 2)]
-        maps[c, 1] = pack_map(padded(steps[0]))
-        for q in range(peers):
-            send(maps.at[c, 1, pl.ds(q % PIECES * piece, piece)], c * peers + q, room)
     for c in range(columns):
         steps = [
             (-mul(inverse[s, c], before[s, c]), mul(inverse[s, c], source[s, c]))
@@ -171,6 +164,13 @@
             fold = (full // 8 + 1) // 2 * 8
             values[c, q, 0:fold] = pack_slice(pair, q % 2)
             send(values.at[c, q, pl.ds(0, fold)], c * peers + q, room + piece)
+    for c in range(columns):
+        steps = [-mul(inverse[s, c], after[s, c]) for s in range(positions)]
+        while len(steps) > 1:
+            steps = [float_by_float(*steps[k : k + 2]) for k in range(0, len(steps), 2)]
+        maps[c, 1] = pack_map(padded(steps[0]))
+        for q in range(peers):
+            send(maps.at[c, 1, pl.ds(q % PIECES * piece, piece)], c * peers + q, room)
     for copy in copies:
         copy.wait()
 

time: 134 us -> 134 us (level)
  no operation moved by 1% of the time
where the time goes in v7:
time: 134 us; the launch traced here: 132 us
  blocking collectives  42.5 us (32%)
  starting transfers between devices  33.6 us (25%)
  Pallas kernels  32.8 us (24%)
  waiting for transfers between devices  18.5 us (14%)
  local copies, waits for them, and re-layouts  4.31 us (3%)
    all_to_all x3, blocking collectives, exchange(): return lax.all_to_all(x, 'sweep', 0, 0, axis_index_groups=groups)  42.5 us
    pallas_call x16, Pallas kernels, call(): pl.pallas_call(with_copies if kept else kernel, out_shape=[jax.ShapeDtype...  32.8 us
    all_to_all x3, starting transfers between devices, exchange(): return lax.all_to_all(x, 'sweep', 0, 0, axis_index_groups=groups)  17.5 us
    ppermute x2, starting transfers between devices, from_below(): return lax.ppermute(x, 'cross', [(i, i + 1) for i in range(ends)])  10.3 us
    ppermute x2, waiting for transfers between devices, from_above(): return lax.ppermute(x, 'cross', [(i + 1, i) for i in range(ends)])  7.53 us
    ppermute x1, waiting for transfers between devices, shards(): lax.ppermute(own, ('sweep', 'cross'), [(i * wide + c, (i // ROW * ROW + (...  5.53 us
    all_to_all x3, waiting for transfers between devices, exchange(): return lax.all_to_all(x, 'sweep', 0, 0, axis_index_groups=groups)  5.41 us
    ppermute x2, starting transfers between devices, from_above(): return lax.ppermute(x, 'cross', [(i + 1, i) for i in range(ends)])  3.84 us
  transfers between devices with their start and end apart: 8, of which 5 were waited for; matrix products, arithmetic and copies ran while one was open for 0% of the time, Pallas kernels for 16%

profile of v7, /device:TPU:1, one launch (start us, length us, event | category | flops | bytes accessed | tf_op | source)
XLA Modules:
  0.0 132.1 jit_solution(2924815999648069093)
XLA Ops:
  0.0 1.3 copy.44
  1.3 0.1 copy.43
  1.4 0.0 copy-done.11
  1.4 0.2 copy-done.13
  1.6 0.2 copy_bitcast_fusion.7
  1.7 3.5 %shard_map.64 = f32[8,288,128]{2,1,0:T(8,128)} custom-call(s32[1]{0:T(128)} %bitcast.turn.refs_0_, bf16[4,2,135,135]{3,2,1,0:T(8,128)(2,1)S(1)} %bitcast.34, bf16[4,2,135,135]{3,2,1,0:T(8,128)(2,1)S(1)} %get-tuple-element.68.before, bf16[4,2,135,135]{3,2,1,0:T(8,128)(2,1)S(1)} %get-tuple-element.67.after, bf16[4,2,135,256]{3,2,1,0:T(8,128)(2,1)S(1)} %bitcast.35), custom_call_target="tpu_custom_call" | custom-call | flops 4000000000 | bytes 4000000 | tf_op jit(solution)/shard_map/pallas_call | solution.py:447
  5.2 0.0 copy-start.10
  5.2 7.8 %all-to-all-start = ((f32[8,288,128]{2,1,0:T(8,128)}), f32[8,288,128]{2,1,0:T(8,128)S(1)}, u32[]{:S(2)}, u32[]{:S(2)}) async-start(f32[8,288,128]{2,1,0:T(8,128)} %shard_map.64), calls=%async_computation | async-start | bytes 2359296 | tf_op jit(solution)/shard_map/all_to_all | solution.py:487
  13.0 0.1 copy.42
  13.1 0.1 copy.41
  13.2 0.1 copy.40
  13.3 3.8 %shard_map.65 = (f32[4,416,128]{2,1,0:T(8,128)}, f32[4,416,128]{2,1,0:T(8,128)}, f32[4,2,136,256]{3,2,1,0:T(8,128)}, f32[4,2,136,256]{3,2,1,0:T(8,128)}) custom-call(bf16[4,2,135,135]{3,2,1,0:T(8,128)(2,1)S(1)} %bitcast.30, bf16[4,2,135,135]{3,2,1,0:T(8,128)(2,1)S(1)} %bitcast.36, bf16[4,2,135,256]{3,2,1,0:T(8,128)(2,1)S(1)} %bitcast.37), custom_call_target="tpu_custom_call" | custom-call | flops 3000000000 | bytes 3000000 | tf_op jit(solution)/shard_map/pallas_call | solution.py:447
  17.1 4.8 %collective-permute-start = (f32[4,416,128]{2,1,0:T(8,128)}, f32[4,416,128]{2,1,0:T(8,128)S(1)}, u32[]{:S(2)}, u32[]{:S(2)}) collective-permute-start(f32[4,416,128]{2,1,0:T(8,128)} %get-tuple-element.45), channel_id=1, source_target_pairs={{0,1},{1,2},{2,3},{3,4},{4,5},{5,6},{6,7},{7,8},{8,9},{9,10},{10,1... | collective-permute-start | bytes 2555912 | tf_op jit(solution)/shard_map/ppermute | solution.py:490
  21.9 1.9 %collective-permute-start.1 = (f32[4,416,128]{2,1,0:T(8,128)}, f32[4,416,128]{2,1,0:T(8,128)S(1)}, u32[]{:S(2)}, u32[]{:S(2)}) collective-permute-start(f32[4,416,128]{2,1,0:T(8,128)} %get-tuple-element.46), channel_id=1, source_target_pairs={{1,0},{2,1},{3,2},{4,3},{5,4},{6,5},{7,6},{8,7},{9,8},{10,9},{11,1... | collective-permute-start | bytes 2555912 | tf_op jit(solution)/shard_map/ppermute | solution.py:493
  23.8 0.1 copy.39
  24.0 2.5 %shard_map.66 = (f32[4,2,136,256]{3,2,1,0:T(8,128)}, f32[4,2,136,256]{3,2,1,0:T(8,128)}) custom-call(bf16[4,2,135,135]{3,2,1,0:T(8,128)(2,1)S(1)} %bitcast.31, bf16[4,2,135,135]{3,2,1,0:T(8,128)(2,1)S(1)} %bitcast.38), custom_call_target="tpu_custom_call" | custom-call | flops 2000000000 | bytes 2000000 | tf_op jit(solution)/shard_map/pallas_call | solution.py:447
  26.5 0.2 copy_bitcast_fusion.3
  26.7 1.1 copy-done.7
  27.7 0.3 copy-done.8
  28.1 4.7 %shard_map.67 = (f32[2,3,136,256]{3,2,1,0:T(8,128)}, f32[3,2,3,136,256]{4,3,2,1,0:T(8,128)}) custom-call(bf16[4,2,135,135]{3,2,1,0:T(8,128)(2,1)S(1)} %bitcast.32, bf16[4,2,135,135]{3,2,1,0:T(8,128)(2,1)S(1)} %get-tuple-element.70.refs_1_, bf16[4,2,135,135]{3,2,1,0:T(8,128)(2,1)S(1)} %get-tuple-element.69.refs_2_, f32[4,2,136,256]{3,2,1,0:T(8,128)S(1)} %copy-done.8, ...), custom_call_target="tpu_custom_call" | custom-call | flops 4000000000 | bytes 4000000 | tf_op jit(solution)/shard_map/pallas_call | solution.py:447
  32.8 3.6 %collective-permute-done.1.refs_4_ = f32[4,416,128]{2,1,0:T(8,128)S(1)} collective-permute-done((f32[4,416,128]{2,1,0:T(8,128)}, f32[4,416,128]{2,1,0:T(8,128)S(1)}, u32[]{:S(2)}, u32[]{:S(2)}) %collective-permute-start.1) | collective-permute-done | bytes 852000 | tf_op jit(solution)/shard_map/ppermute | solution.py:493
  36.4 4.3 %shard_map.68 = (f32[2,2,136,256]{3,2,1,0:T(8,128)}, f32[3,2,2,136,256]{4,3,2,1,0:T(8,128)}) custom-call(bf16[4,2,135,135]{3,2,1,0:T(8,128)(2,1)S(1)} %bitcast.33, bf16[4,2,135,135]{3,2,1,0:T(8,128)(2,1)S(1)} %get-tuple-element.70.refs_1_, bf16[4,2,135,135]{3,2,1,0:T(8,128)(2,1)S(1)} %get-tuple-element.69.refs_2_, ...), custom_call_target="tpu_custom_call" | custom-call | flops 3000000000 | bytes 3000000 | tf_op jit(solution)/shard_map/pallas_call | solution.py:447
  40.8 2.5 %all-to-all-done.received = f32[8,288,128]{2,1,0:T(8,128)S(1)} async-done(((f32[8,288,128]{2,1,0:T(8,128)}), f32[8,288,128]{2,1,0:T(8,128)S(1)}, u32[]{:S(2)}, u32[]{:S(2)}) %all-to-all-start) | async-done | bytes 1179680 | tf_op jit(solution)/shard_map/all_to_all | solution.py:487
  43.3 1.8 %shard_map.69 = (f32[8,72,128]{2,1,0:T(8,128)S(1)}, f32[4,216,128]{2,1,0:T(8,128)}) custom-call(f32[8,288,128]{2,1,0:T(8,128)S(1)} %all-to-all-done.received), custom_call_target="tpu_custom_call" | custom-call | flops 1500000000 | bytes 1500000 | tf_op jit(solution)/shard_map/pallas_call | solution.py:447
  45.1 5.8 %all-to-all-start.1 = ((f32[4,216,128]{2,1,0:T(8,128)}), f32[4,216,128]{2,1,0:T(8,128)S(1)}, u32[]{:S(2)}, u32[]{:S(2)}) async-start(f32[4,216,128]{2,1,0:T(8,128)} %get-tuple-element.51), calls=%async_computation.1 | async-start | bytes 884736 | tf_op jit(solution)/shard_map/all_to_all | solution.py:487
  50.9 1.9 %collective-permute-start.2 = (f32[8,72,128]{2,1,0:T(8,128)S(1)}, f32[8,72,128]{2,1,0:T(8,128)S(1)}, u32[]{:S(2)}, u32[]{:S(2)}) collective-permute-start(f32[8,72,128]{2,1,0:T(8,128)S(1)} %get-tuple-element.50.own), channel_id=1, source_target_pairs={{0,16},{1,113},{2,18},{3,115},{4,20},{5,117},{6,22},{7,119},{8,24}... | collective-permute-start | bytes 884744 | tf_op jit(solution)/shard_map/ppermute | solution.py:559
  52.8 1.5 %shard_map.70.states = f32[7,136,256]{2,1,0:T(8,128)S(1)} custom-call(f32[8,288,128]{2,1,0:T(8,128)S(1)} %all-to-all-done.received), custom_call_target="tpu_custom_call" | custom-call | flops 2000000000 | bytes 2000000 | tf_op jit(solution)/shard_map/pallas_call | solution.py:447
  54.3 5.5 %collective-permute-done.2.other = f32[8,72,128]{2,1,0:T(8,128)S(1)} collective-permute-done((f32[8,72,128]{2,1,0:T(8,128)S(1)}, f32[8,72,128]{2,1,0:T(8,128)S(1)}, u32[]{:S(2)}, u32[]{:S(2)}) %collective-permute-start.2) | collective-permute-done | bytes 294944 | tf_op jit(solution)/shard_map/ppermute | solution.py:559
  59.8 1.3 shard_map.71
  61.1 14.5 %all_to_all.30.received.refs_1_ = f32[8,72,128]{2,1,0:T(8,128)S(1)} all-to-all(f32[8,72,128]{2,1,0:T(8,128)S(1)} %get-tuple-element.53), channel_id=1, replica_groups={{0,16,32,48,64,80,96,112},{128,144,160,176,192,208,224,240},{256,272,28..., dimensions={0} | all-to-all | bytes 589824 | tf_op jit(solution)/shard_map/all_to_all | solution.py:487
  75.7 5.4 %collective-permute-start.3 = (f32[4,72,128]{2,1,0:T(8,128)S(1)}, f32[4,72,128]{2,1,0:T(8,128)S(1)}, u32[]{:S(2)}, u32[]{:S(2)}) collective-permute-start(f32[4,72,128]{2,1,0:T(8,128)S(1)} %get-tuple-element.54), channel_id=1, source_target_pairs={{0,1},{1,2},{2,3},{3,4},{4,5},{5,6},{6,7},{7,8},{8,9},{9,10},{10,1... | collective-permute-start | bytes 442376 | tf_op jit(solution)/shard_map/ppermute | solution.py:490
  81.1 1.9 %collective-permute-start.4 = (f32[4,72,128]{2,1,0:T(8,128)S(1)}, f32[4,72,128]{2,1,0:T(8,128)S(1)}, u32[]{:S(2)}, u32[]{:S(2)}) collective-permute-start(f32[4,72,128]{2,1,0:T(8,128)S(1)} %get-tuple-element.55), channel_id=1, source_target_pairs={{1,0},{2,1},{3,2},{4,3},{5,4},{6,5},{7,6},{8,7},{9,8},{10,9},{11,1... | collective-permute-start | bytes 442376 | tf_op jit(solution)/shard_map/ppermute | solution.py:493
  83.1 0.6 shard_map.73.part
  83.7 0.0 copy-start.2
  83.7 3.9 %collective-permute-done.4.above.refs_3_ = f32[4,72,128]{2,1,0:T(8,128)S(1)} collective-permute-done((f32[4,72,128]{2,1,0:T(8,128)S(1)}, f32[4,72,128]{2,1,0:T(8,128)S(1)}, u32[]{:S(2)}, u32[]{:S(2)}) %collective-permute-start.4) | collective-permute-done | bytes 147488 | tf_op jit(solution)/shard_map/ppermute | solution.py:493
  87.6 0.6 shard_map.74
  88.2 12.5 %all_to_all.31.blocks = f32[8,72,128]{2,1,0:T(8,128)S(1)} all-to-all(f32[8,72,128]{2,1,0:T(8,128)S(1)} %get-tuple-element.58), channel_id=1, replica_groups={{0,16,32,48,64,80,96,112},{128,144,160,176,192,208,224,240},{256,272,28..., dimensions={0} | all-to-all | bytes 589824 | tf_op jit(solution)/shard_map/all_to_all | solution.py:487
  100.7 1.8 %shard_map.75 = f32[4,216,128]{2,1,0:T(8,128)} custom-call(f32[8,144,128]{2,1,0:T(8,128)S(1)} %copy-done.2, f32[8,72,128]{2,1,0:T(8,128)S(1)} %all_to_all.31.blocks), custom_call_target="tpu_custom_call" | custom-call | flops 1500000000 | bytes 1500000 | tf_op jit(solution)/shard_map/pallas_call | solution.py:447
  102.4 4.0 %all-to-all-start.4 = ((f32[4,216,128]{2,1,0:T(8,128)}), f32[4,216,128]{2,1,0:T(8,128)S(1)}, u32[]{:S(2)}, u32[]{:S(2)}) async-start(f32[4,216,128]{2,1,0:T(8,128)} %shard_map.75), calls=%async_computation.4 | async-start | bytes 884736 | tf_op jit(solution)/shard_map/all_to_all | solution.py:487
  106.4 1.5 %shard_map.77.states = f32[7,136,256]{2,1,0:T(8,128)S(1)} custom-call(f32[8,144,128]{2,1,0:T(8,128)S(1)} %copy-done.2, f32[8,72,128]{2,1,0:T(8,128)S(1)} %all_to_all.31.blocks), custom_call_target="tpu_custom_call" | custom-call | flops 2500000000 | bytes 2500000 | tf_op jit(solution)/shard_map/pallas_call | solution.py:447
  107.9 0.2 copy-done.3
  108.1 0.5 copy-done.6
  108.6 2.3 %shard_map.76.rest = f32[3,2,136,256]{3,2,1,0:T(8,128)} custom-call(s32[1]{0:T(128)} %bitcast.turn.refs_0_, f32[8,72,128]{2,1,0:T(8,128)S(1)} %all_to_all.30.received.refs_1_, f32[4,72,128]{2,1,0:T(8,128)S(1)} %collective-permute-done.3.below.refs_2_, f32[4,72,128]{2,1,0:T(8,128)S(1)} %collective-permute-done.4.above.refs_3_, ...), custom_call_target="tpu_custom_call" | custom-call | flops 3000000000 | bytes 3000000 | tf_op jit(solution)/shard_map/pallas_call | solution.py:447
  110.9 0.0 copy-start.5
  110.9 2.9 %all-to-all-done.4.received = f32[4,216,128]{2,1,0:T(8,128)S(1)} async-done(((f32[4,216,128]{2,1,0:T(8,128)}), f32[4,216,128]{2,1,0:T(8,128)S(1)}, u32[]{:S(2)}, u32[]{:S(2)}) %all-to-all-start.4) | async-done | bytes 442400 | tf_op jit(solution)/shard_map/all_to_all | solution.py:487
  113.8 1.1 shard_map.78
  114.9 15.5 %all_to_all.32.received = f32[8,72,128]{2,1,0:T(8,128)S(1)} all-to-all(f32[8,72,128]{2,1,0:T(8,128)S(1)} %shard_map.78), channel_id=1, replica_groups={{0,16,32,48,64,80,96,112},{128,144,160,176,192,208,224,240},{256,272,28..., dimensions={0} | all-to-all | bytes 589824 | tf_op jit(solution)/shard_map/all_to_all | solution.py:487
  130.4 1.6 %shard_map.79 = f32[2160,128]{1,0:T(8,128)} custom-call(s32[1]{0:T(128)} %bitcast.turn.refs_0_, f32[8,72,128]{2,1,0:T(8,128)S(1)} %all_to_all.32.received, f32[4,2,136,256]{3,2,1,0:T(8,128)S(1)} %copy-done.4, f32[2,136,256]{2,1,0:T(8,128)S(1)} %get-tuple-element.65.first, f32[3,2,136,256]{3,2,1,0:T(8,128)S(1)} %copy-done.5), custom_call_target="tpu_custom_call" | custom-call | flops 2000000000 | bytes 2000000 | tf_op jit(solution)/shard_map/pallas_call | solution.py:447
  (27 shorter events, 0.1 us)
Async XLA Ops:
  0.0 1.3 copy-start.12
  0.0 1.4 %copy-start.11 = (bf16[4,2,1,135,135]{4,1,3,2,0:T(2,128)(2,1)S(1)}, bf16[4,2,1,135,135]{4,1,3,2,0:T(2,128)(2,1)}, u32[]{:S(2)}) copy-start(bf16[4,2,1,135,135]{4,1,3,2,0:T(2,128)(2,1)} %param.8) | copy-start | bytes 874804
  0.0 1.5 %copy-start.13 = (bf16[4,2,1,135,135]{4,1,3,2,0:T(2,128)(2,1)S(1)}, bf16[4,2,1,135,135]{4,1,3,2,0:T(2,128)(2,1)}, u32[]{:S(2)}) copy-start(bf16[4,2,1,135,135]{4,1,3,2,0:T(2,128)(2,1)} %param.9) | copy-start | bytes 874804
  5.2 7.8 %copy-start.10 = (bf16[4,2,1,135,135]{4,1,3,2,0:T(2,128)(2,1)S(1)}, bf16[4,2,1,135,135]{4,1,3,2,0:T(2,128)(2,1)}, u32[]{:S(2)}) copy-start(bf16[4,2,1,135,135]{4,1,3,2,0:T(2,128)(2,1)} %param.7) | copy-start | bytes 874804
  5.2 38.1 %all-to-all-start = ((f32[8,288,128]{2,1,0:T(8,128)}), f32[8,288,128]{2,1,0:T(8,128)S(1)}, u32[]{:S(2)}, u32[]{:S(2)}) async-start(f32[8,288,128]{2,1,0:T(8,128)} %shard_map.64), calls=%async_computation | async-start | bytes 2359296 | tf_op jit(solution)/shard_map/all_to_all | solution.py:487
  17.1 15.7 %collective-permute-start = (f32[4,416,128]{2,1,0:T(8,128)}, f32[4,416,128]{2,1,0:T(8,128)S(1)}, u32[]{:S(2)}, u32[]{:S(2)}) collective-permute-start(f32[4,416,128]{2,1,0:T(8,128)} %get-tuple-element.45), channel_id=1, source_target_pairs={{0,1},{1,2},{2,3},{3,4},{4,5},{5,6},{6,7},{7,8},{8,9},{9,10},{10,1... | collective-permute-start | bytes 2555912 | tf_op jit(solution)/shard_map/ppermute | solution.py:490
  21.9 14.5 %collective-permute-start.1 = (f32[4,416,128]{2,1,0:T(8,128)}, f32[4,416,128]{2,1,0:T(8,128)S(1)}, u32[]{:S(2)}, u32[]{:S(2)}) collective-permute-start(f32[4,416,128]{2,1,0:T(8,128)} %get-tuple-element.46), channel_id=1, source_target_pairs={{1,0},{2,1},{3,2},{4,3},{5,4},{6,5},{7,6},{8,7},{9,8},{10,9},{11,1... | collective-permute-start | bytes 2555912 | tf_op jit(solution)/shard_map/ppermute | solution.py:493
  23.9 2.6 %copy-start.14 = (bf16[4,2,1,135,135]{4,1,3,2,0:T(2,128)(2,1)S(1)}, bf16[4,2,1,135,135]{4,1,3,2,0:T(2,128)(2,1)}, u32[]{:S(2)}) copy-start(bf16[4,2,1,135,135]{4,1,3,2,0:T(2,128)(2,1)} %param.11) | copy-start | bytes 874804
  23.9 2.6 %copy-start.15 = (bf16[4,2,1,135,135]{4,1,3,2,0:T(2,128)(2,1)S(1)}, bf16[4,2,1,135,135]{4,1,3,2,0:T(2,128)(2,1)}, u32[]{:S(2)}) copy-start(bf16[4,2,1,135,135]{4,1,3,2,0:T(2,128)(2,1)} %param.10) | copy-start | bytes 874804
  23.9 2.7 %copy-start.9 = (f32[4,2,136,256]{3,2,1,0:T(8,128)S(1)}, f32[4,2,136,256]{3,2,1,0:T(8,128)}, u32[]{:S(2)}) copy-start(f32[4,2,136,256]{3,2,1,0:T(8,128)} %get-tuple-element.40.refs_4_) | copy-start | bytes 3342340
  26.5 1.2 copy-start.7
  26.5 1.6 %copy-start.8 = (f32[4,2,136,256]{3,2,1,0:T(8,128)S(1)}, f32[4,2,136,256]{3,2,1,0:T(8,128)}, u32[]{:S(2)}) copy-start(f32[4,2,136,256]{3,2,1,0:T(8,128)} %get-tuple-element.39.refs_3_) | copy-start | bytes 3342340
  45.1 14.8 %all-to-all-start.1 = ((f32[4,216,128]{2,1,0:T(8,128)}), f32[4,216,128]{2,1,0:T(8,128)S(1)}, u32[]{:S(2)}, u32[]{:S(2)}) async-start(f32[4,216,128]{2,1,0:T(8,128)} %get-tuple-element.51), calls=%async_computation.1 | async-start | bytes 884736 | tf_op jit(solution)/shard_map/all_to_all | solution.py:487
  50.9 9.0 %collective-permute-start.2 = (f32[8,72,128]{2,1,0:T(8,128)S(1)}, f32[8,72,128]{2,1,0:T(8,128)S(1)}, u32[]{:S(2)}, u32[]{:S(2)}) collective-permute-start(f32[8,72,128]{2,1,0:T(8,128)S(1)} %get-tuple-element.50.own), channel_id=1, source_target_pairs={{0,16},{1,113},{2,18},{3,115},{4,20},{5,117},{6,22},{7,119},{8,24}... | collective-permute-start | bytes 884744 | tf_op jit(solution)/shard_map/ppermute | solution.py:559
  59.8 23.2 %copy-start = (f32[2,3,136,256]{3,2,1,0:T(8,128)S(1)}, f32[2,3,136,256]{3,2,1,0:T(8,128)}, u32[]{:S(2)}) copy-start(f32[2,3,136,256]{3,2,1,0:T(8,128)} %get-tuple-element.57.plan) | copy-start | bytes 2506756
  59.8 23.2 %copy-start.1 = (f32[2,2,136,256]{3,2,1,0:T(8,128)S(1)}, f32[2,2,136,256]{3,2,1,0:T(8,128)}, u32[]{:S(2)}) copy-start(f32[2,2,136,256]{3,2,1,0:T(8,128)} %get-tuple-element.56.far_plan.plan) | copy-start | bytes 1671172
  75.7 8.0 %collective-permute-start.3 = (f32[4,72,128]{2,1,0:T(8,128)S(1)}, f32[4,72,128]{2,1,0:T(8,128)S(1)}, u32[]{:S(2)}, u32[]{:S(2)}) collective-permute-start(f32[4,72,128]{2,1,0:T(8,128)S(1)} %get-tuple-element.54), channel_id=1, source_target_pairs={{0,1},{1,2},{2,3},{3,4},{4,5},{5,6},{6,7},{7,8},{8,9},{9,10},{10,1... | collective-permute-start | bytes 442376 | tf_op jit(solution)/shard_map/ppermute | solution.py:490
  81.1 6.5 %collective-permute-start.4 = (f32[4,72,128]{2,1,0:T(8,128)S(1)}, f32[4,72,128]{2,1,0:T(8,128)S(1)}, u32[]{:S(2)}, u32[]{:S(2)}) collective-permute-start(f32[4,72,128]{2,1,0:T(8,128)S(1)} %get-tuple-element.55), channel_id=1, source_target_pairs={{1,0},{2,1},{3,2},{4,3},{5,4},{6,5},{7,6},{8,7},{9,8},{10,9},{11,1... | collective-permute-start | bytes 442376 | tf_op jit(solution)/shard_map/ppermute | solution.py:493
  83.7 17.0 %copy-start.2 = (f32[8,144,128]{2,1,0:T(8,128)S(1)}, f32[8,144,128]{2,1,0:T(8,128)}, u32[]{:S(2)}) copy-start(f32[8,144,128]{2,1,0:T(8,128)} %get-tuple-element.52.matrices) | copy-start | bytes 1769476
  102.4 11.3 %all-to-all-start.4 = ((f32[4,216,128]{2,1,0:T(8,128)}), f32[4,216,128]{2,1,0:T(8,128)S(1)}, u32[]{:S(2)}, u32[]{:S(2)}) async-start(f32[4,216,128]{2,1,0:T(8,128)} %shard_map.75), calls=%async_computation.4 | async-start | bytes 884736 | tf_op jit(solution)/shard_map/all_to_all | solution.py:487
  106.4 1.7 %copy-start.3 = (f32[3,2,3,136,256]{4,3,2,1,0:T(8,128)S(1)}, f32[3,2,3,136,256]{4,3,2,1,0:T(8,128)}, u32[]{:S(2)}) copy-start(f32[3,2,3,136,256]{4,3,2,1,0:T(8,128)} %get-tuple-element.61.refs_4_) | copy-start | bytes 7520260
  106.4 2.2 %copy-start.6 = (f32[3,2,2,136,256]{4,3,2,1,0:T(8,128)S(1)}, f32[3,2,2,136,256]{4,3,2,1,0:T(8,128)}, u32[]{:S(2)}) copy-start(f32[3,2,2,136,256]{4,3,2,1,0:T(8,128)} %get-tuple-element.62.refs_5_) | copy-start | bytes 5013508
  110.9 19.5 %copy-start.5 = (f32[3,2,136,256]{3,2,1,0:T(8,128)S(1)}, f32[3,2,136,256]{3,2,1,0:T(8,128)}, u32[]{:S(2)}) copy-start(f32[3,2,136,256]{3,2,1,0:T(8,128)} %shard_map.76.rest) | copy-start | bytes 2506756
  113.8 16.6 %copy-start.4 = (f32[4,2,136,256]{3,2,1,0:T(8,128)S(1)}, f32[4,2,136,256]{3,2,1,0:T(8,128)}, u32[]{:S(2)}) copy-start(f32[4,2,136,256]{3,2,1,0:T(8,128)} %get-tuple-element.64.maps) | copy-start | bytes 3342340
